TPU v7x, 128 devices: a whole 4x4x4 slice. The times are simulated.
128 devices in a mesh: dp: 8 (over y, z_hi), seq: 2 (over core), tensor: 8 (over z_lo, x).
Axes of the slice: x: 4, y: 4, z: 4 (z_hi: 2, z_lo: 2; z = z_hi * 2 + z_lo), core: 2. Of those that a mesh axis runs over, the one named last changes fastest.
Arguments:
- inputs: bfloat16 [24, 512, 1152], P('dp', 'seq'), may hold values from -6 to 6
- picture_ids: int32 [24, 512], P('dp', 'seq'), may hold values from -1 to 3, as said below
- cotangent: bfloat16 [24, 512, 1152], P('dp', 'seq'), may hold values from -6 to 6
- norm_gain: float32 [2, 2, 1152], replicated, may hold values from 0.5 to 1.5
- norm_bias: float32 [2, 2, 1152], replicated, may hold values from -1.75 to 1.75
- w_qkv: bfloat16 [2, 3, 1152, 1152], P(None, None, None, 'tensor'), may hold values from -0.1875 to 0.1875
- q_bias: float32 [2, 1152], P(None, 'tensor'), may hold values from -1.75 to 1.75
- v_bias: float32 [2, 1152], P(None, 'tensor'), may hold values from -0.3125 to 0.3125
- w_out: bfloat16 [2, 1152, 1152], P(None, 'tensor'), may hold values from -3 to 3
- out_bias: float32 [2, 1152], replicated, may hold values from -1.75 to 1.75
- w_up: bfloat16 [2, 1152, 4304], P(None, None, 'tensor'), may hold values from -0.1875 to 0.1875
- up_bias: float32 [2, 4304], P(None, 'tensor'), may hold values from -3 to 3
- w_down: bfloat16 [2, 4304, 1152], P(None, 'tensor'), may hold values from -0.125 to 0.125
- down_bias: float32 [2, 1152], replicated, may hold values from -1.75 to 1.75
Outputs:
- outputs: bfloat16 [24, 512, 1152], P('dp', 'seq')
- input_grad: float32 [24, 512, 1152], P('dp', 'seq')
- norm_gain_grad: float32 [2, 2, 1152], replicated
- norm_bias_grad: float32 [2, 2, 1152], replicated
- w_qkv_grad: float32 [2, 3, 1152, 1152], P(None, None, None, 'tensor')
- q_bias_grad: float32 [2, 1152], P(None, 'tensor')
- v_bias_grad: float32 [2, 1152], P(None, 'tensor')
- w_out_grad: float32 [2, 1152, 1152], P(None, 'tensor')
- out_bias_grad: float32 [2, 1152], replicated
- w_up_grad: float32 [2, 1152, 4304], P(None, None, 'tensor')
- up_bias_grad: float32 [2, 4304], P(None, 'tensor')
- w_down_grad: float32 [2, 4304, 1152], P(None, 'tensor')
- down_bias_grad: float32 [2, 1152], replicated
Inputs may be any that keep to these rules, and one draw needn't show every extreme that they name: `picture_ids`: in each row the slots hold pictures numbered 0, 1, 2, 3 in this order, each a run of consecutive slots, followed by 1 to 64 pad slots of -1; picture 2 covers the slots 512 // 4 to 383 and more.
All inputs are finite; a program needn't handle non-finite values.
Results may differ from a plain program's by a relative error of at most 0.025.
Values may be sent and summed in bfloat16 or wider, within the bound.
No kernel may reach another device: no remote copies, remote signals or barrier semaphores. Data moves between devices by JAX's collectives and lax.ppermute only.
A program may use at most 192 MiB of HBM per device.

v0:
```python
import jax
import jax.numpy as jnp
from jax import lax
from jax.sharding import PartitionSpec as P

HEAD_DIM = 72


norm_eps = 1e-06
gelu_coef = 0.7978845608028654


def from_partner(value, axis, stride):
    mask = 2**stride
    pairs = [(source, source ^ mask) for source in range(lax.axis_size(axis))]
    return lax.ppermute(value, axis, pairs)


def as_sent(array):

    def short(part):
        return part.astype(jnp.bfloat16) if part.dtype == jnp.float32 else part

    return jax.tree.map(short, array)


def normalize(stream, weight_gain, weight_shift):
    row_mean = jnp.mean(stream, axis=-1, keepdims=True)
    centred = stream - row_mean
    row_var = jnp.mean(centred * centred, axis=-1, keepdims=True)
    return centred * lax.rsqrt(row_var + norm_eps) * weight_gain + weight_shift


def gelu_tanh(stream):
    return (
        0.5 * stream * (1.0 + jnp.tanh(gelu_coef * (stream + 0.044715 * stream * stream * stream)))
    )


def slot_mask(query_ids, key_ids):
    return (key_ids[None, :] >= 0) & (
        (query_ids[:, None] == key_ids[None, :]) | (query_ids[:, None] < 0)
    )


def split_heads(matrix, head_dim):
    return matrix.reshape(matrix.shape[0], matrix.shape[1] // head_dim, head_dim)


def score_block(query, all_keys, allowed, head_dim):
    raw_scores = jnp.einsum(
        "qhd,khd->hqk",
        split_heads(query, head_dim),
        split_heads(all_keys, head_dim),
        preferred_element_type=jnp.float32,
    )
    return jnp.where(allowed[None], raw_scores * head_dim ** (-0.5), -1e30)


def tensor_branch(partial_sum):
    return lax.psum(partial_sum.astype(jnp.bfloat16), "tensor").astype(jnp.float32)


def tensor_norm_grad(partial_sum):
    return lax.psum(partial_sum.astype(jnp.bfloat16), "tensor").astype(jnp.float32)


def attend(normed, query_ids, w_qkv, q_bias, v_bias, head_dim):
    length = normed.shape[0]
    projected = jnp.einsum("td,sdc->stc", normed, w_qkv, preferred_element_type=jnp.float32)
    query = (projected[0] + q_bias).astype(jnp.bfloat16)
    key_proj = projected[1].astype(jnp.bfloat16)
    value_proj = (projected[2] + v_bias).astype(jnp.bfloat16)
    far_keys, far_values, far_ids = from_partner((key_proj, value_proj, query_ids), "seq", 0)
    all_keys = jnp.concatenate([key_proj, far_keys], axis=0)
    all_values = jnp.concatenate([value_proj, far_values], axis=0)
    key_ids = jnp.concatenate([query_ids, far_ids], axis=0)
    scores = score_block(query, all_keys, slot_mask(query_ids, key_ids), head_dim)
    row_max = jnp.max(scores, axis=-1, keepdims=True)
    expanded = jnp.exp(scores - row_max)
    row_total = jnp.sum(expanded, axis=-1, keepdims=True)
    probs_low = (expanded / row_total).astype(jnp.bfloat16)
    mixed = (
        jnp.einsum(
            "hqk,khd->qhd",
            probs_low,
            split_heads(all_values, head_dim),
            preferred_element_type=jnp.float32,
        )
        .reshape(length, -1)
        .astype(jnp.bfloat16)
    )
    return (query, all_keys, all_values, key_ids, row_max, row_total, mixed)


def attend_back(
    mid_low,
    normed,
    query,
    all_keys,
    all_values,
    query_ids,
    key_ids,
    row_max,
    row_total,
    mixed,
    w_out,
    head_dim,
):
    length = normed.shape[0]
    d_w_out = jnp.einsum("tc,td->cd", mixed, mid_low, preferred_element_type=jnp.float32)
    d_mixed = jnp.einsum("td,cd->tc", mid_low, w_out, preferred_element_type=jnp.float32).astype(
        jnp.bfloat16
    )
    scores = score_block(query, all_keys, slot_mask(query_ids, key_ids), head_dim)
    probs = jnp.exp(scores - row_max) / row_total
    probs_low = probs.astype(jnp.bfloat16)
    mixed_heads = split_heads(d_mixed, head_dim)
    query_heads = split_heads(query, head_dim)
    key_heads = split_heads(all_keys, head_dim)
    value_heads = split_heads(all_values, head_dim)
    d_probs = jnp.einsum(
        "qhd,khd->hqk", mixed_heads, value_heads, preferred_element_type=jnp.float32
    )
    inner_sum = jnp.sum(d_probs * probs, axis=-1, keepdims=True)
    d_raw = (probs * (d_probs - inner_sum) * head_dim ** (-0.5)).astype(jnp.bfloat16)
    key_rows = all_keys.shape[0]
    d_query = (
        jnp.einsum("hqk,khd->qhd", d_raw, key_heads, preferred_element_type=jnp.float32)
        .reshape(length, -1)
        .astype(jnp.bfloat16)
    )
    d_keys = jnp.einsum(
        "hqk,qhd->khd", d_raw, query_heads, preferred_element_type=jnp.float32
    ).reshape(key_rows, -1)
    d_values = jnp.einsum(
        "hqk,qhd->khd", probs_low, mixed_heads, preferred_element_type=jnp.float32
    ).reshape(key_rows, -1)
    back_keys, back_values = (
        from_partner(d_keys[length:].astype(jnp.bfloat16), "seq", 0).astype(jnp.float32),
        from_partner(d_values[length:].astype(jnp.bfloat16), "seq", 0).astype(jnp.float32),
    )
    d_key = (d_keys[:length] + back_keys).astype(jnp.bfloat16)
    d_value = (d_values[:length] + back_values).astype(jnp.bfloat16)
    d_q_bias = jnp.sum(d_query.astype(jnp.float32), axis=0)
    d_v_bias = jnp.sum(d_value.astype(jnp.float32), axis=0)
    stacked = jnp.stack([d_query, d_key, d_value])
    d_w_qkv = jnp.einsum("td,stc->sdc", normed, stacked, preferred_element_type=jnp.float32)
    return (d_w_out, stacked, d_w_qkv, d_q_bias, d_v_bias)


def layer_forward(stream, query_ids, params, head_dim):
    gains, shifts, w_qkv, q_bias, v_bias, w_out, out_bias, w_up, up_bias, w_down, down_bias = params
    normed = normalize(stream, gains[0], shifts[0]).astype(jnp.bfloat16)
    query, all_keys, all_values, key_ids, row_max, row_total, mixed = attend(
        normed, query_ids, w_qkv, q_bias, v_bias, head_dim
    )
    after_attn = (
        stream + tensor_branch(jnp.dot(mixed, w_out, preferred_element_type=jnp.float32)) + out_bias
    )
    normed_two = normalize(after_attn, gains[1], shifts[1]).astype(jnp.bfloat16)
    up_proj = jnp.dot(normed_two, w_up, preferred_element_type=jnp.float32) + up_bias
    activated = gelu_tanh(up_proj).astype(jnp.bfloat16)
    result = (
        after_attn
        + tensor_branch(jnp.dot(activated, w_down, preferred_element_type=jnp.float32))
        + down_bias
    )
    kept_values = (
        stream,
        normed,
        query,
        all_keys,
        all_values,
        query_ids,
        key_ids,
        row_max,
        row_total,
        mixed,
        after_attn,
        normed_two,
        up_proj,
        activated,
    )
    return (result, kept_values)


def layer_backward(grad_flow, kept_values, params, head_dim):
    gains, shifts, w_qkv, q_bias, v_bias, w_out, out_bias, w_up, up_bias, w_down, down_bias = params
    (
        stream,
        normed,
        query,
        all_keys,
        all_values,
        query_ids,
        key_ids,
        row_max,
        row_total,
        mixed,
        after_attn,
        normed_two,
        up_proj,
        activated,
    ) = kept_values
    grad_low = grad_flow.astype(jnp.bfloat16)
    d_w_down = jnp.einsum("tf,td->fd", activated, grad_low, preferred_element_type=jnp.float32)
    d_down_bias = jnp.sum(grad_flow, axis=0)
    d_activated = jnp.einsum("td,fd->tf", grad_low, w_down, preferred_element_type=jnp.float32)
    gelu_pull = jax.vjp(gelu_tanh, up_proj)[1]
    d_up = gelu_pull(d_activated)[0].astype(jnp.bfloat16)
    d_up_bias = jnp.sum(d_up.astype(jnp.float32), axis=0)
    d_w_up = jnp.einsum("td,tf->df", normed_two, d_up, preferred_element_type=jnp.float32)
    d_normed_two = tensor_norm_grad(
        jnp.einsum("tf,df->td", d_up, w_up, preferred_element_type=jnp.float32)
    )
    norm_pull_two = jax.vjp(normalize, after_attn, gains[1], shifts[1])[1]
    d_after, d_gain_two, d_shift_two = norm_pull_two(d_normed_two)
    grad_mid = grad_flow + d_after
    mid_low = grad_mid.astype(jnp.bfloat16)
    d_out_bias = jnp.sum(grad_mid, axis=0)
    d_w_out, stacked, d_w_qkv, d_q_bias, d_v_bias = attend_back(
        mid_low,
        normed,
        query,
        all_keys,
        all_values,
        query_ids,
        key_ids,
        row_max,
        row_total,
        mixed,
        w_out,
        head_dim,
    )
    d_normed = tensor_norm_grad(
        jnp.einsum("stc,sdc->td", stacked, w_qkv, preferred_element_type=jnp.float32)
    )
    norm_pull_one = jax.vjp(normalize, stream, gains[0], shifts[0])[1]
    d_stream, d_gain_one, d_shift_one = norm_pull_one(d_normed)
    pieces = (
        jnp.stack([d_gain_one, d_gain_two]),
        jnp.stack([d_shift_one, d_shift_two]),
        d_w_qkv,
        d_q_bias,
        d_v_bias,
        d_w_out,
        d_out_bias,
        d_w_up,
        d_up_bias,
        d_w_down,
        d_down_bias,
    )
    return (grad_mid + d_stream, pieces)


def local(
    inputs,
    picture_ids,
    cotangent,
    norm_gain,
    norm_bias,
    w_qkv,
    q_bias,
    v_bias,
    w_out,
    out_bias,
    w_up,
    up_bias,
    w_down,
    down_bias,
):
    head_dim = HEAD_DIM
    layers = w_qkv.shape[0]
    batches = inputs.shape[0]
    weight_set = (
        norm_gain,
        norm_bias,
        w_qkv,
        q_bias,
        v_bias,
        w_out,
        out_bias,
        w_up,
        up_bias,
        w_down,
        down_bias,
    )
    totals = [None for layer_index in range(layers)]
    output_rows = []
    input_rows = []
    for micro_batch in range(batches):
        slot_ids = picture_ids[micro_batch]
        id_floats = slot_ids.astype(jnp.bfloat16)
        stream = inputs[micro_batch].astype(jnp.float32)
        grad_flow = cotangent[micro_batch].astype(jnp.float32) * (slot_ids >= 0)[:, None].astype(
            jnp.float32
        )
        kept_all = []
        for layer_index in range(layers):
            params = tuple((item[layer_index] for item in weight_set))
            stream, kept_values = layer_forward(stream, id_floats, params, head_dim)
            kept_all.append(kept_values)
        output_rows.append(stream.astype(jnp.bfloat16))
        for layer_index in reversed(range(layers)):
            params = tuple((item[layer_index] for item in weight_set))
            grad_flow, pieces = layer_backward(grad_flow, kept_all[layer_index], params, head_dim)
            if totals[layer_index] is None:
                totals[layer_index] = pieces
            else:
                totals[layer_index] = tuple(
                    (
                        first_term + second_term
                        for first_term, second_term in zip(totals[layer_index], pieces)
                    )
                )
        input_rows.append(grad_flow)
    count_each = len(totals[0])
    flat_grads = tuple((item for piece_set in totals for item in piece_set))
    flat_summed = tuple(
        jax.tree.map(
            lambda part: part.astype(jnp.float32), lax.psum(as_sent(flat_grads), ("dp", "seq"))
        )
    )
    summed = [
        list(flat_summed[layer_index * count_each : (layer_index + 1) * count_each])
        for layer_index in range(layers)
    ]
    stacked_grads = tuple(
        (
            jnp.stack([summed[layer_index][position] for layer_index in range(layers)])
            for position in range(len(summed[0]))
        )
    )
    return (
        jnp.stack(output_rows),
        jnp.stack(input_rows),
        stacked_grads[0],
        stacked_grads[1],
        stacked_grads[2],
        stacked_grads[3],
        stacked_grads[4],
        stacked_grads[5],
        stacked_grads[6],
        stacked_grads[7],
        stacked_grads[8],
        stacked_grads[9],
        stacked_grads[10],
    )


def solution(mesh):
    placed = (
        P("dp", "seq", None),
        P("dp", "seq"),
        P("dp", "seq", None),
        P(),
        P(),
        P(None, None, None, "tensor"),
        P(None, "tensor"),
        P(None, "tensor"),
        P(None, "tensor", None),
        P(),
        P(None, None, "tensor"),
        P(None, "tensor"),
        P(None, "tensor", None),
        P(),
    )
    return jax.shard_map(
        local,
        mesh=mesh,
        in_specs=placed,
        out_specs=(
            P("dp", "seq", None),
            P("dp", "seq", None),
            P(),
            P(),
            P(None, None, None, "tensor"),
            P(None, "tensor"),
            P(None, "tensor"),
            P(None, "tensor", None),
            P(),
            P(None, None, "tensor"),
            P(None, "tensor"),
            P(None, "tensor", None),
            P(),
        ),
        check_vma=False,
    )
```

profile of v0, /device:TPU:9, one launch (start us, length us, event | category | flops | bytes accessed | tf_op | source)
XLA Modules:
  0.0 1479.8 jit_solution(8325555674960073599)
XLA Ops:
  13.2 2.6 fusion.572
  20.1 8.1 fusion.571
  38.6 8.1 fusion.570
  47.4 3.1 copy.44
  59.1 54.0 %all-reduce.48.cloned.1.call-done = (bf16[256,1152]{1,0:T(8,128)(2,1)}, bf16[256,1152]{1,0:T(8,128)(2,1)}) async-done(((bf16[256,1152]{1,0:T(8,128)(2,1)}, bf16[256,1152]{1,0:T(8,128)(2,1)}), (bf16[256,1152]{1,0:T(8,128)(2,1)}, bf16[256,1152]{1,0:T(8,128)(2,1)})) %all-reduce.48.cloned.1.call-update) | async-done | bytes 1179664 | tf_op jit(solution)/shard_map/psum | solution.py:61
  113.2 2.5 fusion.212
  123.2 71.4 %all-reduce.24.cloned.1.call-done = bf16[256,1152]{1,0:T(8,128)(2,1)} async-done(((bf16[256,1152]{1,0:T(8,128)(2,1)}), bf16[256,1152]{1,0:T(8,128)(2,1)}) %all-reduce.24.cloned.1.call-update) | async-done | bytes 589840 | tf_op jit(solution)/shard_map/psum | solution.py:61
  198.7 5.7 collective-permute-start.8
  215.3 67.1 %all-reduce.26.cloned.1.call-done = bf16[256,1152]{1,0:T(8,128)(2,1)} async-done(((bf16[256,1152]{1,0:T(8,128)(2,1)}), bf16[256,1152]{1,0:T(8,128)(2,1)}) %all-reduce.26.cloned.1.call-update) | async-done | bytes 589840 | tf_op jit(solution)/shard_map/psum | solution.py:61
  285.9 2.7 convert_reduce_fusion.16
  291.0 6.0 collective-permute-start.10
  297.9 3.0 fusion.577
  300.9 64.8 %all-reduce.28.cloned.1.call-done = bf16[256,1152]{1,0:T(8,128)(2,1)} async-done(((bf16[256,1152]{1,0:T(8,128)(2,1)}), bf16[256,1152]{1,0:T(8,128)(2,1)}) %all-reduce.28.cloned.1.call-update) | async-done | bytes 589840 | tf_op jit(solution)/shard_map/psum | solution.py:65
  365.7 2.6 convert_reduce_fusion.7
  377.0 5.8 collective-permute-start.20
  382.7 5.5 convolution_bitcast_fusion.13
  388.3 5.7 convert_reduce_fusion.28
  398.2 2.6 fusion.26
  405.8 64.3 %all-reduce.30.cloned.1.call-done = bf16[256,1152]{1,0:T(8,128)(2,1)} async-done(((bf16[256,1152]{1,0:T(8,128)(2,1)}), bf16[256,1152]{1,0:T(8,128)(2,1)}) %all-reduce.30.cloned.1.call-update) | async-done | bytes 589840 | tf_op jit(solution)/shard_map/psum | solution.py:65
  480.6 75.9 %all-reduce.46.cloned.1.call-done = (bf16[256,1152]{1,0:T(8,128)(2,1)}, bf16[256,1152]{1,0:T(8,128)(2,1)}) async-done(((bf16[256,1152]{1,0:T(8,128)(2,1)}, bf16[256,1152]{1,0:T(8,128)(2,1)}), (bf16[256,1152]{1,0:T(8,128)(2,1)}, bf16[256,1152]{1,0:T(8,128)(2,1)})) %all-reduce.46.cloned.1.call-update) | async-done | bytes 1179664 | tf_op jit(solution)/shard_map/psum | solution.py:65
  556.5 3.1 fusion.127
  566.7 77.6 %all-reduce.44.cloned.1.call-done = (bf16[256,1152]{1,0:T(8,128)(2,1)}, bf16[256,1152]{1,0:T(8,128)(2,1)}) async-done(((bf16[256,1152]{1,0:T(8,128)(2,1)}, bf16[256,1152]{1,0:T(8,128)(2,1)}), (bf16[256,1152]{1,0:T(8,128)(2,1)}, bf16[256,1152]{1,0:T(8,128)(2,1)})) %all-reduce.44.cloned.1.call-update) | async-done | bytes 1179664 | tf_op jit(solution)/shard_map/psum | solution.py:61
  651.4 5.8 collective-permute-start.14
  659.2 3.1 fusion.579
  663.9 2.5 convolution_convert_fusion.34
  668.0 3.1 fusion.578
  679.9 3.1 convolution_convert_fusion.10
  687.8 64.0 %all-reduce.42.cloned.1.call-done = (bf16[256,1152]{1,0:T(8,128)(2,1)}, bf16[256,1152]{1,0:T(8,128)(2,1)}) async-done(((bf16[256,1152]{1,0:T(8,128)(2,1)}, bf16[256,1152]{1,0:T(8,128)(2,1)}), (bf16[256,1152]{1,0:T(8,128)(2,1)}, bf16[256,1152]{1,0:T(8,128)(2,1)})) %all-reduce.42.cloned.1.call-update) | async-done | bytes 1179664 | tf_op jit(solution)/shard_map/psum | solution.py:61
  768.8 2.8 convolution_add_fusion.1
  771.7 2.8 fusion.18
  774.8 3.1 convolution_convert_fusion.14
  782.4 69.7 %all-reduce.40.cloned.1.call-done = (bf16[256,1152]{1,0:T(8,128)(2,1)}, bf16[256,1152]{1,0:T(8,128)(2,1)}) async-done(((bf16[256,1152]{1,0:T(8,128)(2,1)}, bf16[256,1152]{1,0:T(8,128)(2,1)}), (bf16[256,1152]{1,0:T(8,128)(2,1)}, bf16[256,1152]{1,0:T(8,128)(2,1)})) %all-reduce.40.cloned.1.call-update) | async-done | bytes 1179664 | tf_op jit(solution)/shard_map/psum | solution.py:65
  852.2 3.3 convert_reduce_fusion.11
  857.3 2.6 fusion.560
  866.9 5.8 convert_reduce_fusion.29
  872.6 5.5 convolution_bitcast_fusion.17
  880.5 2.5 convolution_bitcast_fusion.8
  885.2 5.8 convert_reduce_fusion.27
  891.0 5.5 convolution_bitcast_fusion.9
  897.5 5.8 collective-permute-start.24
  904.3 2.7 convolution_add_fusion.13
  914.1 2.5 fusion.32
  928.2 57.9 %all-reduce.38.cloned.1.call-done = (bf16[256,1152]{1,0:T(8,128)(2,1)}, bf16[256,1152]{1,0:T(8,128)(2,1)}) async-done(((bf16[256,1152]{1,0:T(8,128)(2,1)}, bf16[256,1152]{1,0:T(8,128)(2,1)}), (bf16[256,1152]{1,0:T(8,128)(2,1)}, bf16[256,1152]{1,0:T(8,128)(2,1)})) %all-reduce.38.cloned.1.call-update) | async-done | bytes 1179664 | tf_op jit(solution)/shard_map/psum | solution.py:65
  986.1 3.3 convert_reduce_fusion.10
  999.4 3.4 fusion.22
  1008.0 68.7 %all-reduce.36.cloned.1.call-done = (bf16[256,1152]{1,0:T(8,128)(2,1)}, bf16[256,1152]{1,0:T(8,128)(2,1)}) async-done(((bf16[256,1152]{1,0:T(8,128)(2,1)}, bf16[256,1152]{1,0:T(8,128)(2,1)}), (bf16[256,1152]{1,0:T(8,128)(2,1)}, bf16[256,1152]{1,0:T(8,128)(2,1)})) %all-reduce.36.cloned.1.call-update) | async-done | bytes 1179664 | tf_op jit(solution)/shard_map/psum | solution.py:65
  1076.8 3.5 fusion.175
  1082.6 2.8 fusion.555
  1091.1 5.7 convert_reduce_fusion.31
  1096.9 5.5 convolution_bitcast_fusion.11
  1109.4 5.8 convert_reduce_fusion.30
  1115.2 5.5 convolution_bitcast_fusion.7
  1121.4 2.7 fusion.556
  1125.1 2.5 convolution_bitcast_fusion.14
  1131.4 6.1 collective-permute-start.22
  1137.5 5.6 convolution_bitcast_fusion.15
  1143.1 5.8 convert_reduce_fusion.32
  1160.8 3.0 convolution_add_fusion.3
  1181.5 73.8 %all-reduce.34.cloned.1.call-done = (bf16[256,1152]{1,0:T(8,128)(2,1)}, bf16[256,1152]{1,0:T(8,128)(2,1)}, bf16[256,1152]{1,0:T(8,128)(2,1)}, bf16[256,1152]{1,0...) async-done(((bf16[256,1152]{1,0:T(8,128)(2,1)}, bf16[256,1152]{1,0:T(8,128)(2,1)}, bf16[256,1152]{1,0:T(8,128)(2,1)}, bf16[256,1152]{1,0:T(8,128)(2,1)}, ...) | async-done | bytes 3538960 | tf_op jit(solution)/shard_map/psum | solution.py:61
  1261.9 57.3 %all-reduce = (bf16[1,2,1152]{2,1,0:T(2,128)(2,1)}, bf16[1,2,1152]{2,1,0:T(2,128)(2,1)}, bf16[1,2,1152]{2,1,0:T(2,128)(2,1)}, bf16[1,2,1152]{2,1,0:T(2,128)(2,1)...) all-reduce(bf16[1,2,1152]{2,1,0:T(2,128)(2,1)} %fusion.452, ...), channel_id=1, replica_groups=mesh['dp'=8,'seq'=2,'tensor'=8] {'dp','seq'}, use_global_device_ids=true, to_apply=%region_103.104 | all-reduce | flops 15476 | bytes 61904 | tf_op jit(solution)/shard_map/psum | solution.py:322
  1330.3 2.6 fusion.220
  1339.7 114.7 %all-reduce.32.cloned.1.call-done = (bf16[1,3,1152,144]{2,3,1,0:T(8,128)(2,1)}, bf16[1,3,1152,144]{2,3,1,0:T(8,128)(2,1)}, bf16[1,144,1152]{2,1,0:T(8,128)(2,1)}...) async-done(((bf16[1,3,1152,144]{2,3,1,0:T(8,128)(2,1)}, ...) | async-done | bytes 7612432 | tf_op jit(solution)/shard_map/psum | solution.py:322
  1456.4 6.1 copy.33
  1462.8 6.1 copy.34
  (1155 shorter events, 268.4 us)
Async XLA Ops:
  7.2 106.0 %all-reduce.48.cloned.1.call-start = ((), (), s32[]{:S(2)}) async-start(), calls=%async_computation.12 | async-start | bytes 2359296 | tf_op jit(solution)/shard_map/psum | solution.py:61
  8.6 20.1 %collective-permute-start.1 = (bf16[256]{0:T(256)(128)(2,1)S(1)}, bf16[256]{0:T(256)(128)(2,1)S(1)}, u32[]{:S(2)}, u32[]{:S(2)}) collective-permute-start(bf16[256]{0:T(256)(128)(2,1)S(1)} %get-tuple-element.120), channel_id=1, source_target_pairs={{0,8},{8,0},{1,9},{9,1},{2,10},{10,2},{3,11},{11,3},{4,12},{12,4},... | collective-permute-start | bytes 1544 | tf_op jit(solution)/shard_map/ppermute | solution.py:16
  9.3 110.4 %collective-permute-start.11 = (bf16[256]{0:T(256)(128)(2,1)}, bf16[256]{0:T(256)(128)(2,1)}, u32[]{:S(2)}, u32[]{:S(2)}) collective-permute-start(bf16[256]{0:T(256)(128)(2,1)} %get-tuple-element.121), channel_id=1, source_target_pairs={{0,8},{8,0},{1,9},{9,1},{2,10},{10,2},{3,11},{11,3},{4,12},{12,4},... | collective-permute-start | bytes 1544 | tf_op jit(solution)/shard_map/ppermute | solution.py:16
  9.3 19.1 %collective-permute-start.6 = (bf16[256]{0:T(256)(128)(2,1)S(1)}, bf16[256]{0:T(256)(128)(2,1)S(1)}, u32[]{:S(2)}, u32[]{:S(2)}) collective-permute-start(bf16[256]{0:T(256)(128)(2,1)S(1)} %get-tuple-element.122), channel_id=1, source_target_pairs={{0,8},{8,0},{1,9},{9,1},{2,10},{10,2},{3,11},{11,3},{4,12},{12,4},... | collective-permute-start | bytes 1544 | tf_op jit(solution)/shard_map/ppermute | solution.py:16
  16.7 99.5 %copy-start.102 = (f32[1152]{0:T(1024)}, f32[1152]{0:T(1024)S(1)}, u32[]{:S(2)}) copy-start(f32[1152]{0:T(1024)S(1)} %get-tuple-element.281) | copy-start | bytes 13828
  18.0 14.6 collective-permute-start.7
  18.7 10.8 collective-permute-start.2
  19.4 8.8 copy-start.318
  20.0 8.2 copy-start.322
  28.3 8.0 copy-start.184
  28.4 7.9 collective-permute-start.5
  28.7 7.7 copy-start.178
  28.7 2.4 collective-permute-start
  37.1 9.6 copy-start.132
  38.4 156.2 %all-reduce.24.cloned.1.call-start = ((), (), s32[]{:S(2)}) async-start(), calls=%async_computation | async-start | bytes 1179648 | tf_op jit(solution)/shard_map/psum | solution.py:61
  54.8 58.4 %copy-start.224 = (f32[256]{0:T(256)S(1)}, f32[256]{0:T(256)}, u32[]{:S(2)}) copy-start(f32[256]{0:T(256)} %get-tuple-element.277) | copy-start | bytes 3076
  56.6 59.5 %copy-start.364 = (f32[538]{0:T(1024)}, f32[538]{0:T(1024)S(1)}, u32[]{:S(2)}) copy-start(f32[538]{0:T(1024)S(1)} %get-tuple-element.119) | copy-start | bytes 6460
  119.7 162.7 %all-reduce.26.cloned.1.call-start = ((), (), s32[]{:S(2)}) async-start(), calls=%async_computation.1 | async-start | bytes 1179648 | tf_op jit(solution)/shard_map/psum | solution.py:61
  198.7 9.4 collective-permute-start.8
  204.3 1.3 collective-permute-start.9
  213.0 69.4 %copy-start.179 = (f32[1152]{0:T(1024)S(1)}, f32[1152]{0:T(1024)}, u32[]{:S(2)}) copy-start(f32[1152]{0:T(1024)} %get-tuple-element.116) | copy-start | bytes 13828
  213.0 152.7 %all-reduce.28.cloned.1.call-start = ((), (), s32[]{:S(2)}) async-start(), calls=%async_computation.2 | async-start | bytes 1179648 | tf_op jit(solution)/shard_map/psum | solution.py:65
  214.9 82.0 %collective-permute-start.12 = (bf16[256,144]{0,1:T(8,128)(2,1)S(1)}, bf16[256,144]{0,1:T(8,128)(2,1)}, u32[]{:S(2)}, u32[]{:S(2)}) collective-permute-start(bf16[256,144]{0,1:T(8,128)(2,1)S(1)} %fusion.440), channel_id=1, source_target_pairs={{0,8},{8,0},{1,9},{9,1},{2,10},{10,2},{3,11},{11,3},{4,12},{12,4},... | collective-permute-start | bytes 221192 | tf_op jit(solution)/shard_map/ppermute | solution.py:16
  283.8 85.6 %copy-start.199 = (f32[256]{0:T(256)}, f32[256]{0:T(256)S(1)}, u32[]{:S(2)}) copy-start(f32[256]{0:T(256)S(1)} %broadcast_multiply_fusion.4) | copy-start | bytes 3076
  284.1 85.4 %copy-start.291 = (f32[256]{0:T(256)}, f32[256]{0:T(256)S(1)}, u32[]{:S(2)}) copy-start(f32[256]{0:T(256)S(1)} %fusion.473) | copy-start | bytes 3076
  290.8 179.3 %all-reduce.30.cloned.1.call-start = ((), (), s32[]{:S(2)}) async-start(), calls=%async_computation.3 | async-start | bytes 1179648 | tf_op jit(solution)/shard_map/psum | solution.py:65
  291.0 77.3 %copy-start.185 = (bf16[256,2,72]{0,2,1:T(8,128)(2,1)}, bf16[256,2,72]{0,2,1:T(8,128)(2,1)S(1)}, u32[]{:S(2)}) copy-start(bf16[256,2,72]{0,2,1:T(8,128)(2,1)S(1)} %add_convert_fusion.13) | copy-start | bytes 221188
  291.0 109.9 %collective-permute-start.10 = (bf16[256,144]{0,1:T(8,128)(2,1)S(1)}, bf16[256,144]{0,1:T(8,128)(2,1)}, u32[]{:S(2)}, u32[]{:S(2)}) collective-permute-start(bf16[256,144]{0,1:T(8,128)(2,1)S(1)} %fusion.403), channel_id=1, source_target_pairs={{0,8},{8,0},{1,9},{9,1},{2,10},{10,2},{3,11},{11,3},{4,12},{12,4},... | collective-permute-start | bytes 221192 | tf_op jit(solution)/shard_map/ppermute | solution.py:16
  297.9 70.4 %copy-start.161 = (bf16[512,144]{0,1:T(8,128)(2,1)}, bf16[512,144]{0,1:T(8,128)(2,1)S(1)}, u32[]{:S(2)}) copy-start(bf16[512,144]{0,1:T(8,128)(2,1)S(1)} %pad_maximum_fusion.17) | copy-start | bytes 442372
  377.0 19.9 %collective-permute-start.20 = (bf16[256,144]{0,1:T(8,128)(2,1)S(1)}, bf16[256,144]{0,1:T(8,128)(2,1)}, u32[]{:S(2)}, u32[]{:S(2)}) collective-permute-start(bf16[256,144]{0,1:T(8,128)(2,1)S(1)} %bitcast.908), channel_id=1, source_target_pairs={{0,8},{8,0},{1,9},{9,1},{2,10},{10,2},{3,11},{11,3},{4,12},{12,4},... | collective-permute-start | bytes 221192 | tf_op jit(solution)/shard_map/ppermute | solution.py:16
  396.8 1.3 collective-permute-start.19
  400.8 155.6 %all-reduce.46.cloned.1.call-start = ((), (), s32[]{:S(2)}) async-start(), calls=%async_computation.11 | async-start | bytes 2359296 | tf_op jit(solution)/shard_map/psum | solution.py:65
  401.8 68.3 %copy-start.197 = (f32[256]{0:T(256)S(1)}, f32[256]{0:T(256)}, u32[]{:S(2)}) copy-start(f32[256]{0:T(256)} %copy-done.196) | copy-start | bytes 3076
  403.6 68.7 %copy-start.134 = (bf16[2,72,256]{2,1,0:T(8,128)(2,1)}, bf16[2,72,256]{2,1,0:T(8,128)(2,1)S(1)}, u32[]{:S(2)}) copy-start(bf16[2,72,256]{2,1,0:T(8,128)(2,1)S(1)} %convolution_convert_fusion.31) | copy-start | bytes 221188
  403.6 68.7 %copy-start.339 = (f32[256]{0:T(256)S(1)}, f32[256]{0:T(256)}, u32[]{:S(2)}) copy-start(f32[256]{0:T(256)} %copy-done.338) | copy-start | bytes 3076
  403.6 68.7 %copy-start.272 = (f32[256]{0:T(256)S(1)}, f32[256]{0:T(256)}, u32[]{:S(2)}) copy-start(f32[256]{0:T(256)} %copy-done.271) | copy-start | bytes 3076
  477.3 79.1 %copy-start.15 = (bf16[256,1152]{1,0:T(8,128)(2,1)S(1)}, bf16[256,1152]{1,0:T(8,128)(2,1)}, u32[]{:S(2)}) copy-start(bf16[256,1152]{1,0:T(8,128)(2,1)} %get-tuple-element.165) | copy-start | bytes 1769476
  478.9 165.4 %all-reduce.44.cloned.1.call-start = ((), (), s32[]{:S(2)}) async-start(), calls=%async_computation.10 | async-start | bytes 2359296 | tf_op jit(solution)/shard_map/psum | solution.py:61
  566.6 185.2 %all-reduce.42.cloned.1.call-start = ((), (), s32[]{:S(2)}) async-start(), calls=%async_computation.9 | async-start | bytes 2359296 | tf_op jit(solution)/shard_map/psum | solution.py:61
  649.9 7.8 copy-start.317
  651.4 15.0 %collective-permute-start.14 = (bf16[256,144]{0,1:T(8,128)(2,1)}, bf16[256,144]{0,1:T(8,128)(2,1)}, u32[]{:S(2)}, u32[]{:S(2)}) collective-permute-start(bf16[256,144]{0,1:T(8,128)(2,1)} %fusion.441), channel_id=1, source_target_pairs={{0,8},{8,0},{1,9},{9,1},{2,10},{10,2},{3,11},{11,3},{4,12},{12,4},... | collective-permute-start | bytes 221192 | tf_op jit(solution)/shard_map/ppermute | solution.py:16
  657.1 1.4 collective-permute-start.4
  657.2 5.0 collective-permute-start.3
  657.6 15.6 %collective-permute-start.13 = (bf16[256,144]{0,1:T(8,128)(2,1)}, bf16[256,144]{0,1:T(8,128)(2,1)}, u32[]{:S(2)}, u32[]{:S(2)}) collective-permute-start(bf16[256,144]{0,1:T(8,128)(2,1)} %get-tuple-element.236), channel_id=1, source_target_pairs={{0,8},{8,0},{1,9},{9,1},{2,10},{10,2},{3,11},{11,3},{4,12},{12,4},... | collective-permute-start | bytes 221192 | tf_op jit(solution)/shard_map/ppermute | solution.py:16
  679.5 172.6 %all-reduce.40.cloned.1.call-start = ((), (), s32[]{:S(2)}) async-start(), calls=%async_computation.8 | async-start | bytes 2359296 | tf_op jit(solution)/shard_map/psum | solution.py:65
  679.9 7.4 copy-start.333
  774.5 211.5 %all-reduce.38.cloned.1.call-start = ((), (), s32[]{:S(2)}) async-start(), calls=%async_computation.7 | async-start | bytes 2359296 | tf_op jit(solution)/shard_map/psum | solution.py:65
  897.5 14.5 collective-permute-start.24
  904.2 5.0 collective-permute-start.16
  907.0 5.0 collective-permute-start.23
  908.7 1.8 collective-permute-start.15
  914.0 162.7 %all-reduce.36.cloned.1.call-start = ((), (), s32[]{:S(2)}) async-start(), calls=%async_computation.6 | async-start | bytes 2359296 | tf_op jit(solution)/shard_map/psum | solution.py:65
  999.0 256.3 %all-reduce.34.cloned.1.call-start = ((), (), s32[]{:S(2)}) async-start(), calls=%async_computation.5 | async-start | bytes 7077888 | tf_op jit(solution)/shard_map/psum | solution.py:61
  1005.9 70.8 %copy-start.17 = (bf16[256,1152]{1,0:T(8,128)(2,1)S(1)}, bf16[256,1152]{1,0:T(8,128)(2,1)}, u32[]{:S(2)}) copy-start(bf16[256,1152]{1,0:T(8,128)(2,1)} %get-tuple-element.164) | copy-start | bytes 1769476
  1005.9 70.8 %copy-start.19 = (bf16[256,1152]{1,0:T(8,128)(2,1)S(1)}, bf16[256,1152]{1,0:T(8,128)(2,1)}, u32[]{:S(2)}) copy-start(bf16[256,1152]{1,0:T(8,128)(2,1)} %get-tuple-element.166) | copy-start | bytes 1769476
  1005.9 70.8 %copy-start.104 = (f32[1152]{0:T(1024)S(1)}, f32[1152]{0:T(1024)}, u32[]{:S(2)}) copy-start(f32[1152]{0:T(1024)} %copy-done.102) | copy-start | bytes 13828
  1131.4 21.8 %collective-permute-start.22 = (bf16[256,144]{0,1:T(8,128)(2,1)}, bf16[256,144]{0,1:T(8,128)(2,1)}, u32[]{:S(2)}, u32[]{:S(2)}) collective-permute-start(bf16[256,144]{0,1:T(8,128)(2,1)} %bitcast.143), channel_id=1, source_target_pairs={{0,8},{8,0},{1,9},{9,1},{2,10},{10,2},{3,11},{11,3},{4,12},{12,4},... | collective-permute-start | bytes 221192 | tf_op jit(solution)/shard_map/ppermute | solution.py:16
  1152.1 5.1 collective-permute-start.18
  1152.2 3.5 collective-permute-start.26
  1152.7 1.5 collective-permute-start.21
  1152.8 3.0 collective-permute-start.25
  1153.2 4.0 collective-permute-start.17
  1159.3 295.0 %all-reduce.32.cloned.1.call-start = ((), (), s32[]{:S(2)}) async-start(), calls=%async_computation.4 | async-start | bytes 15335424 | tf_op jit(solution)/shard_map/psum | solution.py:322
  1258.1 72.2 %copy-start.4 = (f32[256,1152]{1,0:T(8,128)S(1)}, f32[256,1152]{1,0:T(8,128)}, u32[]{:S(2)}) copy-start(f32[256,1152]{1,0:T(8,128)} %copy-done.1) | copy-start | bytes 3538948
  (364 other events, 900.6 us)
Sparse Core Ops, SparseCore 0:
  38.5 74.6 all-reduce.47
  119.8 74.7 all-reduce.23
  213.1 69.1 all-reduce.25
  291.0 74.6 all-reduce.27
  401.0 69.1 all-reduce.29
  479.0 77.4 all-reduce.45
  566.7 77.4 all-reduce.43
  679.7 72.1 all-reduce.41
  774.6 77.4 all-reduce.39
  914.2 71.8 all-reduce.37
  999.2 77.4 all-reduce.35
  1159.4 95.8 all-reduce.33
  1259.9 194.3 all-reduce.31
where the time goes:
time: 1490 us; the launch traced here: 1480 us
  waiting for transfers between devices  927 us (62%)
  matrix products  228 us (15%)
  other arithmetic  113 us (8%)
  local copies, waits for them, and re-layouts  94.1 us (6%)
  blocking collectives  57.3 us (4%)
  starting transfers between devices  42.4 us (3%)
  between operations  18.6 us (1%)
    psum x6, waiting for transfers between devices, tensor_branch(): lax.psum(partial_sum.astype(jnp.bfloat16), 'tensor').astype(jnp.float32)  408 us
    psum x6, waiting for transfers between devices, tensor_norm_grad(): lax.psum(partial_sum.astype(jnp.bfloat16), 'tensor').astype(jnp.float32)  401 us
    psum x1, waiting for transfers between devices, local(): lax.psum(as_sent(flat_grads), ('dp', 'seq'))  115 us
    psum x1, blocking collectives, local(): lax.psum(as_sent(flat_grads), ('dp', 'seq'))  57.3 us
    unnamed x764, local copies, waits for them, and re-layouts  43.4 us
    ppermute x27, starting transfers between devices, from_partner(): return lax.ppermute(value, axis, pairs)  40.7 us
    dot_general x6, matrix products, attend_back(): jnp.einsum('hqk,khd->qhd', d_raw, key_heads, preferred_element_type=jnp.f...  34.7 us
    dot_general x6, matrix products, attend_back(): jnp.einsum('hqk,qhd->khd', d_raw, query_heads, preferred_element_type=jnp...  33.2 us
  transfers between devices with their start and end apart: 40, of which 16 were waited for; matrix products, arithmetic and copies ran while one was open for 15% of the time, Pallas kernels for 0%

commit v1 on v0

v1 whole, which is shorter than its diff:
```python
import functools

import jax
import jax.numpy as jnp
from jax import lax
from jax.experimental import pallas as pl
from jax.experimental.pallas import tpu as pltpu
from jax.sharding import Mesh
from jax.sharding import PartitionSpec as P

HEAD_DIM = 72
SCALE = HEAD_DIM**-0.5
D = 1152
CW = 144
FW = 538
FP = 576
NA = 256
NB = 128
NT = NA + NB
CA = NA // 4
CB = NB // 4
EXTRA = 8
norm_eps = 1e-06
gelu_coef = 0.7978845608028654
bf16 = jnp.bfloat16
f32 = jnp.float32
SIZES = {"y": 4, "x": 4, "c": 2, "zl": 2, ("zh", "zl"): 4}
Z = ("zh", "zl")
VMEM_LIMIT = 50 * 1024 * 1024


def shift(value, axis, by):
    n = SIZES[axis]
    return lax.ppermute(value, axis, [(i, (i + by) % n) for i in range(n)])


def dot(a, b):
    return lax.dot_general(a, b, (((1,), (0,)), ((), ())), preferred_element_type=f32)


def dot_nt(a, b):
    return lax.dot_general(a, b, (((1,), (1,)), ((), ())), preferred_element_type=f32)


def dot_tn(a, b):
    return lax.dot_general(a, b, (((0,), (0,)), ((), ())), preferred_element_type=f32)


def after(value, anchor):
    return lax.optimization_barrier((value, anchor))[0]


def shaped(shape, dtype):
    return jax.ShapeDtypeStruct(shape, dtype)


CHUNK = CA + CB
SENDS = [shaped((CHUNK, D), bf16)] * 3 + [shaped((CHUNK, D), f32)]


def call(kernel, outs, *args, pos=None):
    specs = [pl.BlockSpec(memory_space=pltpu.VMEM)] * len(args)
    if pos is not None:
        specs = [pl.BlockSpec(memory_space=pltpu.SMEM)] + specs
        args = (pos, *args)
    return pl.pallas_call(
        kernel,
        out_shape=outs,
        in_specs=specs,
        out_specs=[pl.BlockSpec(memory_space=pltpu.VMEM)] * len(outs),
        compiler_params=pltpu.CompilerParams(vmem_limit_bytes=VMEM_LIMIT),
    )(*args)


def whole(chunks):
    if len(chunks) == 1:
        return chunks[0][...]
    return jnp.concatenate([r[:CA] for r in chunks] + [r[CA:] for r in chunks], axis=0)


def put_sends(total, outs):
    for k in range(4):
        ref = outs[k - 1]
        ref[:CA] = total[CA * k : CA * (k + 1)].astype(ref.dtype)
        ref[CA:] = total[NA + CB * k : NA + CB * (k + 1)].astype(ref.dtype)


def ids_kernel(pos, near, far, qid_a, kid_a, qid_b, kid_b):
    first = pos[0] == 0
    x = pos[1]

    def turned(row, n):
        rows = jnp.broadcast_to(row, (8, n))
        return pltpu.roll(rows, (n - x * (n // 4)) % n, axis=1)

    def half(ref):
        return turned(jnp.where(first, ref[0:1], ref[1:2]), NA)

    def quarter(ref, own):
        low, high = ref[2:3, :NB], ref[2:3, NB:]
        return turned(jnp.where(first == own, low, high), NB)

    a, b = half(near), quarter(near, True)
    qid_a[...] = a.astype(f32).T.astype(jnp.int32)
    qid_b[...] = b.astype(f32).T.astype(jnp.int32)
    kid_a[...] = jnp.concatenate([a, half(far)], axis=1)
    kid_b[...] = jnp.concatenate(
        [b, quarter(far, True), quarter(near, False), quarter(far, False)], axis=1
    )


def arrange_ids(pos, near, far):
    i32 = jnp.int32
    outs = [shaped((NA, 8), i32), shaped((8, 2 * NA), i32)]
    outs += [shaped((NB, 8), i32), shaped((8, 4 * NB), i32)]
    return call(ids_kernel, outs, near, far, pos=pos)


def arranged(pos, ref):
    zl, x = pos[0], pos[1]
    rows, quarters = [], []
    for k in range(4):
        a = lax.rem(x + k, 4)
        rows.append(ref[zl, pl.ds(pl.multiple_of(a * CA, CA), CA)])
        quarters.append(ref[2, pl.ds(pl.multiple_of(zl * NB + a * CB, CB), CB)])
    return jnp.concatenate(rows + quarters, axis=0)


def first_kernel(pos, inputs, gain, bias, normed, stream):
    v = arranged(pos, inputs).astype(f32)
    stream[:CA] = v[:CA]
    stream[CA:] = v[NA : NA + CB]
    mean = jnp.mean(v, axis=-1, keepdims=True)
    centred = v - mean
    var = jnp.mean(centred * centred, axis=-1, keepdims=True)
    out = centred * lax.rsqrt(var + norm_eps) * gain[0, 0:1] + bias[0, 0:1]
    normed[...] = out.astype(bf16)


def cotangent_kernel(pos, cotangent, qid_a, qid_b, low, grad, total):
    live = jnp.concatenate([qid_a[...], qid_b[...]], axis=0)[:, :1] >= 0
    v = jnp.where(live, arranged(pos, cotangent).astype(f32), 0.0)
    low[...] = v.astype(bf16)
    own = jnp.concatenate([v[:CA], v[NA : NA + CB]], axis=0)
    grad[...] = own
    total[...] = jnp.sum(own, axis=0, keepdims=True)


def place_kernel(pos, *refs):
    out = refs[8]
    for dz in range(2):
        zl = pos[0] if dz == 0 else 1 - pos[0]
        for k in range(4):
            a = lax.rem(pos[1] + k, 4)
            chunk = refs[dz * 4 + k]
            out[zl, pl.ds(pl.multiple_of(a * CA, CA), CA)] = chunk[:CA].astype(out.dtype)
            out[2, pl.ds(pl.multiple_of(zl * NB + a * CB, CB), CB)] = chunk[CA:].astype(out.dtype)


def placed_rows(pos, slots, dtype):
    return call(place_kernel, [shaped((3, NA, D), dtype)], *slots, pos=pos)[0]


def norm_kernel(layer, at, stream, own, r1, r2, r3, extra, gain, bias, x_out, n_out):
    x = stream[...] + (own[...] + r1[...].astype(f32) + r2[...].astype(f32) + r3[...].astype(f32))
    x = x + extra[layer : layer + 1]
    x_out[...] = x
    mean = jnp.mean(x, axis=-1, keepdims=True)
    centred = x - mean
    var = jnp.mean(centred * centred, axis=-1, keepdims=True)
    g, b = (ref[at[0], at[1] : at[1] + 1] for ref in (gain, bias))
    n_out[...] = (centred * lax.rsqrt(var + norm_eps) * g + b).astype(bf16)


def norm_step(layer, at, stream, got, extra, gain, bias):
    return call(
        functools.partial(norm_kernel, layer, at),
        [shaped((CHUNK, D), f32), shaped((CHUNK, D), bf16)],
        stream, *got, extra, gain, bias,
    )


def result_kernel(layer, stream, own, r1, r2, r3, extra, out):
    x = stream[...] + (own[...] + r1[...].astype(f32) + r2[...].astype(f32) + r3[...].astype(f32))
    out[...] = (x + extra[layer : layer + 1]).astype(bf16)


def norm_back_kernel(at, x_ref, own, r1, r2, r3, grad_ref, gain, out, low, sums):
    x = x_ref[...]
    d = own[...] + r1[...].astype(f32) + r2[...].astype(f32) + r3[...].astype(f32)
    mean = jnp.mean(x, axis=-1, keepdims=True)
    centred = x - mean
    var = jnp.mean(centred * centred, axis=-1, keepdims=True)
    r = lax.rsqrt(var + norm_eps)
    xh = centred * r
    e = d * gain[at[0], at[1] : at[1] + 1]
    inner = e - jnp.mean(e, axis=-1, keepdims=True)
    inner = inner - xh * jnp.mean(e * xh, axis=-1, keepdims=True)
    grad = grad_ref[...] + r * inner
    out[...] = grad
    low[...] = grad.astype(bf16)
    sums[0:1] = jnp.sum(d * xh, axis=0, keepdims=True)
    sums[1:2] = jnp.sum(d, axis=0, keepdims=True)
    sums[2:3] = jnp.sum(grad, axis=0, keepdims=True)


def norm_back(at, x, got, grad, gain):
    return call(
        functools.partial(norm_back_kernel, at),
        [shaped((CHUNK, D), f32), shaped((CHUNK, D), bf16), shaped((3, D), f32)],
        x, *got, grad, gain,
    )


def qkv_kernel(layer, n, *refs):
    chunks, (w0, wa, wb, qb0, qb1, vb0, vb1) = refs[:n], refs[n : n + 7]
    q_out, kv_out, part_out = refs[n + 7 : n + 10]
    nt = whole(chunks)
    if n > 1:
        refs[n + 10][...] = nt
    w1 = jnp.concatenate([wa[...], wb[...]], axis=0)
    for g, w, qb, vb in ((0, w0[...], qb0, vb0), (1, w1, qb1, vb1)):
        q_out[g] = (dot_nt(nt, w[:CW]) + qb[layer : layer + 1]).astype(bf16)
        key = dot_nt(w[CW : 2 * CW], nt).astype(bf16)
        value = (dot_nt(nt, w[2 * CW :]) + vb[layer : layer + 1]).T.astype(bf16)
        kv_out[g, 0] = key
        kv_out[g, 1] = value
        part_out[1 - g, 0] = key[:, NA:]
        part_out[1 - g, 1] = value[:, NA:]


def project(layer, chunks, own, far, biases):
    n = len(chunks)
    outs = [shaped((2, NT, CW), bf16), shaped((2, 2, CW, NT), bf16), shaped((2, 2, CW, NB), bf16)]
    if n > 1:
        outs.append(shaped((NT, D), bf16))
    got = call(functools.partial(qkv_kernel, layer, n), outs, *chunks, own, *far, *biases)
    return (*got[:3], got[3] if n > 1 else chunks[0])


def lane_mask(head):
    lane = lax.broadcasted_iota(jnp.int32, (1, CW), 1)
    return (lane < HEAD_DIM) if head == 0 else (lane >= HEAD_DIM)


def row_mask(head):
    place = lax.broadcasted_iota(jnp.int32, (CW, 1), 0)
    return (place < HEAD_DIM) if head == 0 else (place >= HEAD_DIM)


def masked(mask, value):
    return jnp.where(mask, value.astype(f32), 0.0).astype(bf16)


def probabilities(qm, keys, allowed):
    scores = jnp.where(allowed, dot(qm, keys) * SCALE, -1e30)
    expanded = jnp.exp(scores - jnp.max(scores, axis=-1, keepdims=True))
    return expanded / jnp.sum(expanded, axis=-1, keepdims=True)


def slot_mask(qid, kid):
    return (kid >= 0) & ((qid == kid) | (qid < 0))


def attend_kernel(first, count, blocks, *refs):
    n = len(blocks)
    q, kvs, (qid, kid, wo0, wo1) = refs[0], refs[1 : 1 + n], refs[1 + n : 5 + n]
    rest = refs[5 + n :]
    allowed = slot_mask(qid[:, :1], kid[:1])
    mixed_out = rest[0] if first == 0 else rest[1]
    total = None
    for g, wo in ((0, wo0), (1, wo1)):
        keys = jnp.concatenate([r[g, 0, :, b : b + m] for r, (b, m) in zip(kvs, blocks)], axis=1)
        values = jnp.concatenate([r[g, 1, :, b : b + m] for r, (b, m) in zip(kvs, blocks)], axis=1)
        query = q[g, first : first + count]
        mixed = None
        for head in range(2):
            mask = lane_mask(head)
            probs = probabilities(masked(mask, query), keys, allowed).astype(bf16)
            got = dot_nt(probs, values)
            mixed = got if head == 0 else jnp.where(mask, got, mixed)
        mixed = mixed.astype(bf16)
        mixed_out[g] = mixed
        part = dot(mixed, wo[...])
        total = part if total is None else total + part
    if first == 0:
        rest[1][...] = total
    else:
        put_sends(jnp.concatenate([rest[0][...], total], axis=0), rest[2:])


def attend_row(q, kvs, blocks, qid, kid, wo):
    return call(
        functools.partial(attend_kernel, 0, NA, blocks),
        [shaped((2, NA, CW), bf16), shaped((NA, D), f32)],
        q, *kvs, qid, kid, *wo,
    )


def attend_quarter(q, kvs, blocks, qid, kid, wo, total):
    return call(
        functools.partial(attend_kernel, NA, NB, blocks),
        [shaped((2, NB, CW), bf16), *SENDS],
        q, *kvs, qid, kid, *wo, total,
    )


def attend_back_kernel(
    c0, c1, c2, c3, q, kv, kvo, kvz, kvd, qid_a, kid_a, qid_b, kid_b, wo0, wo1,
    mid_out, dq_out, own_out, far_out, z_out,
):
    allowed_a = slot_mask(qid_a[:, :1], kid_a[:1])
    allowed_b = slot_mask(qid_b[:, :1], kid_b[:1])
    mid = whole((c0, c1, c2, c3))
    mid_out[...] = mid
    for g, wo in ((0, wo0), (1, wo1)):
        d_mixed = dot_nt(mid, wo[...]).astype(bf16)
        d_mixed_t = dot_nt(wo[...], mid).astype(bf16)
        query = q[g]
        query_t = query.astype(f32).T.astype(bf16)
        for part in range(2):
            if part == 0:
                allowed, lo, hi = allowed_a, 0, NA
                keys = jnp.concatenate([kv[g, 0, :, :NA], kvo[g, 0, :, :NA]], axis=1)
                values = jnp.concatenate([kv[g, 1, :, :NA], kvo[g, 1, :, :NA]], axis=1)
            else:
                allowed, lo, hi = allowed_b, NA, NT
                keys = jnp.concatenate(
                    [kv[g, 0, :, NA:], kvo[g, 0, :, NA:], kvz[g, 0], kvd[g, 0]], axis=1
                )
                values = jnp.concatenate(
                    [kv[g, 1, :, NA:], kvo[g, 1, :, NA:], kvz[g, 1], kvd[g, 1]], axis=1
                )
            dq, dk, dv = None, None, None
            for head in range(2):
                mask, rmask = lane_mask(head), row_mask(head)
                probs = probabilities(masked(mask, query[lo:hi]), keys, allowed)
                d_probs = dot(masked(mask, d_mixed[lo:hi]), values)
                inner = jnp.sum(d_probs * probs, axis=-1, keepdims=True)
                d_raw = (SCALE * probs * (d_probs - inner)).astype(bf16)
                got_q = dot_nt(keys, d_raw)
                got_k = dot(query_t[:, lo:hi], d_raw)
                got_v = dot(d_mixed_t[:, lo:hi], probs.astype(bf16))
                if head == 0:
                    dq, dk, dv = got_q, got_k, got_v
                else:
                    dq = jnp.where(rmask, got_q, dq)
                    dk = jnp.where(rmask, got_k, dk)
                    dv = jnp.where(rmask, got_v, dv)
            dq_out[g, :, lo:hi] = dq.astype(bf16)
            n = hi - lo
            for j, grad in ((0, dk), (1, dv)):
                own_out[g, j, :, lo:hi] = grad[:, :n]
                far_out[g, j, :, lo:hi] = grad[:, n : 2 * n].astype(bf16)
                if part == 1:
                    z_out[1 - g, j] = grad[:, 2 * n : 3 * n]
                    far_out[1 - g, j, :, NT:] = grad[:, 3 * n :].astype(bf16)


def attend_back(chunks, q, kv, kvo, kvz, kvd, ids, wo):
    return call(
        attend_back_kernel,
        [
            shaped((NT, D), bf16),
            shaped((2, CW, NT), bf16),
            shaped((2, 2, CW, NT), f32),
            shaped((2, 2, CW, NT + NB), bf16),
            shaped((2, 2, CW, NB), f32),
        ],
        *chunks, q, kv, kvo, kvz, kvd, *ids, *wo,
    )


def project_back_kernel(dq, own, far, dz, w0, wa, wb, stack_out, sums, *sends):
    total = None
    w1 = jnp.concatenate([wa[...], wb[...]], axis=0)
    for g, w in ((0, w0[...]), (1, w1)):
        stack_out[g, 0] = dq[g]
        sums[g, 0] = jnp.sum(dq[g].astype(f32), axis=-1, keepdims=True)
        for j in range(2):
            grad = own[g, j] + far[g, j, :, :NT].astype(f32)
            low = jnp.concatenate(
                [grad[:, :NA], grad[:, NA:] + dz[g, j].astype(f32)], axis=1
            ).astype(bf16)
            stack_out[g, 1 + j] = low
            if j == 1:
                sums[g, 1] = jnp.sum(low.astype(f32), axis=-1, keepdims=True)
        for j in range(3):
            part = dot_tn(stack_out[g, j], w[CW * j : CW * (j + 1)])
            total = part if total is None else total + part
    put_sends(total, sends)


def project_back(dq, own, far, dz, w0, w1):
    return call(
        project_back_kernel,
        [shaped((2, 3, CW, NT), bf16), shaped((2, 2, CW, 1), f32), *SENDS],
        dq, own, far, dz, w0, *w1,
    )


def mlp_kernel(layer, c0, c1, c2, c3, wu0, wu1, ub0, ub1, wd0, wd1, nt_out, up_out, act_out, *sends):
    nt = whole((c0, c1, c2, c3))
    nt_out[...] = nt
    total = None
    for g, wu, ub, wd in ((0, wu0, ub0, wd0), (1, wu1, ub1, wd1)):
        u = dot_nt(nt, wu[...]) + ub[layer : layer + 1]
        up_out[g] = u
        act = (0.5 * u * (1.0 + jnp.tanh(gelu_coef * (u + 0.044715 * u * u * u)))).astype(bf16)
        act_out[g] = act
        part = dot(act, wd[...])
        total = part if total is None else total + part
    put_sends(total, sends)


def mlp(layer, chunks, own, oth, ub0, ub1):
    return call(
        functools.partial(mlp_kernel, layer),
        [
            shaped((NT, D), bf16),
            shaped((2, NT, FP), f32),
            shaped((2, NT, FP), bf16),
            *SENDS,
        ],
        *chunks, own[2], oth[2], ub0, ub1, own[3], oth[3],
    )


def mlp_back_kernel(n, *refs):
    chunks, (up, wu0, wu1, wd0, wd1) = refs[:n], refs[n : n + 5]
    d_up_out, sums = refs[n + 5 : n + 7]
    sends = refs[n + 7 : n + 11]
    low = whole(chunks)
    if n > 1:
        refs[n + 11][...] = low
    total = None
    for g, wu, wd in ((0, wu0, wd0), (1, wu1, wd1)):
        d_act = dot_nt(low, wd[...])
        u = up[g]
        t = jnp.tanh(gelu_coef * (u + 0.044715 * u * u * u))
        slope = 0.5 * (1.0 + t) + 0.5 * u * (1.0 - t * t) * (
            gelu_coef * (1.0 + 3 * 0.044715 * u * u)
        )
        d_up = (d_act * slope).astype(bf16)
        d_up_out[g] = d_up
        sums[g] = jnp.sum(d_up.astype(f32), axis=0, keepdims=True)
        part = dot(d_up, wu[...])
        total = part if total is None else total + part
    put_sends(total, sends)


def mlp_back(chunks, up, own, oth):
    n = len(chunks)
    outs = [shaped((2, NT, FP), bf16), shaped((2, 1, FP), f32), *SENDS]
    if n > 1:
        outs.append(shaped((NT, D), bf16))
    got = call(
        functools.partial(mlp_back_kernel, n), outs, *chunks, up, own[2], oth[2], own[3], oth[3]
    )
    return got[0], got[1], got[2:6], (got[6] if n > 1 else chunks[0])


def mlp_weights_kernel(pos, d_up, act, nt, low, keep_out, sent_out):
    first = pos[2] == 0
    for j, (a, b) in enumerate(((d_up, nt), (act, low))):
        for out, g in ((keep_out, 0), (sent_out, 1)):
            picked = jnp.where(first, a[g], a[1 - g])
            out[j] = dot_tn(picked, b[...]).astype(bf16)


def attend_weights_kernel(
    pos, stacked, mixed_a, mixed_b, normed, mid, wide, near, beside, keep_out, sent_out
):
    first = pos[2] == 0
    for out, g in ((keep_out, 0), (sent_out, 1)):
        for j in range(3):
            picked = jnp.where(first, stacked[g, j], stacked[1 - g, j])
            out[j, :CW] = dot(picked, normed[...]).astype(bf16)
        mixed = [jnp.concatenate([mixed_a[i], mixed_b[i]], axis=0) for i in (g, 1 - g)]
        out[3, :CW] = dot_tn(jnp.where(first, mixed[0], mixed[1]), mid[...]).astype(bf16)
        extra = (near, beside) if g == 0 else (beside, near)
        extra = jnp.where(first, extra[0][...], extra[1][...])
        if g == 0:
            extra = extra + wide[...]
        out[:, CW:] = extra.astype(bf16)


def plain_weights_kernel(pos, stacked, mixed_a, mixed_b, normed, mid, keep_out, sent_out):
    first = pos[2] == 0
    for out, g in ((keep_out, 0), (sent_out, 1)):
        for j in range(3):
            picked = jnp.where(first, stacked[g, j], stacked[1 - g, j])
            out[j] = dot(picked, normed[...]).astype(bf16)
        mixed = [jnp.concatenate([mixed_a[i], mixed_b[i]], axis=0) for i in (g, 1 - g)]
        out[3] = dot_tn(jnp.where(first, mixed[0], mixed[1]), mid[...]).astype(bf16)


def mlp_final_kernel(pos, full0, other0, full1, other1, up, down):
    first = pos[2] == 0
    for layer, (full, other) in enumerate(((full0, other0), (full1, other1))):
        for j, out in enumerate((up, down)):
            got = jnp.where(first, full[j], other[j])
            out[:, layer, :] = got[:FW].astype(f32)


def mlp_final(pos, sums):
    args = [part for total in sums for part in total]
    return call(mlp_final_kernel, [shaped((FW, 2, D), f32)] * 2, *args, pos=pos)


def attend_final_kernel(pos, full0, other0, full1, other1, qkv, out, wide, narrow):
    first = pos[2] == 0
    for layer, (full, other) in enumerate(((full0, other0), (full1, other1))):
        got = jnp.where(first, full[...], other[...]).astype(f32)
        for j in range(3):
            qkv[layer, j] = got[j, :CW]
        out[layer] = got[3, :CW]
        if layer == 0:
            narrow[...] = got[:, CW:]
            wide[...] = got[:, CW:].astype(bf16)


def attend_final(pos, sums):
    args = [part for total in sums for part in total]
    outs = [shaped((2, 3, CW, D), f32), shaped((2, CW, D), f32)]
    outs += [shaped((4, EXTRA, D), bf16), shaped((4, EXTRA, D), f32)]
    return call(attend_final_kernel, outs, *args, pos=pos)


def gather_x(chunk):
    return [chunk] + [shift(chunk, "x", -k) for k in (1, 2, 3)]


def scatter_x(sends):
    return [sends[3]] + [shift(sends[k - 1], "x", k) for k in (1, 2, 3)]


def rolled(blocks, by):
    return lax.dynamic_slice_in_dim(jnp.concatenate([blocks, blocks], axis=0), by, 4, axis=0)


def pieces_of(value, index):
    return [
        lax.dynamic_index_in_dim(value, (index + k) % 4, 0, keepdims=False) for k in range(4)
    ]


def scatter_ring(pieces, axis):
    return [pieces[0]] + [shift(pieces[k], axis, k) for k in (1, 2, 3)]


def gather_ring(piece, axis, some):
    got = [piece]
    for k in (1, 2, 3):
        if not some:
            got.append(shift(piece, axis, -k))
        elif axis == "y":
            pairs = [
                (((y + k) % 4) * 4 + e, y * 4 + e) for y in range(4) for e in (0, 3)
            ]
            got.append(lax.ppermute(piece, ("y", "c", "zl"), pairs))
        else:
            pairs = []
            for z in range(4):
                c = z % 2
                src = (z + k) % 4
                pairs.append(
                    ((src // 2) * 4 + c * 2 + src % 2, (z // 2) * 4 + c * 2 + z % 2)
                )
            got.append(lax.ppermute(piece, ("zh", "c", "zl"), pairs))
    return got


def total_of(parts):
    return sum(part.astype(f32) for part in parts).astype(bf16)


class WeightSum:
    def __init__(self, kept, sent, where, y_first, direct):
        y, z = where
        self.one, self.two = (("y", y), (Z, z)) if y_first else ((Z, z), ("y", y))
        self.shape = kept.shape
        self.rows = kept.shape[0] * kept.shape[1] // 4
        self.direct = direct
        self.pending = (kept, shift(sent, "c", 1))
        self.step = 0

    def advance(self, anchor, late=None):
        pending = self.pending if anchor is None else after(self.pending, anchor)
        step, self.step = self.step, self.step + 1
        r = self.rows
        if step == 0:
            both = total_of(pending if late is None else (*pending, late)).reshape(4, r, D)
            feed = pieces_of(both, self.one[1])
            self.pending = scatter_ring(feed, self.one[0])
        elif step == 1 and self.direct:
            feed = total_of(pending)
            self.pending = [feed] + [shift(feed, self.two[0], k) for k in (1, 2, 3)]
            self.step += 1
        elif step == 1:
            piece = total_of(pending).reshape(4, r // 4, D)
            feed = pieces_of(piece, self.two[1])
            self.pending = scatter_ring(feed, self.two[0])
        elif step == 2:
            feed = total_of(pending)
            self.pending = gather_ring(feed, self.two[0], self.two[0] == Z)
        elif step == 3:
            if self.direct:
                feed = total_of(pending)
            else:
                feed = rolled(jnp.stack(pending), (4 - self.two[1]) % 4).reshape(r, D)
            self.pending = gather_ring(feed, self.one[0], True)
        else:
            feed = rolled(jnp.stack(pending), (4 - self.one[1]) % 4).reshape(self.shape)
            self.pending = (feed, shift(feed, "c", 1))
        return feed

    def finish(self):
        while self.step < 5:
            self.advance(None)
        return self.pending


def local(
    inputs,
    picture_ids,
    cotangent,
    norm_gain,
    norm_bias,
    w_qkv,
    q_bias,
    v_bias,
    w_out,
    out_bias,
    w_up,
    up_bias,
    w_down,
    down_bias,
):
    layers = w_qkv.shape[0]
    zl, c, x, y = (lax.axis_index(name) for name in ("zl", "c", "x", "y"))
    z = lax.axis_index("zh") * 2 + zl
    where = (y, z)
    pos = jnp.stack([zl, x, jnp.where(zl == c, 0, 1)]).astype(jnp.int32)

    wq_t = jnp.swapaxes(w_qkv, 2, 3).reshape(layers, 3 * CW, D)
    half = 3 * CW // 2

    def far_projection(own):
        return shift(own[:half], Z, 1), shift(own[half:], Z, -1)

    wq = [(wq_t[0], far_projection(wq_t[0]))]
    up_bias = jnp.pad(up_bias, ((0, 0), (0, FP - FW)))
    qb_far, vb_far, ids_far = shift(q_bias, "zl", 1), shift(v_bias, "zl", 1), shift(picture_ids, "c", 1)
    biases = (q_bias, qb_far, v_bias, vb_far)
    normed, stream = call(
        first_kernel, [shaped((NT, D), bf16), shaped((CHUNK, D), f32)],
        inputs, norm_gain, norm_bias, pos=pos,
    )

    w_out, w_up, w_down, up_bias = after((w_out, w_up, w_down, up_bias), normed)
    ub_far = shift(up_bias, "zl", 1)
    pad = ((0, FP - FW), (0, 0))
    rest = [
        (w_out[layer], jnp.pad(w_up[layer].T, pad), jnp.pad(w_down[layer], pad))
        for layer in range(layers)
    ]
    far_out = [shift(rest[0][0], Z, 1)]
    far_mlp = []
    ids = arrange_ids(pos, picture_ids, ids_far)

    chunks = [normed]
    kept = []
    weights = []
    for layer in range(layers):
        q, kv, part, normed = project(layer, chunks, *wq[layer], biases)
        kvo = shift(kv, "c", 1)
        kvz = shift(part, "zl", 1)
        kvd = shift(kvz, "c", 1)
        wo = (rest[layer][0], far_out[layer])
        mixed_a, total_a = attend_row(q, (kv, kvo), ((0, NA), (0, NA)), ids[0], ids[1], wo)
        up_sent, down_sent = after(rest[layer][1:], kvz)
        far_mlp.append((shift(up_sent, Z, 1), shift(down_sent, Z, -1)))
        mixed_b, *sends = attend_quarter(
            q, (kv, kvo, kvz, kvd), ((NA, NB), (NA, NB), (0, NB), (0, NB)),
            ids[2], ids[3], wo, total_a,
        )
        got = scatter_x(sends)
        middle, low = norm_step(layer, (layer, 1), stream, got, out_bias, norm_gain, norm_bias)
        own = (wq[layer][0], *rest[layer])
        oth = (wq[layer][1], far_out[layer], *far_mlp[layer])
        weights.append((own, oth))
        normed_two, up, act, *sends = mlp(layer, gather_x(low), own, oth, up_bias, ub_far)
        got = scatter_x(sends)
        kept.append(
            (stream, normed, q, kv, kvo, kvz, kvd, mixed_a, mixed_b, middle, normed_two, up, act)
        )
        if layer < layers - 1:
            next_q, next_out = after((wq_t[layer + 1], rest[layer + 1][0]), sends[0])
            wq.append((wq_t[layer + 1], far_projection(next_q)))
            far_out.append(shift(next_out, Z, 1))
            stream, low = norm_step(
                layer, (layer + 1, 0), middle, got, down_bias, norm_gain, norm_bias
            )
            chunks = gather_x(low)

    low, grad_flow, d_down_bias = call(
        cotangent_kernel,
        [shaped((NT, D), bf16), shaped((CHUNK, D), f32), shaped((1, D), f32)],
        after(cotangent, normed_two), ids[0], ids[2], pos=pos,
    )
    result = call(
        functools.partial(result_kernel, layers - 1), [shaped((CHUNK, D), bf16)],
        middle, *got, down_bias,
    )[0]
    chunks = [low]
    zeros = jnp.zeros((1, D), f32)
    wide = [[None] * 6 for _ in range(layers)]
    narrow = [None] * layers
    sums = {}
    for layer in reversed(range(layers)):
        own, oth = weights[layer]
        (stream_in, normed, q, kv, kvo, kvz, kvd, mixed_a, mixed_b, middle, normed_two, up, act) = (
            kept[layer]
        )
        last = layer == layers - 1
        d_up, d_up_bias, sends, grad_low = mlp_back(chunks, up, own, oth)
        got = scatter_x(sends)
        kept_m, sent_m = call(
            mlp_weights_kernel, [shaped((2, FP, D), bf16)] * 2,
            d_up, act, normed_two, grad_low, pos=pos,
        )
        feeds = [sent_m]
        if last:
            far_m = shift(sent_m, "c", 1)
            out_far = shift(after(result, sends[0]), "zl", 1)
        else:
            feeds.append(sums["a1"].advance(sends[0]))
            sums["m0"] = WeightSum(kept_m, sent_m, where, True, False)
        got = after(got, feeds)
        grad_mid, mid_low, norm_two = norm_back((layer, 1), middle, got, grad_flow, norm_gain)
        mid_chunks = gather_x(mid_low)
        if last:
            both = total_of((kept_m, after(far_m, mid_low)))
            sum_m1 = lax.psum(both, ("y", "zh", "zl"))
            feeds = [both]
        else:
            feeds = [sums["m0"].advance(mid_low), sums["a1"].advance(mid_low)]
        mid_chunks = after(mid_chunks, feeds)
        mid, dq, d_own, d_far, d_z = attend_back(
            mid_chunks, q, kv, kvo, kvz, kvd, ids, (own[1], oth[1])
        )
        d_far = shift(d_far, "c", 1)
        d_z = shift((d_z + d_far[..., NT:].astype(f32)).astype(bf16), "zl", 1)
        if last:
            near, beside = after((result, out_far), mid)
            out_slots = gather_x(near) + gather_x(beside)
        stacked, d_qv_bias, *sends = project_back(dq, d_own, d_far, d_z, own[0], oth[0])
        got = scatter_x(sends)
        wide[layer][1], wide[layer][3], wide[layer][4] = (norm_two[i : i + 1] for i in range(3))
        wide[layer][5] = d_down_bias
        narrow[layer] = [
            jnp.concatenate(
                [
                    d_qv_bias[g].reshape(1, 2 * CW),
                    d_up_bias[g],
                    jnp.zeros((1, D - 2 * CW - FP), f32),
                ],
                axis=1,
            )
            for g in range(2)
        ]
        extra = [jnp.zeros((4, 0, D), f32)] * 3
        if not last:
            rows = [row for part in wide for row in part]
            rows = [zeros if row is None else row for row in rows]
            rows = jnp.concatenate(rows + [zeros] * (4 * EXTRA - len(rows)), axis=0)
            extra = [rows.reshape(4, EXTRA, D)]
            for g in range(2):
                rows = [part[g] for part in narrow]
                rows = [zeros] * (6 * layers) + rows
                rows = jnp.concatenate(rows + [zeros] * (4 * EXTRA - len(rows)), axis=0)
                extra.append(rows.reshape(4, EXTRA, D))
        if last:
            kept_a, sent_a = call(
                plain_weights_kernel, [shaped((4, CW, D), bf16)] * 2,
                stacked, mixed_a, mixed_b, normed, mid, pos=pos,
            )
            sums["a1"] = WeightSum(kept_a, sent_a, where, False, True)
            feeds = [sent_a]
        else:
            kept_a, sent_a = call(
                attend_weights_kernel, [shaped((4, CW + EXTRA, D), bf16)] * 2,
                stacked, mixed_a, mixed_b, normed, mid, *extra, pos=pos,
            )
            sums["a0"] = WeightSum(kept_a, sent_a, where, True, True)
            feeds = [sent_a, sums["m0"].advance(sends[0]), sums["a1"].advance(sends[0])]
        got = after(got, feeds)
        grad_flow, low, norm_one = norm_back((layer, 0), stream_in, got, grad_mid, norm_gain)
        if layer > 0:
            wide[layer][0], wide[layer][2] = norm_one[0:1], norm_one[1:2]
            chunks = gather_x(low)
            feeds = sums["a1"].advance(low)
            chunks = after(chunks, feeds)
        d_down_bias = norm_one[2:3]

    in_far = shift(low, "zl", 1)
    late = jnp.zeros((4 * EXTRA, D), f32)
    late = late.at[0].set(norm_one[0]).at[2].set(norm_one[1]).reshape(4, EXTRA, D)
    late = jnp.pad(late, ((0, 0), (CW, 0), (0, 0)))
    sums["a0"].advance(low, late)
    sums["m0"].advance(low)
    in_slots = gather_x(low) + gather_x(in_far)
    outputs = placed_rows(pos, out_slots, bf16)
    sum_m1 = (sum_m1, shift(after(sum_m1, low), "c", 1))
    sum_m0 = sums["m0"].finish()
    sum_a0 = sums["a0"].finish()
    sum_a1 = sums["a1"].finish()
    d_qkv, d_out, wide_sum, narrow_sum = attend_final(pos, (sum_a0, sum_a1))
    wide_sum = total_of((wide_sum, shift(wide_sum, "zl", 1)))
    wide_sum = sum(part.astype(f32) for part in gather_x(wide_sum)).reshape(4 * EXTRA, D)
    input_grad = placed_rows(pos, in_slots, f32)
    d_up, d_down = mlp_final(pos, (sum_m0, sum_m1))
    wide_sum = wide_sum[: 6 * layers].reshape(layers, 6, D)
    narrow_sum = narrow_sum.reshape(4 * EXTRA, D)[6 * layers : 7 * layers]
    return (
        outputs,
        input_grad,
        wide_sum[:, 0:2],
        wide_sum[:, 2:4],
        jnp.swapaxes(d_qkv, 2, 3),
        narrow_sum[:, :CW],
        narrow_sum[:, CW : 2 * CW],
        d_out,
        wide_sum[:, 4],
        jnp.transpose(d_up, (1, 2, 0)),
        narrow_sum[:, 2 * CW : 2 * CW + FW],
        jnp.transpose(d_down, (1, 0, 2)),
        wide_sum[:, 5],
    )


def solution(mesh):
    cut = Mesh(mesh.devices.reshape(4, 2, 2, 2, 4), ("y", "zh", "c", "zl", "x"))
    dp, tensor = ("y", "zh"), ("zl", "x")
    weight_specs = (
        P(),
        P(),
        P(None, None, None, tensor),
        P(None, tensor),
        P(None, tensor),
        P(None, tensor, None),
        P(),
        P(None, None, tensor),
        P(None, tensor),
        P(None, tensor, None),
        P(),
    )
    return jax.shard_map(
        local,
        mesh=cut,
        in_specs=(P(dp, "c", None), P(dp, "c"), P(dp, "c", None), *weight_specs),
        out_specs=(P(dp, "c", None), P(dp, "c", None), *weight_specs),
        check_vma=False,
    )
```

time: 1490 us -> 762 us (0.51)
  the two profiles are of different devices: /device:TPU:9 before, /device:TPU:38 now
where the time goes in v1:
time: 762 us; the launch traced here: 752 us
  waiting for transfers between devices  334 us (44%)
  starting transfers between devices  209 us (27%)
  Pallas kernels  112 us (15%)
  local copies, waits for them, and re-layouts  62.1 us (8%)
  other arithmetic  18.2 us (2%)
  between operations  16.3 us (2%)
    ppermute x110, waiting for transfers between devices, shift(): return lax.ppermute(value, axis, [(i, (i + by) % n) for i in range(n)])  251 us
    ppermute x110, starting transfers between devices, shift(): return lax.ppermute(value, axis, [(i, (i + by) % n) for i in range(n)])  178 us
    pallas_call x33, Pallas kernels, call(): pl.pallas_call(kernel, out_shape=outs, in_specs=specs, out_specs=[pl.Bloc...  112 us
    psum x1, waiting for transfers between devices, local(): sum_m1 = lax.psum(both, ('y', 'zh', 'zl'))  81.2 us
    unnamed x283, local copies, waits for them, and re-layouts  39.8 us
    ppermute x6, starting transfers between devices, gather_ring(): got.append(lax.ppermute(piece, ('zh', 'c', 'zl'), pairs))  26.1 us
  transfers between devices with their start and end apart: 123, of which 53 were waited for; matrix products, arithmetic and copies ran while one was open for 7% of the time, Pallas kernels for 7%

profile of v1, /device:TPU:38, one launch (start us, length us, event | category | flops | bytes accessed | tf_op | source)
XLA Modules:
  0.0 752.3 jit_solution(8710032294321946564)
XLA Ops:
  39.1 29.6 %collective-permute-done.8.refs_6_.refs_8_.wo1 = bf16[144,1152]{1,0:T(8,128)(2,1)S(1)} collective-permute-done((bf16[144,1152]{1,0:T(8,128)(2,1)S(1)}, bf16[144,1152]{1,0:T(8,128)(2,1)S(1)}, u32[]{:S(2)}, u32[]{:S(2)}) %collective-permute-start.8) | collective-permute-done | bytes 331808 | tf_op jit(solution)/shard_map/ppermute | solution.py:34
  71.6 3.2 shard_map.241
  78.4 3.4 collective-permute-done.9.r1
  81.8 3.6 collective-permute-start.16
  92.6 3.8 collective-permute-done.12.c1
  98.3 5.7 shard_map.243
  111.1 4.4 collective-permute-done.18.r1
  118.5 4.2 collective-permute-done.20.r3
  127.7 5.0 collective-permute-done.21.refs_1_
  133.6 3.3 shard_map.245
  136.9 3.9 collective-permute-start.27
  141.1 4.5 collective-permute-done.27.refs_3_.kvz
  148.8 24.4 %collective-permute-done.29.refs_6_.refs_8_.wo1 = bf16[144,1152]{1,0:T(8,128)(2,1)S(1)} collective-permute-done((bf16[144,1152]{1,0:T(8,128)(2,1)S(1)}, bf16[144,1152]{1,0:T(8,128)(2,1)S(1)}, u32[]{:S(2)}, u32[]{:S(2)}) %collective-permute-start.29) | collective-permute-done | bytes 331808 | tf_op jit(solution)/shard_map/ppermute | solution.py:34
  182.1 5.7 collective-permute-done.30.r1
  192.2 3.6 collective-permute-start.34
  198.3 3.8 collective-permute-done.34.c2
  202.2 5.7 shard_map.249
  208.8 6.8 shard_map.252
  215.6 5.8 shard_map.253
  224.5 9.2 %collective-permute-done.42.r1 = bf16[96,1152]{1,0:T(8,128)(2,1)S(1)} collective-permute-done((bf16[96,1152]{1,0:T(8,128)(2,1)S(1)}, bf16[96,1152]{1,0:T(8,128)(2,1)S(1)}, u32[]{:S(2)}, u32[]{:S(2)}) %collective-permute-start.42) | collective-permute-done | bytes 221216 | tf_op jit(solution)/shard_map/ppermute | solution.py:34
  233.7 3.4 collective-permute-done.44.r3
  242.5 4.0 add_convert_fusion.1
  246.5 6.0 collective-permute-done.45.c1
  255.9 8.7 %shard_map.255 = (bf16[384,1152]{1,0:T(8,128)(2,1)}, bf16[2,144,384]{2,1,0:T(8,128)(2,1)S(1)}, f32[2,2,144,384]{3,2,1,0:T(8,128)}, bf16[2,2,144,512]{3,2,1,0:T(8,128)(2,1)}, f32[2,2,144,128]{3,2,1,0:T(8,128)S(1)}) custom-call(bf16[96,1152]{1,0:T(8,128)(2,1)} %get-tuple-element.283.c0, bf16[96,1152]{1,0:T(8,128)(2,1)} %collective-permute-done.45.c1, ...), custom_call_target="tpu_custom_call" | custom-call | tf_op jit(solution)/shard_map/pallas_call | solution.py:66
  269.6 4.1 collective-permute-done.56.dz
  273.8 4.2 shard_map.257
  278.0 3.6 shard_map.258
  285.0 9.5 %collective-permute-done.57.r1 = bf16[96,1152]{1,0:T(8,128)(2,1)S(1)} collective-permute-done((bf16[96,1152]{1,0:T(8,128)(2,1)}, bf16[96,1152]{1,0:T(8,128)(2,1)S(1)}, u32[]{:S(2)}, u32[]{:S(2)}) %collective-permute-start.57) | collective-permute-done | bytes 221216 | tf_op jit(solution)/shard_map/ppermute | solution.py:34
  308.4 7.6 %collective-permute-done.60.refs_1_ = bf16[96,1152]{1,0:T(8,128)(2,1)S(1)} collective-permute-done((bf16[96,1152]{1,0:T(8,128)(2,1)S(1)}, bf16[96,1152]{1,0:T(8,128)(2,1)S(1)}, u32[]{:S(2)}, u32[]{:S(2)}) %collective-permute-start.60) | collective-permute-done | bytes 221216 | tf_op jit(solution)/shard_map/ppermute | solution.py:34
  316.6 7.6 %shard_map.260 = (bf16[2,384,576]{2,1,0:T(8,128)(2,1)S(1)}, f32[2,1,576]{2,1,0:T(1,128)S(1)}, bf16[96,1152]{1,0:T(8,128)(2,1)S(1)}, bf16[96,1152]{1,0:T(8,128)(2...) custom-call(bf16[96,1152]{1,0:T(8,128)(2,1)S(1)} %get-tuple-element.312.refs_0_, ...), custom_call_target="tpu_custom_call" | custom-call | tf_op jit(solution)/shard_map/pallas_call | solution.py:66
  324.2 5.7 shard_map.261
  330.0 3.8 collective-permute-start.68
  336.4 4.1 collective-permute-done.67
  342.4 6.7 collective-permute-done.69
  357.9 6.7 collective-permute-done.66.r3
  370.5 4.0 collective-permute-start.71
  383.8 3.4 collective-permute-done.71.c2
  387.2 7.4 shard_map.263
  403.4 4.9 collective-permute-start.78
  414.2 4.0 shard_map.264
  419.0 13.7 %collective-permute-start.87 = (bf16[144,1152]{1,0:T(8,128)(2,1)}, bf16[144,1152]{1,0:T(8,128)(2,1)S(1)}, u32[]{:S(2)}, u32[]{:S(2)}) collective-permute-start(bf16[144,1152]{1,0:T(8,128)(2,1)} %add_convert_fusion.6), channel_id=1, source_target_pairs={{20,0},{8,12},{4,16},{24,28},{21,1},{9,13},{5,17},{25,29},{22,2},{... | collective-permute-start | bytes 995336 | tf_op jit(solution)/shard_map/ppermute | solution.py:570
  449.6 3.3 collective-permute-start.112
  454.3 3.8 shard_map.265
  465.4 3.7 collective-permute-start.114
  474.1 4.0 collective-permute-start.116
  487.1 81.2 %all-reduce.9.cloned.1.call-done.full1 = bf16[2,576,1152]{2,1,0:T(8,128)(2,1)} async-done(((bf16[2,576,1152]{2,1,0:T(8,128)(2,1)}), bf16[2,576,1152]{2,1,0:T(8,128)(2,1)}) %all-reduce.9.cloned.1.call-update) | async-done | bytes 2654224 | tf_op jit(solution)/shard_map/psum | solution.py:745
  577.5 5.4 collective-permute-done.98
  582.9 4.6 collective-permute-done.97
  587.5 4.5 collective-permute-done.96
  592.1 21.4 %collective-permute-start.101 = (bf16[152,1152]{1,0:T(8,128)(2,1)S(1)}, bf16[152,1152]{1,0:T(8,128)(2,1)S(1)}, u32[]{:S(2)}, u32[]{:S(2)}) collective-permute-start(bf16[152,1152]{1,0:T(8,128)(2,1)S(1)} %fusion.2), channel_id=1, source_target_pairs={{0,20},{4,0},{16,4},{20,16},{1,21},{5,1},{17,5},{21,17},{2,22},{6,... | collective-permute-start | bytes 1050632 | tf_op jit(solution)/shard_map/ppermute | solution.py:34
  615.1 7.7 %collective-permute-done.101 = bf16[152,1152]{1,0:T(8,128)(2,1)S(1)} collective-permute-done((bf16[152,1152]{1,0:T(8,128)(2,1)S(1)}, bf16[152,1152]{1,0:T(8,128)(2,1)S(1)}, u32[]{:S(2)}, u32[]{:S(2)}) %collective-permute-start.101) | collective-permute-done | bytes 350240 | tf_op jit(solution)/shard_map/ppermute | solution.py:34
  623.4 3.2 collective-permute-done.100
  631.1 23.6 %collective-permute-start.120 = (bf16[2,576,1152]{2,1,0:T(8,128)(2,1)S(1)}, bf16[2,576,1152]{2,1,0:T(8,128)(2,1)}, u32[]{:S(2)}, u32[]{:S(2)}) collective-permute-start(bf16[2,576,1152]{2,1,0:T(8,128)(2,1)S(1)} %bitcast.136), channel_id=1, source_target_pairs={{0,8},{8,0},{1,9},{9,1},{2,10},{10,2},{3,11},{11,3},{4,12},{12,4},... | collective-permute-start | bytes 7962632 | tf_op jit(solution)/shard_map/ppermute | solution.py:34
  657.2 11.1 %collective-permute-done.52.refs_5_ = bf16[96,1152]{1,0:T(8,128)(2,1)S(1)} collective-permute-done((bf16[96,1152]{1,0:T(8,128)(2,1)S(1)}, bf16[96,1152]{1,0:T(8,128)(2,1)S(1)}, u32[]{:S(2)}, u32[]{:S(2)}) %collective-permute-start.52) | collective-permute-done | bytes 221216 | tf_op jit(solution)/shard_map/ppermute | solution.py:34
  668.3 7.8 %collective-permute-done.54.refs_7_ = bf16[96,1152]{1,0:T(8,128)(2,1)S(1)} collective-permute-done((bf16[96,1152]{1,0:T(8,128)(2,1)S(1)}, bf16[96,1152]{1,0:T(8,128)(2,1)S(1)}, u32[]{:S(2)}, u32[]{:S(2)}) %collective-permute-start.54) | collective-permute-done | bytes 221216 | tf_op jit(solution)/shard_map/ppermute | solution.py:34
  676.1 8.3 %collective-permute-done.88.refs_1_ = bf16[96,1152]{1,0:T(8,128)(2,1)S(1)} collective-permute-done((bf16[96,1152]{1,0:T(8,128)(2,1)S(1)}, bf16[96,1152]{1,0:T(8,128)(2,1)S(1)}, u32[]{:S(2)}, u32[]{:S(2)}) %collective-permute-start.88) | collective-permute-done | bytes 221216 | tf_op jit(solution)/shard_map/ppermute | solution.py:34
  684.4 7.7 %collective-permute-done.89.refs_2_ = bf16[96,1152]{1,0:T(8,128)(2,1)S(1)} collective-permute-done((bf16[96,1152]{1,0:T(8,128)(2,1)S(1)}, bf16[96,1152]{1,0:T(8,128)(2,1)S(1)}, u32[]{:S(2)}, u32[]{:S(2)}) %collective-permute-start.89) | collective-permute-done | bytes 221216 | tf_op jit(solution)/shard_map/ppermute | solution.py:34
  692.8 5.2 collective-permute-done.90.refs_3_
  698.0 7.3 collective-permute-start.91
  705.3 3.9 collective-permute-done.91.refs_4_
  709.2 3.4 collective-permute-start.93
  713.7 4.6 shard_map.268
  724.8 9.2 %shard_map.269 = (f32[538,2,1152]{2,1,0:T(2,128)}, f32[538,2,1152]{2,1,0:T(2,128)}) custom-call(s32[3]{0:T(128)S(1)} %pad_add_fusion.pos, bf16[2,576,1152]{2,1,0:T(8,128)(2,1)S(1)} %bitcast.137, bf16[2,576,1152]{2,1,0:T(8,128)(2,1)} %collective-permute-done.120.other0, bf16[2,576,1152]{2,1,0:T(8,128)(2,1)} %all-reduce.9.cloned.1.call-done.full1, ...), custom_call_target="tpu_custom_call" | custom-call | tf_op jit(solution)/shard_map/pallas_call | solution.py:66
  734.8 3.4 collective-permute-start.109
  (574 shorter events, 235.1 us)
Async XLA Ops:
  7.2 561.2 %all-reduce.9.cloned.1.call-start = ((), (), s32[]{:S(2)}) async-start(), calls=%async_computation | async-start | bytes 5308416 | tf_op jit(solution)/shard_map/psum | solution.py:745
  11.0 13.4 %collective-permute-start = (bf16[216,1152]{1,0:T(8,128)(2,1)}, bf16[216,1152]{1,0:T(8,128)(2,1)S(1)}, u32[]{:S(2)}, u32[]{:S(2)}) collective-permute-start(bf16[216,1152]{1,0:T(8,128)(2,1)} %get-tuple-element.438), channel_id=1, source_target_pairs={{0,4},{4,16},{16,20},{20,0},{1,5},{5,17},{17,21},{21,1},{2,6},{6,1... | collective-permute-start | bytes 1493000 | tf_op jit(solution)/shard_map/ppermute | solution.py:34
  12.9 13.0 %collective-permute-start.1 = (bf16[216,1152]{1,0:T(8,128)(2,1)}, bf16[216,1152]{1,0:T(8,128)(2,1)S(1)}, u32[]{:S(2)}, u32[]{:S(2)}) collective-permute-start(bf16[216,1152]{1,0:T(8,128)(2,1)} %get-tuple-element.437), channel_id=1, source_target_pairs={{0,20},{4,0},{16,4},{20,16},{1,21},{5,1},{17,5},{21,17},{2,22},{6,... | collective-permute-start | bytes 1493000 | tf_op jit(solution)/shard_map/ppermute | solution.py:34
  33.0 64.3 %collective-permute-start.15 = (bf16[576,1152]{1,0:T(8,128)(2,1)S(1)}, bf16[576,1152]{1,0:T(8,128)(2,1)S(1)}, u32[]{:S(2)}, u32[]{:S(2)}) collective-permute-start(bf16[576,1152]{1,0:T(8,128)(2,1)S(1)} %pad.27.wu0.refs_5_), channel_id=1, source_target_pairs={{0,4},{4,16},{16,20},{20,0},{1,5},{5,17},{17,21},{21,1},{2,6},{6,1... | collective-permute-start | bytes 3981320 | tf_op jit(solution)/shard_map/ppermute | solution.py:34
  34.7 62.5 %collective-permute-start.17 = (bf16[576,1152]{1,0:T(8,128)(2,1)S(1)}, bf16[576,1152]{1,0:T(8,128)(2,1)}, u32[]{:S(2)}, u32[]{:S(2)}) collective-permute-start(bf16[576,1152]{1,0:T(8,128)(2,1)S(1)} %pad.28.wd0.refs_7_), channel_id=1, source_target_pairs={{0,20},{4,0},{16,4},{20,16},{1,21},{5,1},{17,5},{21,17},{2,22},{6,... | collective-permute-start | bytes 3981320 | tf_op jit(solution)/shard_map/ppermute | solution.py:34
  35.0 33.6 %collective-permute-start.4 = (bf16[2,2,144,384]{3,2,1,0:T(8,128)(2,1)S(1)}, bf16[2,2,144,384]{3,2,1,0:T(8,128)(2,1)S(1)}, u32[]{:S(2)}, u32[]{:S(2)}) collective-permute-start(bf16[2,2,144,384]{3,2,1,0:T(8,128)(2,1)S(1)} %get-tuple-element.220.refs_1_.kv), channel_id=1, source_target_pairs={{0,8},{8,0},{1,9},{9,1},{2,10},{10,2},{3,11},{11,3},{4,12},{12,4},... | collective-permute-start | bytes 1327112 | tf_op jit(solution)/shard_map/ppermute | solution.py:34
  35.1 33.5 %collective-permute-start.8 = (bf16[144,1152]{1,0:T(8,128)(2,1)S(1)}, bf16[144,1152]{1,0:T(8,128)(2,1)S(1)}, u32[]{:S(2)}, u32[]{:S(2)}) collective-permute-start(bf16[144,1152]{1,0:T(8,128)(2,1)S(1)} %get-tuple-element.444.refs_5_.refs_7_.wo0), channel_id=1, source_target_pairs={{0,4},{4,16},{16,20},{20,0},{1,5},{5,17},{17,21},{21,1},{2,6},{6,1... | collective-permute-start | bytes 995336 | tf_op jit(solution)/shard_map/ppermute | solution.py:34
  38.1 33.6 %collective-permute-start.6 = (bf16[2,2,144,128]{3,2,1,0:T(8,128)(2,1)S(1)}, bf16[2,2,144,128]{3,2,1,0:T(8,128)(2,1)S(1)}, u32[]{:S(2)}, u32[]{:S(2)}) collective-permute-start(bf16[2,2,144,128]{3,2,1,0:T(8,128)(2,1)S(1)} %collective-permute-done.5.refs_3_.kvz), channel_id=1, source_target_pairs={{0,8},{8,0},{1,9},{9,1},{2,10},{10,2},{3,11},{11,3},{4,12},{12,4},... | collective-permute-start | bytes 442376 | tf_op jit(solution)/shard_map/ppermute | solution.py:34
  104.2 29.4 %collective-permute-start.24 = (bf16[216,1152]{1,0:T(8,128)(2,1)S(1)}, bf16[216,1152]{1,0:T(8,128)(2,1)S(1)}, u32[]{:S(2)}, u32[]{:S(2)}) collective-permute-start(bf16[216,1152]{1,0:T(8,128)(2,1)S(1)} %get-tuple-element.436), channel_id=1, source_target_pairs={{0,4},{4,16},{16,20},{20,0},{1,5},{5,17},{17,21},{21,1},{2,6},{6,1... | collective-permute-start | bytes 1493000 | tf_op jit(solution)/shard_map/ppermute | solution.py:34
  105.8 27.8 %collective-permute-start.25 = (bf16[216,1152]{1,0:T(8,128)(2,1)S(1)}, bf16[216,1152]{1,0:T(8,128)(2,1)S(1)}, u32[]{:S(2)}, u32[]{:S(2)}) collective-permute-start(bf16[216,1152]{1,0:T(8,128)(2,1)S(1)} %get-tuple-element.435), channel_id=1, source_target_pairs={{0,20},{4,0},{16,4},{20,16},{1,21},{5,1},{17,5},{21,17},{2,22},{6,... | collective-permute-start | bytes 1493000 | tf_op jit(solution)/shard_map/ppermute | solution.py:34
  145.6 56.6 %collective-permute-start.36 = (bf16[576,1152]{1,0:T(8,128)(2,1)S(1)}, bf16[576,1152]{1,0:T(8,128)(2,1)}, u32[]{:S(2)}, u32[]{:S(2)}) collective-permute-start(bf16[576,1152]{1,0:T(8,128)(2,1)S(1)} %pad.29.wu0.refs_2_), channel_id=1, source_target_pairs={{0,4},{4,16},{16,20},{20,0},{1,5},{5,17},{17,21},{21,1},{2,6},{6,1... | collective-permute-start | bytes 3981320 | tf_op jit(solution)/shard_map/ppermute | solution.py:34
  146.5 55.6 %collective-permute-start.37 = (bf16[576,1152]{1,0:T(8,128)(2,1)S(1)}, bf16[576,1152]{1,0:T(8,128)(2,1)}, u32[]{:S(2)}, u32[]{:S(2)}) collective-permute-start(bf16[576,1152]{1,0:T(8,128)(2,1)S(1)} %pad.30.wd0.refs_4_), channel_id=1, source_target_pairs={{0,20},{4,0},{16,4},{20,16},{1,21},{5,1},{17,5},{21,17},{2,22},{6,... | collective-permute-start | bytes 3981320 | tf_op jit(solution)/shard_map/ppermute | solution.py:34
  147.6 25.6 %collective-permute-start.26 = (bf16[2,2,144,384]{3,2,1,0:T(8,128)(2,1)S(1)}, bf16[2,2,144,384]{3,2,1,0:T(8,128)(2,1)S(1)}, u32[]{:S(2)}, u32[]{:S(2)}) collective-permute-start(bf16[2,2,144,384]{3,2,1,0:T(8,128)(2,1)S(1)} %get-tuple-element.247.refs_1_.kv), channel_id=1, source_target_pairs={{0,8},{8,0},{1,9},{9,1},{2,10},{10,2},{3,11},{11,3},{4,12},{12,4},... | collective-permute-start | bytes 1327112 | tf_op jit(solution)/shard_map/ppermute | solution.py:34
  147.6 25.6 %collective-permute-start.29 = (bf16[144,1152]{1,0:T(8,128)(2,1)S(1)}, bf16[144,1152]{1,0:T(8,128)(2,1)S(1)}, u32[]{:S(2)}, u32[]{:S(2)}) collective-permute-start(bf16[144,1152]{1,0:T(8,128)(2,1)S(1)} %get-tuple-element.249.refs_5_.refs_7_.wo0), channel_id=1, source_target_pairs={{0,4},{4,16},{16,20},{20,0},{1,5},{5,17},{17,21},{21,1},{2,6},{6,1... | collective-permute-start | bytes 995336 | tf_op jit(solution)/shard_map/ppermute | solution.py:34
  148.5 27.7 %collective-permute-start.28 = (bf16[2,2,144,128]{3,2,1,0:T(8,128)(2,1)S(1)}, bf16[2,2,144,128]{3,2,1,0:T(8,128)(2,1)S(1)}, u32[]{:S(2)}, u32[]{:S(2)}) collective-permute-start(bf16[2,2,144,128]{3,2,1,0:T(8,128)(2,1)S(1)} %collective-permute-done.27.refs_3_.kvz), channel_id=1, source_target_pairs={{0,8},{8,0},{1,9},{9,1},{2,10},{10,2},{3,11},{11,3},{4,12},{12,4},... | collective-permute-start | bytes 442376 | tf_op jit(solution)/shard_map/ppermute | solution.py:34
  221.4 21.1 %collective-permute-start.48 = (bf16[2,576,1152]{2,1,0:T(8,128)(2,1)}, bf16[2,576,1152]{2,1,0:T(8,128)(2,1)S(1)}, u32[]{:S(2)}, u32[]{:S(2)}) collective-permute-start(bf16[2,576,1152]{2,1,0:T(8,128)(2,1)} %get-tuple-element.274), channel_id=1, source_target_pairs={{0,8},{8,0},{1,9},{9,1},{2,10},{10,2},{3,11},{11,3},{4,12},{12,4},... | collective-permute-start | bytes 7962632 | tf_op jit(solution)/shard_map/ppermute | solution.py:34
  223.6 13.5 %collective-permute-start.44 = (bf16[96,1152]{1,0:T(8,128)(2,1)S(1)}, bf16[96,1152]{1,0:T(8,128)(2,1)S(1)}, u32[]{:S(2)}, u32[]{:S(2)}) collective-permute-start(bf16[96,1152]{1,0:T(8,128)(2,1)S(1)} %get-tuple-element.271), channel_id=1, source_target_pairs={{0,3},{1,0},{2,1},{3,2},{4,7},{5,4},{6,5},{7,6},{8,11},{9,8},{10,9... | collective-permute-start | bytes 663560 | tf_op jit(solution)/shard_map/ppermute | solution.py:34
  239.1 13.4 %collective-permute-start.45 = (bf16[96,1152]{1,0:T(8,128)(2,1)}, bf16[96,1152]{1,0:T(8,128)(2,1)}, u32[]{:S(2)}, u32[]{:S(2)}) collective-permute-start(bf16[96,1152]{1,0:T(8,128)(2,1)} %get-tuple-element.283.c0), channel_id=1, source_target_pairs={{0,3},{1,0},{2,1},{3,2},{4,7},{5,4},{6,5},{7,6},{8,11},{9,8},{10,9... | collective-permute-start | bytes 663560 | tf_op jit(solution)/shard_map/ppermute | solution.py:34
  239.1 13.4 %collective-permute-start.46 = (bf16[96,1152]{1,0:T(8,128)(2,1)}, bf16[96,1152]{1,0:T(8,128)(2,1)}, u32[]{:S(2)}, u32[]{:S(2)}) collective-permute-start(bf16[96,1152]{1,0:T(8,128)(2,1)} %get-tuple-element.283.c0), channel_id=1, source_target_pairs={{0,2},{1,3},{2,0},{3,1},{4,6},{5,7},{6,4},{7,5},{8,10},{9,11},{10,... | collective-permute-start | bytes 663560 | tf_op jit(solution)/shard_map/ppermute | solution.py:34
  281.5 25.0 %collective-permute-start.63 = (bf16[4,144,1152]{2,1,0:T(8,128)(2,1)}, bf16[4,144,1152]{2,1,0:T(8,128)(2,1)}, u32[]{:S(2)}, u32[]{:S(2)}) collective-permute-start(bf16[4,144,1152]{2,1,0:T(8,128)(2,1)} %get-tuple-element.302), channel_id=1, source_target_pairs={{0,8},{8,0},{1,9},{9,1},{2,10},{10,2},{3,11},{11,3},{4,12},{12,4},... | collective-permute-start | bytes 3981320 | tf_op jit(solution)/shard_map/ppermute | solution.py:34
  281.5 13.0 %collective-permute-start.57 = (bf16[96,1152]{1,0:T(8,128)(2,1)}, bf16[96,1152]{1,0:T(8,128)(2,1)S(1)}, u32[]{:S(2)}, u32[]{:S(2)}) collective-permute-start(bf16[96,1152]{1,0:T(8,128)(2,1)} %get-tuple-element.295), channel_id=1, source_target_pairs={{0,1},{1,2},{2,3},{3,0},{4,5},{5,6},{6,7},{7,4},{8,9},{9,10},{10,1... | collective-permute-start | bytes 663560 | tf_op jit(solution)/shard_map/ppermute | solution.py:34
  284.1 13.7 %collective-permute-start.59 = (bf16[96,1152]{1,0:T(8,128)(2,1)}, bf16[96,1152]{1,0:T(8,128)(2,1)S(1)}, u32[]{:S(2)}, u32[]{:S(2)}) collective-permute-start(bf16[96,1152]{1,0:T(8,128)(2,1)} %get-tuple-element.297), channel_id=1, source_target_pairs={{0,3},{1,0},{2,1},{3,2},{4,7},{5,4},{6,5},{7,6},{8,11},{9,8},{10,9... | collective-permute-start | bytes 663560 | tf_op jit(solution)/shard_map/ppermute | solution.py:34
  302.9 13.1 %collective-permute-start.60 = (bf16[96,1152]{1,0:T(8,128)(2,1)S(1)}, bf16[96,1152]{1,0:T(8,128)(2,1)S(1)}, u32[]{:S(2)}, u32[]{:S(2)}) collective-permute-start(bf16[96,1152]{1,0:T(8,128)(2,1)S(1)} %get-tuple-element.312.refs_0_), channel_id=1, source_target_pairs={{0,3},{1,0},{2,1},{3,2},{4,7},{5,4},{6,5},{7,6},{8,11},{9,8},{10,9... | collective-permute-start | bytes 663560 | tf_op jit(solution)/shard_map/ppermute | solution.py:34
  303.0 13.0 %collective-permute-start.61 = (bf16[96,1152]{1,0:T(8,128)(2,1)S(1)}, bf16[96,1152]{1,0:T(8,128)(2,1)S(1)}, u32[]{:S(2)}, u32[]{:S(2)}) collective-permute-start(bf16[96,1152]{1,0:T(8,128)(2,1)S(1)} %get-tuple-element.312.refs_0_), channel_id=1, source_target_pairs={{0,2},{1,3},{2,0},{3,1},{4,6},{5,7},{6,4},{7,5},{8,10},{9,11},{10,... | collective-permute-start | bytes 663560 | tf_op jit(solution)/shard_map/ppermute | solution.py:34
  330.0 46.7 %collective-permute-start.73 = (bf16[2,576,1152]{2,1,0:T(8,128)(2,1)}, bf16[2,576,1152]{2,1,0:T(8,128)(2,1)}, u32[]{:S(2)}, u32[]{:S(2)}) collective-permute-start(bf16[2,576,1152]{2,1,0:T(8,128)(2,1)} %get-tuple-element.325), channel_id=1, source_target_pairs={{0,8},{8,0},{1,9},{9,1},{2,10},{10,2},{3,11},{11,3},{4,12},{12,4},... | collective-permute-start | bytes 7962632 | tf_op jit(solution)/shard_map/ppermute | solution.py:34
  333.8 15.3 %collective-permute-start.69 = (bf16[144,1152]{1,0:T(8,128)(2,1)S(1)}, bf16[144,1152]{1,0:T(8,128)(2,1)S(1)}, u32[]{:S(2)}, u32[]{:S(2)}) collective-permute-start(bf16[144,1152]{1,0:T(8,128)(2,1)S(1)} %get-tuple-element.431), channel_id=1, source_target_pairs={{0,20},{4,0},{16,4},{20,16},{1,21},{5,1},{17,5},{21,17},{2,22},{6,... | collective-permute-start | bytes 995336 | tf_op jit(solution)/shard_map/ppermute | solution.py:34
  333.8 20.7 %collective-permute-start.64 = (bf16[96,1152]{1,0:T(8,128)(2,1)S(1)}, bf16[96,1152]{1,0:T(8,128)(2,1)S(1)}, u32[]{:S(2)}, u32[]{:S(2)}) collective-permute-start(bf16[96,1152]{1,0:T(8,128)(2,1)S(1)} %get-tuple-element.318), channel_id=1, source_target_pairs={{0,1},{1,2},{2,3},{3,0},{4,5},{5,6},{6,7},{7,4},{8,9},{9,10},{10,1... | collective-permute-start | bytes 663560 | tf_op jit(solution)/shard_map/ppermute | solution.py:34
  340.6 15.3 %collective-permute-start.65 = (bf16[96,1152]{1,0:T(8,128)(2,1)S(1)}, bf16[96,1152]{1,0:T(8,128)(2,1)S(1)}, u32[]{:S(2)}, u32[]{:S(2)}) collective-permute-start(bf16[96,1152]{1,0:T(8,128)(2,1)S(1)} %get-tuple-element.319), channel_id=1, source_target_pairs={{0,2},{1,3},{2,0},{3,1},{4,6},{5,7},{6,4},{7,5},{8,10},{9,11},{10,... | collective-permute-start | bytes 663560 | tf_op jit(solution)/shard_map/ppermute | solution.py:34
  350.0 19.6 %collective-permute-start.74 = (bf16[144,1152]{1,0:T(8,128)(2,1)}, bf16[144,1152]{1,0:T(8,128)(2,1)}, u32[]{:S(2)}, u32[]{:S(2)}) collective-permute-start(bf16[144,1152]{1,0:T(8,128)(2,1)} %add_convert_fusion.7), channel_id=1, source_target_pairs={{0,32},{32,64},{64,96},{96,0},{1,33},{33,65},{65,97},{97,1},{2,34}... | collective-permute-start | bytes 995336 | tf_op jit(solution)/shard_map/ppermute | solution.py:34
  351.6 18.1 %collective-permute-start.75 = (bf16[144,1152]{1,0:T(8,128)(2,1)}, bf16[144,1152]{1,0:T(8,128)(2,1)}, u32[]{:S(2)}, u32[]{:S(2)}) collective-permute-start(bf16[144,1152]{1,0:T(8,128)(2,1)} %add_convert_fusion.7), channel_id=1, source_target_pairs={{0,64},{32,96},{64,0},{96,32},{1,65},{33,97},{65,1},{97,33},{2,66}... | collective-permute-start | bytes 995336 | tf_op jit(solution)/shard_map/ppermute | solution.py:34
  354.5 16.0 %collective-permute-start.76 = (bf16[144,1152]{1,0:T(8,128)(2,1)}, bf16[144,1152]{1,0:T(8,128)(2,1)}, u32[]{:S(2)}, u32[]{:S(2)}) collective-permute-start(bf16[144,1152]{1,0:T(8,128)(2,1)} %add_convert_fusion.7), channel_id=1, source_target_pairs={{0,96},{32,0},{64,32},{96,64},{1,97},{33,1},{65,33},{97,65},{2,98}... | collective-permute-start | bytes 995336 | tf_op jit(solution)/shard_map/ppermute | solution.py:34
  364.6 30.9 %collective-permute-start.38 = (bf16[96,1152]{1,0:T(8,128)(2,1)}, bf16[96,1152]{1,0:T(8,128)(2,1)S(1)}, u32[]{:S(2)}, u32[]{:S(2)}) collective-permute-start(bf16[96,1152]{1,0:T(8,128)(2,1)} %copy-done.99), channel_id=1, source_target_pairs={{0,1},{1,2},{2,3},{3,0},{4,5},{5,6},{6,7},{7,4},{8,9},{9,10},{10,1... | collective-permute-start | bytes 663560 | tf_op jit(solution)/shard_map/ppermute | solution.py:34
  369.6 25.9 %collective-permute-start.39 = (bf16[96,1152]{1,0:T(8,128)(2,1)}, bf16[96,1152]{1,0:T(8,128)(2,1)S(1)}, u32[]{:S(2)}, u32[]{:S(2)}) collective-permute-start(bf16[96,1152]{1,0:T(8,128)(2,1)} %copy-done.98), channel_id=1, source_target_pairs={{0,2},{1,3},{2,0},{3,1},{4,6},{5,7},{6,4},{7,5},{8,10},{9,11},{10,... | collective-permute-start | bytes 663560 | tf_op jit(solution)/shard_map/ppermute | solution.py:34
  369.7 14.1 %collective-permute-start.70 = (bf16[96,1152]{1,0:T(8,128)(2,1)S(1)}, bf16[96,1152]{1,0:T(8,128)(2,1)S(1)}, u32[]{:S(2)}, u32[]{:S(2)}) collective-permute-start(bf16[96,1152]{1,0:T(8,128)(2,1)S(1)} %get-tuple-element.343.c0), channel_id=1, source_target_pairs={{0,3},{1,0},{2,1},{3,2},{4,7},{5,4},{6,5},{7,6},{8,11},{9,8},{10,9... | collective-permute-start | bytes 663560 | tf_op jit(solution)/shard_map/ppermute | solution.py:34
  370.5 16.7 %collective-permute-start.71 = (bf16[96,1152]{1,0:T(8,128)(2,1)S(1)}, bf16[96,1152]{1,0:T(8,128)(2,1)S(1)}, u32[]{:S(2)}, u32[]{:S(2)}) collective-permute-start(bf16[96,1152]{1,0:T(8,128)(2,1)S(1)} %get-tuple-element.343.c0), channel_id=1, source_target_pairs={{0,2},{1,3},{2,0},{3,1},{4,6},{5,7},{6,4},{7,5},{8,10},{9,11},{10,... | collective-permute-start | bytes 663560 | tf_op jit(solution)/shard_map/ppermute | solution.py:34
  397.6 21.5 %collective-permute-start.82 = (bf16[288,1152]{1,0:T(8,128)(2,1)}, bf16[288,1152]{1,0:T(8,128)(2,1)}, u32[]{:S(2)}, u32[]{:S(2)}) collective-permute-start(bf16[288,1152]{1,0:T(8,128)(2,1)} %get-tuple-element.420), channel_id=1, source_target_pairs={{0,32},{32,64},{64,96},{96,0},{1,33},{33,65},{65,97},{97,1},{2,34}... | collective-permute-start | bytes 1990664 | tf_op jit(solution)/shard_map/ppermute | solution.py:34
  399.7 33.1 %collective-permute-start.83 = (bf16[288,1152]{1,0:T(8,128)(2,1)}, bf16[288,1152]{1,0:T(8,128)(2,1)}, u32[]{:S(2)}, u32[]{:S(2)}) collective-permute-start(bf16[288,1152]{1,0:T(8,128)(2,1)} %get-tuple-element.419), channel_id=1, source_target_pairs={{0,64},{32,96},{64,0},{96,32},{1,65},{33,97},{65,1},{97,33},{2,66}... | collective-permute-start | bytes 1990664 | tf_op jit(solution)/shard_map/ppermute | solution.py:34
  401.0 32.2 %collective-permute-start.84 = (bf16[288,1152]{1,0:T(8,128)(2,1)}, bf16[288,1152]{1,0:T(8,128)(2,1)}, u32[]{:S(2)}, u32[]{:S(2)}) collective-permute-start(bf16[288,1152]{1,0:T(8,128)(2,1)} %get-tuple-element.418), channel_id=1, source_target_pairs={{0,96},{32,0},{64,32},{96,64},{1,97},{33,1},{65,33},{97,65},{2,98}... | collective-permute-start | bytes 1990664 | tf_op jit(solution)/shard_map/ppermute | solution.py:34
  409.2 28.4 %collective-permute-start.85 = (bf16[144,1152]{1,0:T(8,128)(2,1)}, bf16[144,1152]{1,0:T(8,128)(2,1)}, u32[]{:S(2)}, u32[]{:S(2)}) collective-permute-start(bf16[144,1152]{1,0:T(8,128)(2,1)} %add_convert_fusion.6), channel_id=1, source_target_pairs={{4,0},{24,12},{20,16},{8,28},{5,1},{25,13},{21,17},{9,29},{6,2},{2... | collective-permute-start | bytes 995336 | tf_op jit(solution)/shard_map/ppermute | solution.py:570
  411.9 26.6 %collective-permute-start.86 = (bf16[144,1152]{1,0:T(8,128)(2,1)}, bf16[144,1152]{1,0:T(8,128)(2,1)}, u32[]{:S(2)}, u32[]{:S(2)}) collective-permute-start(bf16[144,1152]{1,0:T(8,128)(2,1)} %add_convert_fusion.6), channel_id=1, source_target_pairs={{16,0},{28,12},{0,16},{12,28},{17,1},{29,13},{1,17},{13,29},{18,2}... | collective-permute-start | bytes 995336 | tf_op jit(solution)/shard_map/ppermute | solution.py:570
  419.0 19.4 %collective-permute-start.87 = (bf16[144,1152]{1,0:T(8,128)(2,1)}, bf16[144,1152]{1,0:T(8,128)(2,1)S(1)}, u32[]{:S(2)}, u32[]{:S(2)}) collective-permute-start(bf16[144,1152]{1,0:T(8,128)(2,1)} %add_convert_fusion.6), channel_id=1, source_target_pairs={{20,0},{8,12},{4,16},{24,28},{21,1},{9,13},{5,17},{25,29},{22,2},{... | collective-permute-start | bytes 995336 | tf_op jit(solution)/shard_map/ppermute | solution.py:570
  432.8 25.3 %collective-permute-start.79 = (bf16[96,1152]{1,0:T(8,128)(2,1)}, bf16[96,1152]{1,0:T(8,128)(2,1)}, u32[]{:S(2)}, u32[]{:S(2)}) collective-permute-start(bf16[96,1152]{1,0:T(8,128)(2,1)} %get-tuple-element.352), channel_id=1, source_target_pairs={{0,1},{1,2},{2,3},{3,0},{4,5},{5,6},{6,7},{7,4},{8,9},{9,10},{10,1... | collective-permute-start | bytes 663560 | tf_op jit(solution)/shard_map/ppermute | solution.py:34
  433.2 26.4 %collective-permute-start.80 = (bf16[96,1152]{1,0:T(8,128)(2,1)}, bf16[96,1152]{1,0:T(8,128)(2,1)}, u32[]{:S(2)}, u32[]{:S(2)}) collective-permute-start(bf16[96,1152]{1,0:T(8,128)(2,1)} %get-tuple-element.353), channel_id=1, source_target_pairs={{0,2},{1,3},{2,0},{3,1},{4,6},{5,7},{6,4},{7,5},{8,10},{9,11},{10,... | collective-permute-start | bytes 663560 | tf_op jit(solution)/shard_map/ppermute | solution.py:34
  437.7 23.3 %collective-permute-start.81 = (bf16[96,1152]{1,0:T(8,128)(2,1)}, bf16[96,1152]{1,0:T(8,128)(2,1)}, u32[]{:S(2)}, u32[]{:S(2)}) collective-permute-start(bf16[96,1152]{1,0:T(8,128)(2,1)} %copy-done.100), channel_id=1, source_target_pairs={{0,3},{1,0},{2,1},{3,2},{4,7},{5,4},{6,5},{7,6},{8,11},{9,8},{10,9... | collective-permute-start | bytes 663560 | tf_op jit(solution)/shard_map/ppermute | solution.py:34
  448.0 15.4 %collective-permute-start.111 = (bf16[72,1152]{1,0:T(8,128)(2,1)}, bf16[72,1152]{1,0:T(8,128)(2,1)}, u32[]{:S(2)}, u32[]{:S(2)}) collective-permute-start(bf16[72,1152]{1,0:T(8,128)(2,1)} %get-tuple-element.441), channel_id=1, source_target_pairs={{0,4},{4,16},{16,20},{20,0},{1,5},{5,17},{17,21},{21,1},{2,6},{6,1... | collective-permute-start | bytes 497672 | tf_op jit(solution)/shard_map/ppermute | solution.py:34
  449.6 13.8 %collective-permute-start.112 = (bf16[72,1152]{1,0:T(8,128)(2,1)}, bf16[72,1152]{1,0:T(8,128)(2,1)}, u32[]{:S(2)}, u32[]{:S(2)}) collective-permute-start(bf16[72,1152]{1,0:T(8,128)(2,1)} %get-tuple-element.440), channel_id=1, source_target_pairs={{0,16},{4,20},{16,0},{20,4},{1,17},{5,21},{17,1},{21,5},{2,18},{6,... | collective-permute-start | bytes 497672 | tf_op jit(solution)/shard_map/ppermute | solution.py:34
  469.1 185.8 %collective-permute-start.49 = (bf16[96,1152]{1,0:T(8,128)(2,1)S(1)}, bf16[96,1152]{1,0:T(8,128)(2,1)S(1)}, u32[]{:S(2)}, u32[]{:S(2)}) collective-permute-start(bf16[96,1152]{1,0:T(8,128)(2,1)S(1)} %shard_map.250.refs_0_), channel_id=1, source_target_pairs={{0,3},{1,0},{2,1},{3,2},{4,7},{5,4},{6,5},{7,6},{8,11},{9,8},{10,9... | collective-permute-start | bytes 663560 | tf_op jit(solution)/shard_map/ppermute | solution.py:34
  470.6 185.2 %collective-permute-start.50 = (bf16[96,1152]{1,0:T(8,128)(2,1)S(1)}, bf16[96,1152]{1,0:T(8,128)(2,1)S(1)}, u32[]{:S(2)}, u32[]{:S(2)}) collective-permute-start(bf16[96,1152]{1,0:T(8,128)(2,1)S(1)} %shard_map.250.refs_0_), channel_id=1, source_target_pairs={{0,2},{1,3},{2,0},{3,1},{4,6},{5,7},{6,4},{7,5},{8,10},{9,11},{10,... | collective-permute-start | bytes 663560 | tf_op jit(solution)/shard_map/ppermute | solution.py:34
  473.4 98.2 %collective-permute-start.95 = (bf16[4,152,1152]{2,1,0:T(8,128)(2,1)}, bf16[4,152,1152]{2,1,0:T(8,128)(2,1)}, u32[]{:S(2)}, u32[]{:S(2)}) collective-permute-start(bf16[4,152,1152]{2,1,0:T(8,128)(2,1)} %get-tuple-element.367), channel_id=1, source_target_pairs={{0,8},{8,0},{1,9},{9,1},{2,10},{10,2},{3,11},{11,3},{4,12},{12,4},... | collective-permute-start | bytes 4202504 | tf_op jit(solution)/shard_map/ppermute | solution.py:34
  485.5 83.7 %collective-permute-start.117 = (bf16[288,1152]{1,0:T(8,128)(2,1)S(1)}, bf16[288,1152]{1,0:T(8,128)(2,1)}, u32[]{:S(2)}, u32[]{:S(2)}) collective-permute-start(bf16[288,1152]{1,0:T(8,128)(2,1)S(1)} %bitcast.145), channel_id=1, source_target_pairs={{32,0},{44,12},{64,32},{76,44},{96,64},{108,76},{0,96},{12,108},{3... | collective-permute-start | bytes 1990664 | tf_op jit(solution)/shard_map/ppermute | solution.py:561
  574.8 12.6 %collective-permute-start.97 = (bf16[152,1152]{1,0:T(8,128)(2,1)S(1)}, bf16[152,1152]{1,0:T(8,128)(2,1)S(1)}, u32[]{:S(2)}, u32[]{:S(2)}) collective-permute-start(bf16[152,1152]{1,0:T(8,128)(2,1)S(1)} %get-tuple-element.430), channel_id=1, source_target_pairs={{0,64},{32,96},{64,0},{96,32},{1,65},{33,97},{65,1},{97,33},{2,66}... | collective-permute-start | bytes 1050632 | tf_op jit(solution)/shard_map/ppermute | solution.py:34
  575.8 16.2 %collective-permute-start.96 = (bf16[152,1152]{1,0:T(8,128)(2,1)S(1)}, bf16[152,1152]{1,0:T(8,128)(2,1)S(1)}, u32[]{:S(2)}, u32[]{:S(2)}) collective-permute-start(bf16[152,1152]{1,0:T(8,128)(2,1)S(1)} %get-tuple-element.428), channel_id=1, source_target_pairs={{0,32},{32,64},{64,96},{96,0},{1,33},{33,65},{65,97},{97,1},{2,34}... | collective-permute-start | bytes 1050632 | tf_op jit(solution)/shard_map/ppermute | solution.py:34
  592.1 30.7 %collective-permute-start.101 = (bf16[152,1152]{1,0:T(8,128)(2,1)S(1)}, bf16[152,1152]{1,0:T(8,128)(2,1)S(1)}, u32[]{:S(2)}, u32[]{:S(2)}) collective-permute-start(bf16[152,1152]{1,0:T(8,128)(2,1)S(1)} %fusion.2), channel_id=1, source_target_pairs={{0,20},{4,0},{16,4},{20,16},{1,21},{5,1},{17,5},{21,17},{2,22},{6,... | collective-permute-start | bytes 1050632 | tf_op jit(solution)/shard_map/ppermute | solution.py:34
  613.5 13.1 %collective-permute-start.100 = (bf16[152,1152]{1,0:T(8,128)(2,1)S(1)}, bf16[152,1152]{1,0:T(8,128)(2,1)S(1)}, u32[]{:S(2)}, u32[]{:S(2)}) collective-permute-start(bf16[152,1152]{1,0:T(8,128)(2,1)S(1)} %fusion.2), channel_id=1, source_target_pairs={{0,16},{4,20},{16,0},{20,4},{1,17},{5,21},{17,1},{21,5},{2,18},{6,... | collective-permute-start | bytes 1050632 | tf_op jit(solution)/shard_map/ppermute | solution.py:34
  614.6 13.8 %collective-permute-start.99 = (bf16[152,1152]{1,0:T(8,128)(2,1)S(1)}, bf16[152,1152]{1,0:T(8,128)(2,1)S(1)}, u32[]{:S(2)}, u32[]{:S(2)}) collective-permute-start(bf16[152,1152]{1,0:T(8,128)(2,1)S(1)} %fusion.2), channel_id=1, source_target_pairs={{0,4},{4,16},{16,20},{20,0},{1,5},{5,17},{17,21},{21,1},{2,6},{6,1... | collective-permute-start | bytes 1050632 | tf_op jit(solution)/shard_map/ppermute | solution.py:34
  622.9 34.3 %collective-permute-start.51 = (bf16[96,1152]{1,0:T(8,128)(2,1)S(1)}, bf16[96,1152]{1,0:T(8,128)(2,1)S(1)}, u32[]{:S(2)}, u32[]{:S(2)}) collective-permute-start(bf16[96,1152]{1,0:T(8,128)(2,1)S(1)} %shard_map.250.refs_0_), channel_id=1, source_target_pairs={{0,1},{1,2},{2,3},{3,0},{4,5},{5,6},{6,7},{7,4},{8,9},{9,10},{10,1... | collective-permute-start | bytes 663560 | tf_op jit(solution)/shard_map/ppermute | solution.py:34
  626.6 98.1 %collective-permute-start.121 = (bf16[2,576,1152]{2,1,0:T(8,128)(2,1)S(1)}, bf16[2,576,1152]{2,1,0:T(8,128)(2,1)}, u32[]{:S(2)}, u32[]{:S(2)}) collective-permute-start(bf16[2,576,1152]{2,1,0:T(8,128)(2,1)S(1)} %copy-done.110), channel_id=1, source_target_pairs={{0,8},{8,0},{1,9},{9,1},{2,10},{10,2},{3,11},{11,3},{4,12},{12,4},... | collective-permute-start | bytes 7962632 | tf_op jit(solution)/shard_map/ppermute | solution.py:34
  631.1 93.6 %collective-permute-start.120 = (bf16[2,576,1152]{2,1,0:T(8,128)(2,1)S(1)}, bf16[2,576,1152]{2,1,0:T(8,128)(2,1)}, u32[]{:S(2)}, u32[]{:S(2)}) collective-permute-start(bf16[2,576,1152]{2,1,0:T(8,128)(2,1)S(1)} %bitcast.136), channel_id=1, source_target_pairs={{0,8},{8,0},{1,9},{9,1},{2,10},{10,2},{3,11},{11,3},{4,12},{12,4},... | collective-permute-start | bytes 7962632 | tf_op jit(solution)/shard_map/ppermute | solution.py:34
  654.9 13.4 %collective-permute-start.52 = (bf16[96,1152]{1,0:T(8,128)(2,1)S(1)}, bf16[96,1152]{1,0:T(8,128)(2,1)S(1)}, u32[]{:S(2)}, u32[]{:S(2)}) collective-permute-start(bf16[96,1152]{1,0:T(8,128)(2,1)S(1)} %collective-permute-done.41.refs_4_), channel_id=1, source_target_pairs={{0,3},{1,0},{2,1},{3,2},{4,7},{5,4},{6,5},{7,6},{8,11},{9,8},{10,9... | collective-permute-start | bytes 663560 | tf_op jit(solution)/shard_map/ppermute | solution.py:34
  655.8 12.5 %collective-permute-start.53 = (bf16[96,1152]{1,0:T(8,128)(2,1)S(1)}, bf16[96,1152]{1,0:T(8,128)(2,1)S(1)}, u32[]{:S(2)}, u32[]{:S(2)}) collective-permute-start(bf16[96,1152]{1,0:T(8,128)(2,1)S(1)} %collective-permute-done.41.refs_4_), channel_id=1, source_target_pairs={{0,2},{1,3},{2,0},{3,1},{4,6},{5,7},{6,4},{7,5},{8,10},{9,11},{10,... | collective-permute-start | bytes 663560 | tf_op jit(solution)/shard_map/ppermute | solution.py:34
  657.1 55.4 %collective-permute-start.105 = (bf16[4,152,1152]{2,1,0:T(8,128)(2,1)S(1)}, bf16[4,152,1152]{2,1,0:T(8,128)(2,1)S(1)}, u32[]{:S(2)}, u32[]{:S(2)}) collective-permute-start(bf16[4,152,1152]{2,1,0:T(8,128)(2,1)S(1)} %constant_dynamic-slice_fusion.2.full0), channel_id=1, source_target_pairs={{0,8},{8,0},{1,9},{9,1},{2,10},{10,2},{3,11},{11,3},{4,12},{12,4},... | collective-permute-start | bytes 4202504 | tf_op jit(solution)/shard_map/ppermute | solution.py:34
  668.3 40.9 %collective-permute-start.106 = (bf16[4,144,1152]{2,1,0:T(8,128)(2,1)S(1)}, bf16[4,144,1152]{2,1,0:T(8,128)(2,1)S(1)}, u32[]{:S(2)}, u32[]{:S(2)}) collective-permute-start(bf16[4,144,1152]{2,1,0:T(8,128)(2,1)S(1)} %constant_dynamic-slice_fusion.3.full1), channel_id=1, source_target_pairs={{0,8},{8,0},{1,9},{9,1},{2,10},{10,2},{3,11},{11,3},{4,12},{12,4},... | collective-permute-start | bytes 3981320 | tf_op jit(solution)/shard_map/ppermute | solution.py:34
  709.2 13.0 %collective-permute-start.93 = (bf16[96,1152]{1,0:T(8,128)(2,1)S(1)}, bf16[96,1152]{1,0:T(8,128)(2,1)S(1)}, u32[]{:S(2)}, u32[]{:S(2)}) collective-permute-start(bf16[96,1152]{1,0:T(8,128)(2,1)S(1)} %collective-permute-done.91.refs_4_), channel_id=1, source_target_pairs={{0,2},{1,3},{2,0},{3,1},{4,6},{5,7},{6,4},{7,5},{8,10},{9,11},{10,... | collective-permute-start | bytes 663560 | tf_op jit(solution)/shard_map/ppermute | solution.py:34
  718.3 15.7 %collective-permute-start.107 = (bf16[4,8,1152]{2,1,0:T(8,128)(2,1)S(1)}, bf16[4,8,1152]{2,1,0:T(8,128)(2,1)S(1)}, u32[]{:S(2)}, u32[]{:S(2)}) collective-permute-start(bf16[4,8,1152]{2,1,0:T(8,128)(2,1)S(1)} %get-tuple-element.386), channel_id=1, source_target_pairs={{0,4},{4,0},{1,5},{5,1},{2,6},{6,2},{3,7},{7,3},{8,12},{12,8},{9,1... | collective-permute-start | bytes 221192 | tf_op jit(solution)/shard_map/ppermute | solution.py:34
  (187 other events, 2389.0 us)
Sparse Core Ops, SparseCore 0:
  473.5 94.8 all-reduce.8

commit v2 on v1

--- a/solution.py
+++ b/solution.py
@@ -399,11 +399,15 @@
     )
 
 
-def mlp_kernel(layer, c0, c1, c2, c3, wu0, wu1, ub0, ub1, wd0, wd1, nt_out, up_out, act_out, *sends):
+def joined(parts):
+    return jnp.concatenate([part[...] for part in parts], axis=0)
+
+
+def mlp_kernel(layer, c0, c1, c2, c3, ub0, ub1, wu0, wd0, wu1, wu2, wd1, wd2, nt_out, up_out, act_out, *sends):
     nt = whole((c0, c1, c2, c3))
     nt_out[...] = nt
     total = None
-    for g, wu, ub, wd in ((0, wu0, ub0, wd0), (1, wu1, ub1, wd1)):
+    for g, wu, ub, wd in ((0, wu0, ub0, wd0), (1, joined((wu1, wu2)), ub1, joined((wd1, wd2)))):
         u = dot_nt(nt, wu[...]) + ub[layer : layer + 1]
         up_out[g] = u
         act = (0.5 * u * (1.0 + jnp.tanh(gelu_coef * (u + 0.044715 * u * u * u)))).astype(bf16)
@@ -422,17 +426,18 @@
             shaped((2, NT, FP), bf16),
             *SENDS,
         ],
-        *chunks, own[2], oth[2], ub0, ub1, own[3], oth[3],
+        *chunks, ub0, ub1, own[2], own[3], *oth[2], *oth[3],
     )
 
 
 def mlp_back_kernel(n, *refs):
-    chunks, (up, wu0, wu1, wd0, wd1) = refs[:n], refs[n : n + 5]
-    d_up_out, sums = refs[n + 5 : n + 7]
-    sends = refs[n + 7 : n + 11]
+    chunks, (up, wu0, wd0) = refs[:n], refs[n : n + 3]
+    wu1, wd1 = joined(refs[n + 3 : n + 5]), joined(refs[n + 5 : n + 7])
+    d_up_out, sums = refs[n + 7 : n + 9]
+    sends = refs[n + 9 : n + 13]
     low = whole(chunks)
     if n > 1:
-        refs[n + 11][...] = low
+        refs[n + 13][...] = low
     total = None
     for g, wu, wd in ((0, wu0, wd0), (1, wu1, wd1)):
         d_act = dot_nt(low, wd[...])
@@ -455,7 +460,7 @@
     if n > 1:
         outs.append(shaped((NT, D), bf16))
     got = call(
-        functools.partial(mlp_back_kernel, n), outs, *chunks, up, own[2], oth[2], own[3], oth[3]
+        functools.partial(mlp_back_kernel, n), outs, *chunks, up, own[2], own[3], *oth[2], *oth[3]
     )
     return got[0], got[1], got[2:6], (got[6] if n > 1 else chunks[0])
 
@@ -465,11 +470,13 @@
     for j, (a, b) in enumerate(((d_up, nt), (act, low))):
         for out, g in ((keep_out, 0), (sent_out, 1)):
             picked = jnp.where(first, a[g], a[1 - g])
-            out[j] = dot_tn(picked, b[...]).astype(bf16)
+            got = dot_tn(picked, b[...]).astype(bf16)
+            for k in range(2):
+                out[2 * j + k] = got[2 * CW * k : 2 * CW * (k + 1)]
 
 
 def attend_weights_kernel(
-    pos, stacked, mixed_a, mixed_b, normed, mid, wide, near, beside, keep_out, sent_out
+    pos, stacked, mixed_a, mixed_b, normed, mid, near, beside, keep_out, sent_out
 ):
     first = pos[2] == 0
     for out, g in ((keep_out, 0), (sent_out, 1)):
@@ -480,8 +487,6 @@
         out[3, :CW] = dot_tn(jnp.where(first, mixed[0], mixed[1]), mid[...]).astype(bf16)
         extra = (near, beside) if g == 0 else (beside, near)
         extra = jnp.where(first, extra[0][...], extra[1][...])
-        if g == 0:
-            extra = extra + wide[...]
         out[:, CW:] = extra.astype(bf16)
 
 
@@ -499,8 +504,8 @@
     first = pos[2] == 0
     for layer, (full, other) in enumerate(((full0, other0), (full1, other1))):
         for j, out in enumerate((up, down)):
-            got = jnp.where(first, full[j], other[j])
-            out[:, layer, :] = got[:FW].astype(f32)
+            got = [jnp.where(first, full[k], other[k]) for k in (2 * j, 2 * j + 1)]
+            out[:, layer, :] = jnp.concatenate(got, axis=0)[:FW].astype(f32)
 
 
 def mlp_final(pos, sums):
@@ -508,7 +513,7 @@
     return call(mlp_final_kernel, [shaped((FW, 2, D), f32)] * 2, *args, pos=pos)
 
 
-def attend_final_kernel(pos, full0, other0, full1, other1, qkv, out, wide, narrow):
+def attend_final_kernel(pos, full0, other0, full1, other1, qkv, out, small):
     first = pos[2] == 0
     for layer, (full, other) in enumerate(((full0, other0), (full1, other1))):
         got = jnp.where(first, full[...], other[...]).astype(f32)
@@ -516,14 +521,13 @@
             qkv[layer, j] = got[j, :CW]
         out[layer] = got[3, :CW]
         if layer == 0:
-            narrow[...] = got[:, CW:]
-            wide[...] = got[:, CW:].astype(bf16)
+            small[...] = got[:, CW:]
 
 
 def attend_final(pos, sums):
     args = [part for total in sums for part in total]
     outs = [shaped((2, 3, CW, D), f32), shaped((2, CW, D), f32)]
-    outs += [shaped((4, EXTRA, D), bf16), shaped((4, EXTRA, D), f32)]
+    outs += [shaped((4, EXTRA, D), f32)]
     return call(attend_final_kernel, outs, *args, pos=pos)
 
 
@@ -575,50 +579,62 @@
     return sum(part.astype(f32) for part in parts).astype(bf16)
 
 
+def pieces_kernel(pos, *refs):
+    ins, outs = refs[:-4], refs[-4:]
+    for k in range(4):
+        block = lax.rem(pos[0] + k, 4)
+        outs[k][...] = sum(ref[block].astype(f32) for ref in ins).astype(bf16)
+
+
+def sum_pieces(index, *parts):
+    shape = parts[0].shape
+    outs = [shaped(shape[1:], bf16)] * 4
+    return call(pieces_kernel, outs, *parts, pos=index)
+
+
+def total_kernel(*refs):
+    refs[-1][...] = sum(ref[...].astype(f32) for ref in refs[:-1]).astype(bf16)
+
+
+def sum_parts(*parts):
+    return call(total_kernel, [shaped(parts[0].shape, bf16)], *parts)[0]
+
+
+def blocks_kernel(pos, *refs):
+    for k in range(4):
+        refs[4][lax.rem(pos[0] + k, 4)] = refs[k][...]
+
+
+def place_blocks(index, parts):
+    return call(blocks_kernel, [shaped((4, *parts[0].shape), bf16)], *parts, pos=index)[0]
+
+
 class WeightSum:
-    def __init__(self, kept, sent, where, y_first, direct):
-        y, z = where
-        self.one, self.two = (("y", y), (Z, z)) if y_first else ((Z, z), ("y", y))
-        self.shape = kept.shape
-        self.rows = kept.shape[0] * kept.shape[1] // 4
-        self.direct = direct
+    def __init__(self, kept, sent, y):
+        self.y = y[None]
         self.pending = (kept, shift(sent, "c", 1))
         self.step = 0
 
-    def advance(self, anchor, late=None):
+    def advance(self, anchor=None, late=None):
         pending = self.pending if anchor is None else after(self.pending, anchor)
         step, self.step = self.step, self.step + 1
-        r = self.rows
         if step == 0:
-            both = total_of(pending if late is None else (*pending, late)).reshape(4, r, D)
-            feed = pieces_of(both, self.one[1])
-            self.pending = scatter_ring(feed, self.one[0])
-        elif step == 1 and self.direct:
-            feed = total_of(pending)
-            self.pending = [feed] + [shift(feed, self.two[0], k) for k in (1, 2, 3)]
-            self.step += 1
+            feed = sum_pieces(self.y, *pending)
+            self.pending = scatter_ring(feed, "y")
         elif step == 1:
-            piece = total_of(pending).reshape(4, r // 4, D)
-            feed = pieces_of(piece, self.two[1])
-            self.pending = scatter_ring(feed, self.two[0])
+            feed = sum_parts(*(pending if late is None else (*pending, late)))
+            self.pending = [feed] + [shift(feed, Z, k) for k in (1, 2, 3)]
         elif step == 2:
-            feed = total_of(pending)
-            self.pending = gather_ring(feed, self.two[0], self.two[0] == Z)
-        elif step == 3:
-            if self.direct:
-                feed = total_of(pending)
-            else:
-                feed = rolled(jnp.stack(pending), (4 - self.two[1]) % 4).reshape(r, D)
-            self.pending = gather_ring(feed, self.one[0], True)
+            feed = sum_parts(*pending)
+            self.pending = gather_ring(feed, "y", True)
         else:
-            feed = rolled(jnp.stack(pending), (4 - self.one[1]) % 4).reshape(self.shape)
+            feed = place_blocks(self.y, pending)
             self.pending = (feed, shift(feed, "c", 1))
         return feed
 
-    def finish(self):
-        while self.step < 5:
-            self.advance(None)
-        return self.pending
+
+def sum_ring(value, axis):
+    return value + sum(shift(value, axis, k) for k in range(1, SIZES[axis]))
 
 
 def local(
@@ -639,8 +655,6 @@
 ):
     layers = w_qkv.shape[0]
     zl, c, x, y = (lax.axis_index(name) for name in ("zl", "c", "x", "y"))
-    z = lax.axis_index("zh") * 2 + zl
-    where = (y, z)
     pos = jnp.stack([zl, x, jnp.where(zl == c, 0, 1)]).astype(jnp.int32)
 
     wq_t = jnp.swapaxes(w_qkv, 2, 3).reshape(layers, 3 * CW, D)
@@ -651,115 +665,124 @@
 
     wq = [(wq_t[0], far_projection(wq_t[0]))]
     up_bias = jnp.pad(up_bias, ((0, 0), (0, FP - FW)))
-    qb_far, vb_far, ids_far = shift(q_bias, "zl", 1), shift(v_bias, "zl", 1), shift(picture_ids, "c", 1)
+    qb_far, vb_far, ub_far = (shift(part, "zl", 1) for part in (q_bias, v_bias, up_bias))
+    ids_far = shift(picture_ids, "c", 1)
     biases = (q_bias, qb_far, v_bias, vb_far)
     normed, stream = call(
         first_kernel, [shaped((NT, D), bf16), shaped((CHUNK, D), f32)],
         inputs, norm_gain, norm_bias, pos=pos,
     )
 
-    w_out, w_up, w_down, up_bias = after((w_out, w_up, w_down, up_bias), normed)
-    ub_far = shift(up_bias, "zl", 1)
+    w_out, w_up, w_down = after((w_out, w_up, w_down), normed)
     pad = ((0, FP - FW), (0, 0))
     rest = [
         (w_out[layer], jnp.pad(w_up[layer].T, pad), jnp.pad(w_down[layer], pad))
         for layer in range(layers)
     ]
     far_out = [shift(rest[0][0], Z, 1)]
-    far_mlp = []
+    far_up, far_down = [[], []], [[], []]
+
+    def fetch(layer, which, part, anchor):
+        half_rows = after(rest[layer][which][part * FP // 2 : (part + 1) * FP // 2], anchor)
+        got = shift(half_rows, Z, 1 if which == 1 else -1)
+        (far_up if which == 1 else far_down)[layer].append(got)
+        return got
+
     ids = arrange_ids(pos, picture_ids, ids_far)
 
-    chunks = [normed]
+    chunks = [after(normed, ub_far)]
     kept = []
     weights = []
     for layer in range(layers):
+        more = layer < layers - 1
         q, kv, part, normed = project(layer, chunks, *wq[layer], biases)
         kvo = shift(kv, "c", 1)
         kvz = shift(part, "zl", 1)
         kvd = shift(kvz, "c", 1)
         wo = (rest[layer][0], far_out[layer])
         mixed_a, total_a = attend_row(q, (kv, kvo), ((0, NA), (0, NA)), ids[0], ids[1], wo)
-        up_sent, down_sent = after(rest[layer][1:], kvz)
-        far_mlp.append((shift(up_sent, Z, 1), shift(down_sent, Z, -1)))
+        if layer == 0:
+            halves = [fetch(0, which, 0, (kvz, far_out[0])) for which in (1, 2)]
         mixed_b, *sends = attend_quarter(
             q, (kv, kvo, kvz, kvd), ((NA, NB), (NA, NB), (0, NB), (0, NB)),
             ids[2], ids[3], wo, total_a,
         )
         got = scatter_x(sends)
+        if layer == 0:
+            later = [fetch(0, which, 1, (halves, got[1])) for which in (1, 2)]
+        else:
+            later = [fetch(layer, which, 1, sends[0]) for which in (1, 2)]
+            low_in, grad_flow, d_down_bias = call(
+                cotangent_kernel,
+                [shaped((NT, D), bf16), shaped((CHUNK, D), f32), shaped((1, D), f32)],
+                after(cotangent, sends[0]), ids[0], ids[2], pos=pos,
+            )
+            got = after(got, low_in)
         middle, low = norm_step(layer, (layer, 1), stream, got, out_bias, norm_gain, norm_bias)
         own = (wq[layer][0], *rest[layer])
-        oth = (wq[layer][1], far_out[layer], *far_mlp[layer])
+        oth = (wq[layer][1], far_out[layer], far_up[layer], far_down[layer])
         weights.append((own, oth))
-        normed_two, up, act, *sends = mlp(layer, gather_x(low), own, oth, up_bias, ub_far)
-        got = scatter_x(sends)
+        chunks = gather_x(low)
+        if more:
+            wq.append((wq_t[layer + 1], far_projection(after(wq_t[layer + 1], chunks[1]))))
+            chunks = after(chunks, later)
+        normed_two, up, act, *sends = mlp(layer, chunks, own, oth, up_bias, ub_far)
         kept.append(
             (stream, normed, q, kv, kvo, kvz, kvd, mixed_a, mixed_b, middle, normed_two, up, act)
         )
-        if layer < layers - 1:
-            next_q, next_out = after((wq_t[layer + 1], rest[layer + 1][0]), sends[0])
-            wq.append((wq_t[layer + 1], far_projection(next_q)))
-            far_out.append(shift(next_out, Z, 1))
+        if more:
+            got = scatter_x(sends)
+            next_far = (wq[layer + 1][1], sends[0])
+            far_out.append(shift(after(rest[layer + 1][0], next_far), Z, 1))
+            halves = [fetch(layer + 1, which, 0, next_far) for which in (1, 2)]
             stream, low = norm_step(
                 layer, (layer + 1, 0), middle, got, down_bias, norm_gain, norm_bias
             )
             chunks = gather_x(low)
-
-    low, grad_flow, d_down_bias = call(
-        cotangent_kernel,
-        [shaped((NT, D), bf16), shaped((CHUNK, D), f32), shaped((1, D), f32)],
-        after(cotangent, normed_two), ids[0], ids[2], pos=pos,
-    )
-    result = call(
-        functools.partial(result_kernel, layers - 1), [shaped((CHUNK, D), bf16)],
-        middle, *got, down_bias,
-    )[0]
-    chunks = [low]
+            chunks = after(chunks, (halves, far_out[layer + 1]))
+
+    last_sends, last_middle = sends, middle
     zeros = jnp.zeros((1, D), f32)
-    wide = [[None] * 6 for _ in range(layers)]
-    narrow = [None] * layers
-    sums = {}
-    for layer in reversed(range(layers)):
+    here = picture_ids[0, 0] > -2
+
+    def apart(work):
+        shapes = jax.eval_shape(work)
+        return lax.cond(
+            here, work, lambda: jax.tree.map(lambda s: jnp.zeros(s.shape, s.dtype), shapes)
+        )
+
+    def feed_forward_back(layer, chunks, grad_flow):
         own, oth = weights[layer]
-        (stream_in, normed, q, kv, kvo, kvz, kvd, mixed_a, mixed_b, middle, normed_two, up, act) = (
-            kept[layer]
-        )
-        last = layer == layers - 1
+        middle, normed_two, up, act = kept[layer][-4:]
         d_up, d_up_bias, sends, grad_low = mlp_back(chunks, up, own, oth)
         got = scatter_x(sends)
         kept_m, sent_m = call(
-            mlp_weights_kernel, [shaped((2, FP, D), bf16)] * 2,
+            mlp_weights_kernel, [shaped((4, 2 * CW, D), bf16)] * 2,
             d_up, act, normed_two, grad_low, pos=pos,
         )
-        feeds = [sent_m]
-        if last:
-            far_m = shift(sent_m, "c", 1)
-            out_far = shift(after(result, sends[0]), "zl", 1)
-        else:
-            feeds.append(sums["a1"].advance(sends[0]))
-            sums["m0"] = WeightSum(kept_m, sent_m, where, True, False)
-        got = after(got, feeds)
+        far_m = shift(sent_m, "c", 1)
+        got = after(got, sent_m)
         grad_mid, mid_low, norm_two = norm_back((layer, 1), middle, got, grad_flow, norm_gain)
+        feed = sum_parts(kept_m, far_m)
+        return grad_mid, mid_low, norm_two, d_up_bias, feed
+
+    def attention_back(layer, mid_low, result=None):
+        own, oth = weights[layer]
+        stream_in, normed, q, kv, kvo, kvz, kvd, mixed_a, mixed_b = kept[layer][:9]
         mid_chunks = gather_x(mid_low)
-        if last:
-            both = total_of((kept_m, after(far_m, mid_low)))
-            sum_m1 = lax.psum(both, ("y", "zh", "zl"))
-            feeds = [both]
-        else:
-            feeds = [sums["m0"].advance(mid_low), sums["a1"].advance(mid_low)]
-        mid_chunks = after(mid_chunks, feeds)
         mid, dq, d_own, d_far, d_z = attend_back(
             mid_chunks, q, kv, kvo, kvz, kvd, ids, (own[1], oth[1])
         )
         d_far = shift(d_far, "c", 1)
         d_z = shift((d_z + d_far[..., NT:].astype(f32)).astype(bf16), "zl", 1)
-        if last:
-            near, beside = after((result, out_far), mid)
-            out_slots = gather_x(near) + gather_x(beside)
+        if result is not None:
+            result = result(mid_chunks[0])
+            d_z = after(d_z, result)
         stacked, d_qv_bias, *sends = project_back(dq, d_own, d_far, d_z, own[0], oth[0])
-        got = scatter_x(sends)
-        wide[layer][1], wide[layer][3], wide[layer][4] = (norm_two[i : i + 1] for i in range(3))
-        wide[layer][5] = d_down_bias
-        narrow[layer] = [
+        return mid, stacked, d_qv_bias, sends, result
+
+    def narrow_rows(d_qv_bias, d_up_bias):
+        return [
             jnp.concatenate(
                 [
                     d_qv_bias[g].reshape(1, 2 * CW),
@@ -770,59 +793,88 @@
             )
             for g in range(2)
         ]
-        extra = [jnp.zeros((4, 0, D), f32)] * 3
-        if not last:
-            rows = [row for part in wide for row in part]
-            rows = [zeros if row is None else row for row in rows]
+
+    def last_result(anchor):
+        got = scatter_x(after(last_sends, anchor))
+        return call(
+            functools.partial(result_kernel, layers - 1), [shaped((CHUNK, D), bf16)],
+            last_middle, *got, down_bias,
+        )[0]
+
+    grad_mid1, mid_low1, norm_two1, d_up_bias1, feed_m1 = feed_forward_back(1, [low_in], grad_flow)
+    sum_m1 = lax.psum(feed_m1, ("y", "zh", "zl"))
+
+    def first_block():
+        stream_in, normed, q, kv, kvo, kvz, kvd, mixed_a, mixed_b = kept[1][:9]
+        mid, stacked, d_qv_bias, sends, result = attention_back(1, mid_low1, last_result)
+        got = scatter_x(sends)
+        kept_a, sent_a = call(
+            plain_weights_kernel, [shaped((4, CW, D), bf16)] * 2,
+            stacked, mixed_a, mixed_b, normed, mid, pos=pos,
+        )
+        far_a = shift(sent_a, "c", 1)
+        grad_flow, low, norm_one = norm_back((1, 0), stream_in, got, grad_mid1, norm_gain)
+        chunks = gather_x(low)
+        out_far = shift(after(result, low), "zl", 1)
+        feed_a = sum_parts(kept_a, far_a)
+        back = feed_forward_back(0, chunks, grad_flow)
+        return d_qv_bias, norm_one, result, out_far, feed_a, back
+
+    d_qv_bias1, norm_one1, result, out_far, feed_a1, back = apart(first_block)
+    grad_mid0, mid_low0, norm_two0, d_up_bias0, feed_m0 = back
+    sum_a1, sum_m0 = lax.psum(after((feed_a1, feed_m0), sum_m1), ("y", "zh", "zl"))
+
+    def second_block():
+        stream_in, normed, q, kv, kvo, kvz, kvd, mixed_a, mixed_b = kept[0][:9]
+        mid, stacked, d_qv_bias0, sends, _ = attention_back(0, mid_low0)
+        got = scatter_x(sends)
+        narrow = (narrow_rows(d_qv_bias0, d_up_bias0), narrow_rows(d_qv_bias1, d_up_bias1))
+        extra = []
+        for g in range(2):
+            rows = [zeros] * (6 * layers) + [part[g] for part in narrow]
             rows = jnp.concatenate(rows + [zeros] * (4 * EXTRA - len(rows)), axis=0)
-            extra = [rows.reshape(4, EXTRA, D)]
-            for g in range(2):
-                rows = [part[g] for part in narrow]
-                rows = [zeros] * (6 * layers) + rows
-                rows = jnp.concatenate(rows + [zeros] * (4 * EXTRA - len(rows)), axis=0)
-                extra.append(rows.reshape(4, EXTRA, D))
-        if last:
-            kept_a, sent_a = call(
-                plain_weights_kernel, [shaped((4, CW, D), bf16)] * 2,
-                stacked, mixed_a, mixed_b, normed, mid, pos=pos,
-            )
-            sums["a1"] = WeightSum(kept_a, sent_a, where, False, True)
-            feeds = [sent_a]
-        else:
-            kept_a, sent_a = call(
-                attend_weights_kernel, [shaped((4, CW + EXTRA, D), bf16)] * 2,
-                stacked, mixed_a, mixed_b, normed, mid, *extra, pos=pos,
-            )
-            sums["a0"] = WeightSum(kept_a, sent_a, where, True, True)
-            feeds = [sent_a, sums["m0"].advance(sends[0]), sums["a1"].advance(sends[0])]
-        got = after(got, feeds)
-        grad_flow, low, norm_one = norm_back((layer, 0), stream_in, got, grad_mid, norm_gain)
-        if layer > 0:
-            wide[layer][0], wide[layer][2] = norm_one[0:1], norm_one[1:2]
-            chunks = gather_x(low)
-            feeds = sums["a1"].advance(low)
-            chunks = after(chunks, feeds)
-        d_down_bias = norm_one[2:3]
+            extra.append(rows.reshape(4, EXTRA, D))
+        kept_a, sent_a = call(
+            attend_weights_kernel, [shaped((4, CW + EXTRA, D), bf16)] * 2,
+            stacked, mixed_a, mixed_b, normed, mid, *extra, pos=pos,
+        )
+        total = WeightSum(kept_a, sent_a, y)
+        total.advance()
+        grad_flow, low, norm_one = norm_back((0, 0), stream_in, got, grad_mid0, norm_gain)
+        return low, norm_one, total.pending
+
+    low, norm_one0, pending = apart(second_block)
+    wide = [
+        [one[0:1], two[0:1], one[1:2], two[1:2], two[2:3], down]
+        for one, two, down in (
+            (norm_one0, norm_two0, norm_one1[2:3]),
+            (norm_one1, norm_two1, d_down_bias),
+        )
+    ]
+    sums = {"a0": WeightSum.__new__(WeightSum)}
+    sums["a0"].y, sums["a0"].pending, sums["a0"].step = y[None], pending, 1
 
     in_far = shift(low, "zl", 1)
-    late = jnp.zeros((4 * EXTRA, D), f32)
-    late = late.at[0].set(norm_one[0]).at[2].set(norm_one[1]).reshape(4, EXTRA, D)
-    late = jnp.pad(late, ((0, 0), (CW, 0), (0, 0)))
-    sums["a0"].advance(low, late)
-    sums["m0"].advance(low)
-    in_slots = gather_x(low) + gather_x(in_far)
-    outputs = placed_rows(pos, out_slots, bf16)
-    sum_m1 = (sum_m1, shift(after(sum_m1, low), "c", 1))
-    sum_m0 = sums["m0"].finish()
-    sum_a0 = sums["a0"].finish()
-    sum_a1 = sums["a1"].finish()
-    d_qkv, d_out, wide_sum, narrow_sum = attend_final(pos, (sum_a0, sum_a1))
-    wide_sum = total_of((wide_sum, shift(wide_sum, "zl", 1)))
-    wide_sum = sum(part.astype(f32) for part in gather_x(wide_sum)).reshape(4 * EXTRA, D)
-    input_grad = placed_rows(pos, in_slots, f32)
+    late = jnp.concatenate([row for part in wide for row in part], axis=0)
+    late = sum_ring(sum_ring(late + shift(late, "c", 1), "x"), "y")
+    out_slots = gather_x(after(jnp.stack([result, out_far]), low))
+    late = jnp.concatenate([late, jnp.zeros((4 * EXTRA - 6 * layers, D), f32)], axis=0)
+    late = lax.dynamic_slice_in_dim(late, y * EXTRA, EXTRA, axis=0)
+    late = jnp.pad(late, ((CW, 0), (0, 0)))
+    feed = sums["a0"].advance(in_far, late)
+    in_slots = gather_x(after(jnp.stack([low, in_far]), feed))
+    outputs = placed_rows(pos, [part[i] for i in range(2) for part in out_slots], bf16)
+    sums["a0"].advance((in_slots, outputs))
+    sum_m1, sum_m0 = ((part, shift(part, "c", 1)) for part in (sum_m1, sum_m0))
+    sum_a1 = (sum_a1, shift(sum_a1, "c", 1))
+    input_grad = placed_rows(pos, [part[i] for i in range(2) for part in in_slots], f32)
     d_up, d_down = mlp_final(pos, (sum_m0, sum_m1))
-    wide_sum = wide_sum[: 6 * layers].reshape(layers, 6, D)
-    narrow_sum = narrow_sum.reshape(4 * EXTRA, D)[6 * layers : 7 * layers]
+    sums["a0"].advance((input_grad, d_up))
+    sum_a0 = sums["a0"].pending
+    d_qkv, d_out, small = attend_final(pos, (sum_a0, sum_a1))
+    small = small.reshape(4 * EXTRA, D)
+    wide_sum = small[: 6 * layers].reshape(layers, 6, D)
+    narrow_sum = small[6 * layers : 7 * layers]
     return (
         outputs,
         input_grad,

time: 762 us -> 545 us (0.72)
  the two profiles are of different devices: /device:TPU:38 before, /device:TPU:9 now
where the time goes in v2:
time: 545 us; the launch traced here: 534 us
  waiting for transfers between devices  232 us (43%)
  starting transfers between devices  122 us (22%)
  Pallas kernels  120 us (22%)
  local copies, waits for them, and re-layouts  42.3 us (8%)
  between operations  16 us (3%)
    ppermute x99, waiting for transfers between devices, shift(): return lax.ppermute(value, axis, [(i, (i + by) % n) for i in range(n)])  232 us
    pallas_call x40, Pallas kernels, call(): pl.pallas_call(kernel, out_shape=outs, in_specs=specs, out_specs=[pl.Bloc...  120 us
    ppermute x99, starting transfers between devices, shift(): return lax.ppermute(value, axis, [(i, (i + by) % n) for i in range(n)])  119 us
  transfers between devices with their start and end apart: 104, of which 53 were waited for; matrix products, arithmetic and copies ran while one was open for 5% of the time, Pallas kernels for 16%

profile of v2, /device:TPU:9, one launch (start us, length us, event | category | flops | bytes accessed | tf_op | source)
XLA Modules:
  0.0 534.5 jit_solution(9014738763119563460)
XLA Ops:
  28.4 3.3 shard_map.238
  53.8 3.0 collective-permute-done.42.r1
  56.8 5.6 %collective-permute-done.43.r2 = bf16[96,1152]{1,0:T(8,128)(2,1)S(1)} collective-permute-done((bf16[96,1152]{1,0:T(8,128)(2,1)S(1)}, bf16[96,1152]{1,0:T(8,128)(2,1)S(1)}, u32[]{:S(2)}, u32[]{:S(2)}) %collective-permute-start.43) | collective-permute-done | bytes 221216 | tf_op jit(solution)/shard_map/ppermute | solution.py:34
  70.0 5.3 collective-permute-start.58
  76.2 5.9 %collective-permute-done.47.c3 = bf16[96,1152]{1,0:T(8,128)(2,1)S(1)} collective-permute-done((bf16[96,1152]{1,0:T(8,128)(2,1)S(1)}, bf16[96,1152]{1,0:T(8,128)(2,1)S(1)}, u32[]{:S(2)}, u32[]{:S(2)}) %collective-permute-start.47) | collective-permute-done | bytes 221216 | tf_op jit(solution)/shard_map/ppermute | solution.py:34
  82.7 5.4 %shard_map.243 = (bf16[384,1152]{1,0:T(8,128)(2,1)}, f32[2,384,576]{2,1,0:T(8,128)}, bf16[2,384,576]{2,1,0:T(8,128)(2,1)}, bf16[96,1152]{1,0:T(8,128)(2,1)S(1)},...) custom-call(bf16[96,1152]{1,0:T(8,128)(2,1)S(1)} %get-tuple-element.428.c0, ...), custom_call_target="tpu_custom_call" | custom-call | tf_op jit(solution)/shard_map/pallas_call | solution.py:66
  89.1 4.3 collective-permute-done.58.refs_5_
  96.6 5.7 %collective-permute-done.53.r2 = bf16[96,1152]{1,0:T(8,128)(2,1)S(1)} collective-permute-done((bf16[96,1152]{1,0:T(8,128)(2,1)S(1)}, bf16[96,1152]{1,0:T(8,128)(2,1)S(1)}, u32[]{:S(2)}, u32[]{:S(2)}) %collective-permute-start.53) | collective-permute-done | bytes 221216 | tf_op jit(solution)/shard_map/ppermute | solution.py:34
  105.2 3.6 collective-permute-start.55
  108.9 7.6 %collective-permute-done.62.refs_6_.refs_8_ = bf16[144,1152]{1,0:T(8,128)(2,1)S(1)} collective-permute-done((bf16[144,1152]{1,0:T(8,128)(2,1)S(1)}, bf16[144,1152]{1,0:T(8,128)(2,1)S(1)}, u32[]{:S(2)}, u32[]{:S(2)}) %collective-permute-start.62) | collective-permute-done | bytes 331808 | tf_op jit(solution)/shard_map/ppermute | solution.py:34
  117.6 4.8 collective-permute-done.57.refs_3_
  125.0 3.8 collective-permute-start.63
  128.8 5.4 %collective-permute-done.64.refs_3_ = bf16[2,2,144,128]{3,2,1,0:T(8,128)(2,1)S(1)} collective-permute-done((bf16[2,2,144,128]{3,2,1,0:T(8,128)(2,1)S(1)}, bf16[2,2,144,128]{3,2,1,0:T(8,128)(2,1)S(1)}, u32[]{:S(2)}, u32[]{:S(2)}) %collective-permute-start.64) | collective-permute-done | bytes 147488 | tf_op jit(solution)/shard_map/ppermute | solution.py:34
  146.9 8.9 %collective-permute-done.66.r1 = bf16[96,1152]{1,0:T(8,128)(2,1)S(1)} collective-permute-done((bf16[96,1152]{1,0:T(8,128)(2,1)S(1)}, bf16[96,1152]{1,0:T(8,128)(2,1)S(1)}, u32[]{:S(2)}, u32[]{:S(2)}) %collective-permute-start.66) | collective-permute-done | bytes 221216 | tf_op jit(solution)/shard_map/ppermute | solution.py:34
  163.0 5.7 %collective-permute-done.69.c1 = bf16[96,1152]{1,0:T(8,128)(2,1)S(1)} collective-permute-done((bf16[96,1152]{1,0:T(8,128)(2,1)S(1)}, bf16[96,1152]{1,0:T(8,128)(2,1)S(1)}, u32[]{:S(2)}, u32[]{:S(2)}) %collective-permute-start.69) | collective-permute-done | bytes 221216 | tf_op jit(solution)/shard_map/ppermute | solution.py:34
  168.7 4.6 collective-permute-done.71.c3
  173.3 6.0 %shard_map.250 = (bf16[384,1152]{1,0:T(8,128)(2,1)}, f32[2,384,576]{2,1,0:T(8,128)}, bf16[2,384,576]{2,1,0:T(8,128)(2,1)}, bf16[96,1152]{1,0:T(8,128)(2,1)}, bf1...) custom-call(bf16[96,1152]{1,0:T(8,128)(2,1)S(1)} %get-tuple-element.461.c0, ...), custom_call_target="tpu_custom_call" | custom-call | tf_op jit(solution)/shard_map/pallas_call | solution.py:66
  179.3 6.4 %shard_map.251 = (bf16[2,384,576]{2,1,0:T(8,128)(2,1)}, f32[2,1,576]{2,1,0:T(1,128)}, bf16[96,1152]{1,0:T(8,128)(2,1)S(1)}, bf16[96,1152]{1,0:T(8,128)(2,1)S(1)}...) custom-call(bf16[384,1152]{1,0:T(8,128)(2,1)} %copy-done.1, f32[2,384,576]{2,1,0:T(8,128)} %get-tuple-element.464.refs_1_, ...), custom_call_target="tpu_custom_call" | custom-call | tf_op jit(solution)/shard_map/pallas_call | solution.py:66
  186.9 5.8 %shard_map.252 = (bf16[4,288,1152]{2,1,0:T(8,128)(2,1)}, bf16[4,288,1152]{2,1,0:T(8,128)(2,1)}) custom-call(s32[3]{0:T(128)S(1)} %pad_add_fusion.pos, bf16[2,384,576]{2,1,0:T(8,128)(2,1)S(1)} %copy-done.9, bf16[2,384,576]{2,1,0:T(8,128)(2,1)S(1)} %copy-done.8, bf16[384,1152]{1,0:T(8,128)(2,1)S(1)} %copy-done.10, bf16[384,1152]{1,0:T(8,128)(2,1)S(1)} %copy-done.2), custom_call_target="tpu_custom_call" | custom-call | tf_op jit(solution)/shard_map/pallas_call | solution.py:66
  193.3 4.8 collective-permute-done.97.refs_1_
  199.6 4.7 shard_map.258
  208.2 8.9 %collective-permute-done.74.r1 = bf16[96,1152]{1,0:T(8,128)(2,1)S(1)} collective-permute-done((bf16[96,1152]{1,0:T(8,128)(2,1)S(1)}, bf16[96,1152]{1,0:T(8,128)(2,1)S(1)}, u32[]{:S(2)}, u32[]{:S(2)}) %collective-permute-start.74) | collective-permute-done | bytes 221216 | tf_op jit(solution)/shard_map/ppermute | solution.py:34
  219.7 114.7 %conditional.2 = (f32[2,2,144,1]{3,2,1,0:T(8,128)}, f32[3,1152]{1,0:T(4,128)}, bf16[4,144,1152]{2,1,0:T(8,128)(2,1)}, f32[96,1152]{1,0:T(8,128)}, bf16[96,1152]{...) conditional(s32[]{:T(128)} %bitcast.12, () %tuple.61, ...), branch_computations={%region_0.1_spmd, %region_1.2_spmd} | conditional | flops 221184 | bytes 97635808 | solution.py:750
  219.8 3.0 collective-permute-start
  223.4 5.1 collective-permute-done.c1
  230.3 5.5 %collective-permute-done.2.c3 = bf16[96,1152]{1,0:T(8,128)(2,1)S(1)} collective-permute-done((bf16[96,1152]{1,0:T(8,128)(2,1)S(1)}, bf16[96,1152]{1,0:T(8,128)(2,1)S(1)}, u32[]{:S(2)}, u32[]{:S(2)}) %collective-permute-start.2) | collective-permute-done | bytes 221216 | tf_op jit(solution)/shard_map/cond/branch_1_fun/ppermute | solution.py:34
  235.8 7.5 %branch_1_fun.15 = (bf16[384,1152]{1,0:T(8,128)(2,1)S(1)}, bf16[2,144,384]{2,1,0:T(8,128)(2,1)S(1)}, f32[2,2,144,384]{3,2,1,0:T(8,128)S(1)}, bf16[2,2,144,512]{3,2,1,0:T(8,128)(2,1)S(1)}, f32[2,2,144,128]{3,2,1,0:T(8,128)S(1)}) custom-call(bf16[96,1152]{1,0:T(8,128)(2,1)S(1)} %get-tuple-element.137.c0, bf16[96,1152]{1,0:T(8,128)(2,1)S(1)} %collective-permute-done.c1, ...), custom_call_target="tpu_custom_call" | custom-call | tf_op jit(solution)/shard_map/cond/branch_1_fun/pallas_call | solution.py:66
  247.1 10.0 %collective-permute-done.5.r1 = bf16[96,1152]{1,0:T(8,128)(2,1)S(1)} collective-permute-done((bf16[96,1152]{1,0:T(8,128)(2,1)S(1)}, bf16[96,1152]{1,0:T(8,128)(2,1)S(1)}, u32[]{:S(2)}, u32[]{:S(2)}) %collective-permute-start.5) | collective-permute-done | bytes 221216 | tf_op jit(solution)/shard_map/cond/branch_1_fun/ppermute | solution.py:34
  261.6 3.1 collective-permute-start.9
  264.7 3.4 collective-permute-done.8.r1
  268.1 6.2 %collective-permute-done.9.r2 = bf16[96,1152]{1,0:T(8,128)(2,1)S(1)} collective-permute-done((bf16[96,1152]{1,0:T(8,128)(2,1)S(1)}, bf16[96,1152]{1,0:T(8,128)(2,1)S(1)}, u32[]{:S(2)}, u32[]{:S(2)}) %collective-permute-start.9) | collective-permute-done | bytes 221216 | tf_op jit(solution)/shard_map/cond/branch_1_fun/ppermute | solution.py:34
  275.7 3.1 collective-permute-start.12
  280.0 7.9 %collective-permute-done.12.refs_1_ = bf16[96,1152]{1,0:T(8,128)(2,1)S(1)} collective-permute-done((bf16[96,1152]{1,0:T(8,128)(2,1)S(1)}, bf16[96,1152]{1,0:T(8,128)(2,1)S(1)}, u32[]{:S(2)}, u32[]{:S(2)}) %collective-permute-start.12) | collective-permute-done | bytes 221216 | tf_op jit(solution)/shard_map/cond/branch_1_fun/ppermute | solution.py:34
  287.9 4.7 collective-permute-done.14.refs_3_
  292.6 5.1 branch_1_fun.21
  297.8 5.8 %branch_1_fun.22 = (bf16[4,288,1152]{2,1,0:T(8,128)(2,1)}, bf16[4,288,1152]{2,1,0:T(8,128)(2,1)}) custom-call(s32[3]{0:T(128)S(1)} %get-tuple-element.176.pos, bf16[2,384,576]{2,1,0:T(8,128)(2,1)S(1)} %get-tuple-element.197.d_up, bf16[2,384,576]{2,1,0:T(8,128)(2,1)S(1)} %copy-done.69, bf16[384,1152]{1,0:T(8,128)(2,1)S(1)} %copy-done.72, ...), custom_call_target="tpu_custom_call" | custom-call | tf_op jit(solution)/shard_map/cond/branch_1_fun/pallas_call | solution.py:66
  304.0 3.3 branch_1_fun.19
  308.9 11.1 %collective-permute-done.15.r1 = bf16[96,1152]{1,0:T(8,128)(2,1)S(1)} collective-permute-done((bf16[96,1152]{1,0:T(8,128)(2,1)S(1)}, bf16[96,1152]{1,0:T(8,128)(2,1)S(1)}, u32[]{:S(2)}, u32[]{:S(2)}) %collective-permute-start.15) | collective-permute-done | bytes 221216 | tf_op jit(solution)/shard_map/cond/branch_1_fun/ppermute | solution.py:34
  320.6 5.1 collective-permute-done.17.r3
  330.5 3.9 branch_1_fun.24
  336.3 81.3 %conditional.3 = (bf16[96,1152]{1,0:T(8,128)(2,1)}, f32[3,1152]{1,0:T(4,128)}, bf16[152,1152]{1,0:T(8,128)(2,1)}, bf16[152,1152]{1,0:T(8,128)(2,1)}, bf16[152,11...) conditional(s32[]{:T(128)} %bitcast.12, () %tuple.80, ...), branch_computations={%region_2.3_spmd, %region_3.4_spmd} | conditional | flops 442368 | bytes 31895008 | solution.py:750
  341.3 3.0 collective-permute-done.21.c2
  344.3 6.7 %collective-permute-done.22.c3 = bf16[96,1152]{1,0:T(8,128)(2,1)S(1)} collective-permute-done((bf16[96,1152]{1,0:T(8,128)(2,1)S(1)}, bf16[96,1152]{1,0:T(8,128)(2,1)S(1)}, u32[]{:S(2)}, u32[]{:S(2)}) %collective-permute-start.22) | collective-permute-done | bytes 221216 | tf_op jit(solution)/shard_map/cond/branch_1_fun/ppermute | solution.py:34
  351.0 7.7 %branch_1_fun.25 = (bf16[384,1152]{1,0:T(8,128)(2,1)S(1)}, bf16[2,144,384]{2,1,0:T(8,128)(2,1)S(1)}, f32[2,2,144,384]{3,2,1,0:T(8,128)S(1)}, bf16[2,2,144,512]{3,2,1,0:T(8,128)(2,1)S(1)}, f32[2,2,144,128]{3,2,1,0:T(8,128)S(1)}) custom-call(bf16[96,1152]{1,0:T(8,128)(2,1)} %copy-done.70, bf16[96,1152]{1,0:T(8,128)(2,1)S(1)} %collective-permute-done.20.c1, ...), custom_call_target="tpu_custom_call" | custom-call | tf_op jit(solution)/shard_map/cond/branch_1_fun/pallas_call | solution.py:66
  362.1 4.8 collective-permute-done.24.dz
  369.4 3.4 branch_1_fun.26
  375.5 4.2 branch_1_fun.28
  383.6 10.3 %collective-permute-done.25.r1 = bf16[96,1152]{1,0:T(8,128)(2,1)S(1)} collective-permute-done((bf16[96,1152]{1,0:T(8,128)(2,1)S(1)}, bf16[96,1152]{1,0:T(8,128)(2,1)S(1)}, u32[]{:S(2)}, u32[]{:S(2)}) %collective-permute-start.25) | collective-permute-done | bytes 221216 | tf_op jit(solution)/shard_map/cond/branch_1_fun/ppermute | solution.py:34
  401.4 6.4 %collective-permute-done.29 = bf16[152,1152]{1,0:T(8,128)(2,1)} collective-permute-done((bf16[152,1152]{1,0:T(8,128)(2,1)S(1)}, bf16[152,1152]{1,0:T(8,128)(2,1)}, u32[]{:S(2)}, u32[]{:S(2)}) %collective-permute-start.29) | collective-permute-done | bytes 350240 | tf_op jit(solution)/shard_map/cond/branch_1_fun/ppermute | solution.py:34
  410.2 7.2 %collective-permute-done.31 = bf16[152,1152]{1,0:T(8,128)(2,1)} collective-permute-done((bf16[152,1152]{1,0:T(8,128)(2,1)S(1)}, bf16[152,1152]{1,0:T(8,128)(2,1)}, u32[]{:S(2)}, u32[]{:S(2)}) %collective-permute-start.31) | collective-permute-done | bytes 350240 | tf_op jit(solution)/shard_map/cond/branch_1_fun/ppermute | solution.py:34
  426.8 4.3 collective-permute-done.82
  432.7 3.0 collective-permute-start.86
  437.6 3.1 collective-permute-done.86
  440.8 6.4 %collective-permute-done.80 = bf16[96,1152]{1,0:T(8,128)(2,1)S(1)} collective-permute-done((bf16[96,1152]{1,0:T(8,128)(2,1)}, bf16[96,1152]{1,0:T(8,128)(2,1)S(1)}, u32[]{:S(2)}, u32[]{:S(2)}) %collective-permute-start.80) | collective-permute-done | bytes 221216 | tf_op jit(solution)/shard_map/ppermute | solution.py:34
  452.9 3.2 collective-permute-start.92
  456.2 3.4 collective-permute-done.79
  460.7 4.3 collective-permute-done.92.refs_2_
  465.0 3.6 collective-permute-start.89
  468.7 3.2 collective-permute-done.93.refs_3_
  475.9 13.8 %collective-permute-done.90 = bf16[2,96,1152]{2,1,0:T(8,128)(2,1)S(1)} collective-permute-done((bf16[2,96,1152]{2,1,0:T(8,128)(2,1)S(1)}, bf16[2,96,1152]{2,1,0:T(8,128)(2,1)S(1)}, u32[]{:S(2)}, u32[]{:S(2)}) %collective-permute-start.90) | collective-permute-done | bytes 442400 | tf_op jit(solution)/shard_map/ppermute | solution.py:34
  496.2 9.2 %shard_map.259 = (f32[538,2,1152]{2,1,0:T(2,128)}, f32[538,2,1152]{2,1,0:T(2,128)}) custom-call(s32[3]{0:T(128)S(1)} %copy-done.87, bf16[4,288,1152]{2,1,0:T(8,128)(2,1)S(1)} %copy-done.3, bf16[4,288,1152]{2,1,0:T(8,128)(2,1)} %copy-done.44, bf16[4,288,1152]{2,1,0:T(8,128)(2,1)} %all-reduce.11.cloned.1.call-done.full1, ...), custom_call_target="tpu_custom_call" | custom-call | tf_op jit(solution)/shard_map/pallas_call | solution.py:66
  505.6 8.8 %collective-permute-start.100 = (bf16[4,152,1152]{2,1,0:T(8,128)(2,1)S(1)}, bf16[4,152,1152]{2,1,0:T(8,128)(2,1)S(1)}, u32[]{:S(2)}, u32[]{:S(2)}) collective-permute-start(bf16[4,152,1152]{2,1,0:T(8,128)(2,1)S(1)} %shard_map.260.full0), channel_id=1, source_target_pairs={{0,8},{8,0},{1,9},{9,1},{2,10},{10,2},{3,11},{11,3},{4,12},{12,4},... | collective-permute-start | bytes 4202504 | tf_op jit(solution)/shard_map/ppermute | solution.py:34
  516.0 3.1 collective-permute-done.101.other1
  520.2 4.5 shard_map.261
  (461 shorter events, 176.9 us)
Async XLA Ops:
  7.2 327.4 %all-reduce.11.cloned.1.call-start = ((), (), s32[]{:S(2)}) async-start(), calls=%async_computation | async-start | bytes 5308416 | tf_op jit(solution)/shard_map/psum | solution.py:805
  7.9 15.7 %collective-permute-start.32 = (f32[2,576]{1,0:T(2,128)S(1)}, f32[2,576]{1,0:T(2,128)S(1)}, u32[]{:S(2)}, u32[]{:S(2)}) collective-permute-start(f32[2,576]{1,0:T(2,128)S(1)} %pad.22.ub0), channel_id=1, source_target_pairs={{0,4},{4,0},{1,5},{5,1},{2,6},{6,2},{3,7},{7,3},{8,12},{12,8},{9,1... | collective-permute-start | bytes 13832 | tf_op jit(solution)/shard_map/ppermute | solution.py:34
  14.5 13.8 %collective-permute-start.33 = (bf16[216,1152]{1,0:T(8,128)(2,1)}, bf16[216,1152]{1,0:T(8,128)(2,1)}, u32[]{:S(2)}, u32[]{:S(2)}) collective-permute-start(bf16[216,1152]{1,0:T(8,128)(2,1)} %get-tuple-element.636), channel_id=1, source_target_pairs={{0,4},{4,16},{16,20},{20,0},{1,5},{5,17},{17,21},{21,1},{2,6},{6,1... | collective-permute-start | bytes 1493000 | tf_op jit(solution)/shard_map/ppermute | solution.py:34
  14.5 13.8 %collective-permute-start.34 = (bf16[216,1152]{1,0:T(8,128)(2,1)}, bf16[216,1152]{1,0:T(8,128)(2,1)}, u32[]{:S(2)}, u32[]{:S(2)}) collective-permute-start(bf16[216,1152]{1,0:T(8,128)(2,1)} %get-tuple-element.635), channel_id=1, source_target_pairs={{0,20},{4,0},{16,4},{20,16},{1,21},{5,1},{17,5},{21,17},{2,22},{6,... | collective-permute-start | bytes 1493000 | tf_op jit(solution)/shard_map/ppermute | solution.py:34
  23.6 17.0 %collective-permute-start.40 = (s32[3,256]{1,0:T(4,128)S(1)}, s32[3,256]{1,0:T(4,128)S(1)}, u32[]{:S(2)}, u32[]{:S(2)}) collective-permute-start(s32[3,256]{1,0:T(4,128)S(1)} %copy-done.19), channel_id=1, source_target_pairs={{0,8},{8,0},{1,9},{9,1},{2,10},{10,2},{3,11},{11,3},{4,12},{12,4},... | collective-permute-start | bytes 9224 | tf_op jit(solution)/shard_map/ppermute | solution.py:34
  28.3 13.1 %collective-permute-start.41 = (bf16[144,1152]{1,0:T(8,128)(2,1)S(1)}, bf16[144,1152]{1,0:T(8,128)(2,1)S(1)}, u32[]{:S(2)}, u32[]{:S(2)}) collective-permute-start(bf16[144,1152]{1,0:T(8,128)(2,1)S(1)} %get-tuple-element.638.refs_5_.refs_7_), channel_id=1, source_target_pairs={{0,4},{4,16},{16,20},{20,0},{1,5},{5,17},{17,21},{21,1},{2,6},{6,1... | collective-permute-start | bytes 995336 | tf_op jit(solution)/shard_map/ppermute | solution.py:34
  41.4 24.3 %collective-permute-start.48 = (bf16[288,1152]{1,0:T(8,128)(2,1)}, bf16[288,1152]{1,0:T(8,128)(2,1)}, u32[]{:S(2)}, u32[]{:S(2)}) collective-permute-start(bf16[288,1152]{1,0:T(8,128)(2,1)} %get-tuple-element.423), channel_id=1, source_target_pairs={{0,4},{4,16},{16,20},{20,0},{1,5},{5,17},{17,21},{21,1},{2,6},{6,1... | collective-permute-start | bytes 1990664 | tf_op jit(solution)/shard_map/ppermute | solution.py:34
  43.7 22.0 %collective-permute-start.49 = (bf16[288,1152]{1,0:T(8,128)(2,1)}, bf16[288,1152]{1,0:T(8,128)(2,1)}, u32[]{:S(2)}, u32[]{:S(2)}) collective-permute-start(bf16[288,1152]{1,0:T(8,128)(2,1)} %get-tuple-element.425), channel_id=1, source_target_pairs={{0,20},{4,0},{16,4},{20,16},{1,21},{5,1},{17,5},{21,17},{2,22},{6,... | collective-permute-start | bytes 1990664 | tf_op jit(solution)/shard_map/ppermute | solution.py:34
  50.0 12.4 %collective-permute-start.43 = (bf16[96,1152]{1,0:T(8,128)(2,1)S(1)}, bf16[96,1152]{1,0:T(8,128)(2,1)S(1)}, u32[]{:S(2)}, u32[]{:S(2)}) collective-permute-start(bf16[96,1152]{1,0:T(8,128)(2,1)S(1)} %get-tuple-element.418), channel_id=1, source_target_pairs={{0,2},{1,3},{2,0},{3,1},{4,6},{5,7},{6,4},{7,5},{8,10},{9,11},{10,... | collective-permute-start | bytes 663560 | tf_op jit(solution)/shard_map/ppermute | solution.py:34
  65.7 16.9 %collective-permute-start.50 = (bf16[288,1152]{1,0:T(8,128)(2,1)S(1)}, bf16[288,1152]{1,0:T(8,128)(2,1)S(1)}, u32[]{:S(2)}, u32[]{:S(2)}) collective-permute-start(bf16[288,1152]{1,0:T(8,128)(2,1)S(1)} %copy-done.76), channel_id=1, source_target_pairs={{0,4},{4,16},{16,20},{20,0},{1,5},{5,17},{17,21},{21,1},{2,6},{6,1... | collective-permute-start | bytes 1990664 | tf_op jit(solution)/shard_map/ppermute | solution.py:34
  66.5 16.2 %collective-permute-start.51 = (bf16[288,1152]{1,0:T(8,128)(2,1)S(1)}, bf16[288,1152]{1,0:T(8,128)(2,1)S(1)}, u32[]{:S(2)}, u32[]{:S(2)}) collective-permute-start(bf16[288,1152]{1,0:T(8,128)(2,1)S(1)} %pad_slice_fusion.2), channel_id=1, source_target_pairs={{0,20},{4,0},{16,4},{20,16},{1,21},{5,1},{17,5},{21,17},{2,22},{6,... | collective-permute-start | bytes 1990664 | tf_op jit(solution)/shard_map/ppermute | solution.py:34
  68.9 13.2 %collective-permute-start.47 = (bf16[96,1152]{1,0:T(8,128)(2,1)S(1)}, bf16[96,1152]{1,0:T(8,128)(2,1)S(1)}, u32[]{:S(2)}, u32[]{:S(2)}) collective-permute-start(bf16[96,1152]{1,0:T(8,128)(2,1)S(1)} %get-tuple-element.428.c0), channel_id=1, source_target_pairs={{0,1},{1,2},{2,3},{3,0},{4,5},{5,6},{6,7},{7,4},{8,9},{9,10},{10,1... | collective-permute-start | bytes 663560 | tf_op jit(solution)/shard_map/ppermute | solution.py:34
  70.0 23.3 %collective-permute-start.58 = (bf16[216,1152]{1,0:T(8,128)(2,1)S(1)}, bf16[216,1152]{1,0:T(8,128)(2,1)S(1)}, u32[]{:S(2)}, u32[]{:S(2)}) collective-permute-start(bf16[216,1152]{1,0:T(8,128)(2,1)S(1)} %get-tuple-element.634), channel_id=1, source_target_pairs={{0,4},{4,16},{16,20},{20,0},{1,5},{5,17},{17,21},{21,1},{2,6},{6,1... | collective-permute-start | bytes 1493000 | tf_op jit(solution)/shard_map/ppermute | solution.py:34
  76.0 17.4 %collective-permute-start.59 = (bf16[216,1152]{1,0:T(8,128)(2,1)S(1)}, bf16[216,1152]{1,0:T(8,128)(2,1)S(1)}, u32[]{:S(2)}, u32[]{:S(2)}) collective-permute-start(bf16[216,1152]{1,0:T(8,128)(2,1)S(1)} %get-tuple-element.633), channel_id=1, source_target_pairs={{0,20},{4,0},{16,4},{20,16},{1,21},{5,1},{17,5},{21,17},{2,22},{6,... | collective-permute-start | bytes 1493000 | tf_op jit(solution)/shard_map/ppermute | solution.py:34
  93.3 29.1 %collective-permute-start.60 = (bf16[288,1152]{1,0:T(8,128)(2,1)S(1)}, bf16[288,1152]{1,0:T(8,128)(2,1)S(1)}, u32[]{:S(2)}, u32[]{:S(2)}) collective-permute-start(bf16[288,1152]{1,0:T(8,128)(2,1)S(1)} %get-tuple-element.439), channel_id=1, source_target_pairs={{0,4},{4,16},{16,20},{20,0},{1,5},{5,17},{17,21},{21,1},{2,6},{6,1... | collective-permute-start | bytes 1990664 | tf_op jit(solution)/shard_map/ppermute | solution.py:34
  93.4 29.0 %collective-permute-start.61 = (bf16[288,1152]{1,0:T(8,128)(2,1)S(1)}, bf16[288,1152]{1,0:T(8,128)(2,1)S(1)}, u32[]{:S(2)}, u32[]{:S(2)}) collective-permute-start(bf16[288,1152]{1,0:T(8,128)(2,1)S(1)} %copy-done.74), channel_id=1, source_target_pairs={{0,20},{4,0},{16,4},{20,16},{1,21},{5,1},{17,5},{21,17},{2,22},{6,... | collective-permute-start | bytes 1990664 | tf_op jit(solution)/shard_map/ppermute | solution.py:34
  96.1 20.4 %collective-permute-start.62 = (bf16[144,1152]{1,0:T(8,128)(2,1)S(1)}, bf16[144,1152]{1,0:T(8,128)(2,1)S(1)}, u32[]{:S(2)}, u32[]{:S(2)}) collective-permute-start(bf16[144,1152]{1,0:T(8,128)(2,1)S(1)} %get-tuple-element.441.refs_5_.refs_7_), channel_id=1, source_target_pairs={{0,4},{4,16},{16,20},{20,0},{1,5},{5,17},{17,21},{21,1},{2,6},{6,1... | collective-permute-start | bytes 995336 | tf_op jit(solution)/shard_map/ppermute | solution.py:34
  105.2 12.4 %collective-permute-start.55 = (bf16[96,1152]{1,0:T(8,128)(2,1)S(1)}, bf16[96,1152]{1,0:T(8,128)(2,1)S(1)}, u32[]{:S(2)}, u32[]{:S(2)}) collective-permute-start(bf16[96,1152]{1,0:T(8,128)(2,1)S(1)} %get-tuple-element.442.refs_0_), channel_id=1, source_target_pairs={{0,3},{1,0},{2,1},{3,2},{4,7},{5,4},{6,5},{7,6},{8,11},{9,8},{10,9... | collective-permute-start | bytes 663560 | tf_op jit(solution)/shard_map/ppermute | solution.py:34
  125.0 11.4 %collective-permute-start.63 = (bf16[2,2,144,384]{3,2,1,0:T(8,128)(2,1)S(1)}, bf16[2,2,144,384]{3,2,1,0:T(8,128)(2,1)S(1)}, u32[]{:S(2)}, u32[]{:S(2)}) collective-permute-start(bf16[2,2,144,384]{3,2,1,0:T(8,128)(2,1)S(1)} %get-tuple-element.447.refs_1_), channel_id=1, source_target_pairs={{0,8},{8,0},{1,9},{9,1},{2,10},{10,2},{3,11},{11,3},{4,12},{12,4},... | collective-permute-start | bytes 1327112 | tf_op jit(solution)/shard_map/ppermute | solution.py:34
  140.6 32.7 %collective-permute-start.72 = (bf16[288,1152]{1,0:T(8,128)(2,1)S(1)}, bf16[288,1152]{1,0:T(8,128)(2,1)S(1)}, u32[]{:S(2)}, u32[]{:S(2)}) collective-permute-start(bf16[288,1152]{1,0:T(8,128)(2,1)S(1)} %copy-done.75), channel_id=1, source_target_pairs={{0,4},{4,16},{16,20},{20,0},{1,5},{5,17},{17,21},{21,1},{2,6},{6,1... | collective-permute-start | bytes 1990664 | tf_op jit(solution)/shard_map/ppermute | solution.py:34
  140.7 32.6 %collective-permute-start.73 = (bf16[288,1152]{1,0:T(8,128)(2,1)}, bf16[288,1152]{1,0:T(8,128)(2,1)S(1)}, u32[]{:S(2)}, u32[]{:S(2)}) collective-permute-start(bf16[288,1152]{1,0:T(8,128)(2,1)} %pad_slice_fusion), channel_id=1, source_target_pairs={{0,20},{4,0},{16,4},{20,16},{1,21},{5,1},{17,5},{21,17},{2,22},{6,... | collective-permute-start | bytes 1990664 | tf_op jit(solution)/shard_map/ppermute | solution.py:34
  143.4 12.4 %collective-permute-start.66 = (bf16[96,1152]{1,0:T(8,128)(2,1)S(1)}, bf16[96,1152]{1,0:T(8,128)(2,1)S(1)}, u32[]{:S(2)}, u32[]{:S(2)}) collective-permute-start(bf16[96,1152]{1,0:T(8,128)(2,1)S(1)} %get-tuple-element.451), channel_id=1, source_target_pairs={{0,1},{1,2},{2,3},{3,0},{4,5},{5,6},{6,7},{7,4},{8,9},{9,10},{10,1... | collective-permute-start | bytes 663560 | tf_op jit(solution)/shard_map/ppermute | solution.py:34
  143.4 12.4 %collective-permute-start.67 = (bf16[96,1152]{1,0:T(8,128)(2,1)S(1)}, bf16[96,1152]{1,0:T(8,128)(2,1)S(1)}, u32[]{:S(2)}, u32[]{:S(2)}) collective-permute-start(bf16[96,1152]{1,0:T(8,128)(2,1)S(1)} %get-tuple-element.452), channel_id=1, source_target_pairs={{0,2},{1,3},{2,0},{3,1},{4,6},{5,7},{6,4},{7,5},{8,10},{9,11},{10,... | collective-permute-start | bytes 663560 | tf_op jit(solution)/shard_map/ppermute | solution.py:34
  143.8 12.3 %collective-permute-start.68 = (bf16[96,1152]{1,0:T(8,128)(2,1)S(1)}, bf16[96,1152]{1,0:T(8,128)(2,1)S(1)}, u32[]{:S(2)}, u32[]{:S(2)}) collective-permute-start(bf16[96,1152]{1,0:T(8,128)(2,1)S(1)} %get-tuple-element.453), channel_id=1, source_target_pairs={{0,3},{1,0},{2,1},{3,2},{4,7},{5,4},{6,5},{7,6},{8,11},{9,8},{10,9... | collective-permute-start | bytes 663560 | tf_op jit(solution)/shard_map/ppermute | solution.py:34
  157.0 11.7 %collective-permute-start.69 = (bf16[96,1152]{1,0:T(8,128)(2,1)S(1)}, bf16[96,1152]{1,0:T(8,128)(2,1)S(1)}, u32[]{:S(2)}, u32[]{:S(2)}) collective-permute-start(bf16[96,1152]{1,0:T(8,128)(2,1)S(1)} %get-tuple-element.461.c0), channel_id=1, source_target_pairs={{0,3},{1,0},{2,1},{3,2},{4,7},{5,4},{6,5},{7,6},{8,11},{9,8},{10,9... | collective-permute-start | bytes 663560 | tf_op jit(solution)/shard_map/ppermute | solution.py:34
  160.0 13.3 %collective-permute-start.71 = (bf16[96,1152]{1,0:T(8,128)(2,1)S(1)}, bf16[96,1152]{1,0:T(8,128)(2,1)S(1)}, u32[]{:S(2)}, u32[]{:S(2)}) collective-permute-start(bf16[96,1152]{1,0:T(8,128)(2,1)S(1)} %get-tuple-element.461.c0), channel_id=1, source_target_pairs={{0,1},{1,2},{2,3},{3,0},{4,5},{5,6},{6,7},{7,4},{8,9},{9,10},{10,1... | collective-permute-start | bytes 663560 | tf_op jit(solution)/shard_map/ppermute | solution.py:34
  204.3 247.5 %all-reduce.13.cloned.1.call-start = ((), (), s32[]{:S(2)}) async-start(), calls=%async_computation.1 | async-start | bytes 7962624 | tf_op jit(solution)/shard_map/psum | solution.py:825
  204.3 12.8 %collective-permute-start.74 = (bf16[96,1152]{1,0:T(8,128)(2,1)S(1)}, bf16[96,1152]{1,0:T(8,128)(2,1)S(1)}, u32[]{:S(2)}, u32[]{:S(2)}) collective-permute-start(bf16[96,1152]{1,0:T(8,128)(2,1)S(1)} %get-tuple-element.466), channel_id=1, source_target_pairs={{0,1},{1,2},{2,3},{3,0},{4,5},{5,6},{6,7},{7,4},{8,9},{9,10},{10,1... | collective-permute-start | bytes 663560 | tf_op jit(solution)/shard_map/ppermute | solution.py:34
  204.4 12.7 %collective-permute-start.75 = (bf16[96,1152]{1,0:T(8,128)(2,1)S(1)}, bf16[96,1152]{1,0:T(8,128)(2,1)S(1)}, u32[]{:S(2)}, u32[]{:S(2)}) collective-permute-start(bf16[96,1152]{1,0:T(8,128)(2,1)S(1)} %get-tuple-element.467), channel_id=1, source_target_pairs={{0,2},{1,3},{2,0},{3,1},{4,6},{5,7},{6,4},{7,5},{8,10},{9,11},{10,... | collective-permute-start | bytes 663560 | tf_op jit(solution)/shard_map/ppermute | solution.py:34
  206.0 11.4 %collective-permute-start.76 = (bf16[96,1152]{1,0:T(8,128)(2,1)S(1)}, bf16[96,1152]{1,0:T(8,128)(2,1)S(1)}, u32[]{:S(2)}, u32[]{:S(2)}) collective-permute-start(bf16[96,1152]{1,0:T(8,128)(2,1)S(1)} %get-tuple-element.468), channel_id=1, source_target_pairs={{0,3},{1,0},{2,1},{3,2},{4,7},{5,4},{6,5},{7,6},{8,11},{9,8},{10,9... | collective-permute-start | bytes 663560 | tf_op jit(solution)/shard_map/ppermute | solution.py:34
  222.8 13.0 %collective-permute-start.2 = (bf16[96,1152]{1,0:T(8,128)(2,1)S(1)}, bf16[96,1152]{1,0:T(8,128)(2,1)S(1)}, u32[]{:S(2)}, u32[]{:S(2)}) collective-permute-start(bf16[96,1152]{1,0:T(8,128)(2,1)S(1)} %get-tuple-element.137.c0), channel_id=1, source_target_pairs={{0,1},{1,2},{2,3},{3,0},{4,5},{5,6},{6,7},{7,4},{8,9},{9,10},{10,1... | collective-permute-start | bytes 663560 | tf_op jit(solution)/shard_map/cond/branch_1_fun/ppermute | solution.py:34
  244.2 12.9 %collective-permute-start.5 = (bf16[96,1152]{1,0:T(8,128)(2,1)S(1)}, bf16[96,1152]{1,0:T(8,128)(2,1)S(1)}, u32[]{:S(2)}, u32[]{:S(2)}) collective-permute-start(bf16[96,1152]{1,0:T(8,128)(2,1)S(1)} %copy-done.99), channel_id=1, source_target_pairs={{0,1},{1,2},{2,3},{3,0},{4,5},{5,6},{6,7},{7,4},{8,9},{9,10},{10,1... | collective-permute-start | bytes 663560 | tf_op jit(solution)/shard_map/cond/branch_1_fun/ppermute | solution.py:34
  244.2 12.9 %collective-permute-start.6 = (bf16[96,1152]{1,0:T(8,128)(2,1)S(1)}, bf16[96,1152]{1,0:T(8,128)(2,1)S(1)}, u32[]{:S(2)}, u32[]{:S(2)}) collective-permute-start(bf16[96,1152]{1,0:T(8,128)(2,1)S(1)} %copy-done.100), channel_id=1, source_target_pairs={{0,2},{1,3},{2,0},{3,1},{4,6},{5,7},{6,4},{7,5},{8,10},{9,11},{10,... | collective-permute-start | bytes 663560 | tf_op jit(solution)/shard_map/cond/branch_1_fun/ppermute | solution.py:34
  246.0 11.6 %collective-permute-start.7 = (bf16[96,1152]{1,0:T(8,128)(2,1)S(1)}, bf16[96,1152]{1,0:T(8,128)(2,1)S(1)}, u32[]{:S(2)}, u32[]{:S(2)}) collective-permute-start(bf16[96,1152]{1,0:T(8,128)(2,1)S(1)} %copy-done.101), channel_id=1, source_target_pairs={{0,3},{1,0},{2,1},{3,2},{4,7},{5,4},{6,5},{7,6},{8,11},{9,8},{10,9... | collective-permute-start | bytes 663560 | tf_op jit(solution)/shard_map/cond/branch_1_fun/ppermute | solution.py:34
  247.1 11.4 %collective-permute-start.4 = (bf16[2,2,144,128]{3,2,1,0:T(8,128)(2,1)S(1)}, bf16[2,2,144,128]{3,2,1,0:T(8,128)(2,1)S(1)}, u32[]{:S(2)}, u32[]{:S(2)}) collective-permute-start(bf16[2,2,144,128]{3,2,1,0:T(8,128)(2,1)S(1)} %add_convert_fusion), channel_id=1, source_target_pairs={{0,4},{4,0},{1,5},{5,1},{2,6},{6,2},{3,7},{7,3},{8,12},{12,8},{9,1... | collective-permute-start | bytes 442376 | tf_op jit(solution)/shard_map/cond/branch_1_fun/ppermute | solution.py:34
  261.6 12.7 %collective-permute-start.9 = (bf16[96,1152]{1,0:T(8,128)(2,1)S(1)}, bf16[96,1152]{1,0:T(8,128)(2,1)S(1)}, u32[]{:S(2)}, u32[]{:S(2)}) collective-permute-start(bf16[96,1152]{1,0:T(8,128)(2,1)S(1)} %get-tuple-element.171), channel_id=1, source_target_pairs={{0,2},{1,3},{2,0},{3,1},{4,6},{5,7},{6,4},{7,5},{8,10},{9,11},{10,... | collective-permute-start | bytes 663560 | tf_op jit(solution)/shard_map/cond/branch_1_fun/ppermute | solution.py:34
  275.7 12.1 %collective-permute-start.12 = (bf16[96,1152]{1,0:T(8,128)(2,1)S(1)}, bf16[96,1152]{1,0:T(8,128)(2,1)S(1)}, u32[]{:S(2)}, u32[]{:S(2)}) collective-permute-start(bf16[96,1152]{1,0:T(8,128)(2,1)S(1)} %get-tuple-element.185.refs_0_), channel_id=1, source_target_pairs={{0,3},{1,0},{2,1},{3,2},{4,7},{5,4},{6,5},{7,6},{8,11},{9,8},{10,9... | collective-permute-start | bytes 663560 | tf_op jit(solution)/shard_map/cond/branch_1_fun/ppermute | solution.py:34
  278.9 13.7 %collective-permute-start.14 = (bf16[96,1152]{1,0:T(8,128)(2,1)S(1)}, bf16[96,1152]{1,0:T(8,128)(2,1)S(1)}, u32[]{:S(2)}, u32[]{:S(2)}) collective-permute-start(bf16[96,1152]{1,0:T(8,128)(2,1)S(1)} %get-tuple-element.185.refs_0_), channel_id=1, source_target_pairs={{0,1},{1,2},{2,3},{3,0},{4,5},{5,6},{6,7},{7,4},{8,9},{9,10},{10,1... | collective-permute-start | bytes 663560 | tf_op jit(solution)/shard_map/cond/branch_1_fun/ppermute | solution.py:34
  303.6 25.4 %collective-permute-start.18 = (bf16[4,288,1152]{2,1,0:T(8,128)(2,1)}, bf16[4,288,1152]{2,1,0:T(8,128)(2,1)S(1)}, u32[]{:S(2)}, u32[]{:S(2)}) collective-permute-start(bf16[4,288,1152]{2,1,0:T(8,128)(2,1)} %get-tuple-element.201), channel_id=1, source_target_pairs={{0,8},{8,0},{1,9},{9,1},{2,10},{10,2},{3,11},{11,3},{4,12},{12,4},... | collective-permute-start | bytes 7962632 | tf_op jit(solution)/shard_map/cond/branch_1_fun/ppermute | solution.py:34
  307.3 20.2 %collective-permute-start.11 = (bf16[4,144,1152]{2,1,0:T(8,128)(2,1)}, bf16[4,144,1152]{2,1,0:T(8,128)(2,1)S(1)}, u32[]{:S(2)}, u32[]{:S(2)}) collective-permute-start(bf16[4,144,1152]{2,1,0:T(8,128)(2,1)} %get-tuple-element.183), channel_id=1, source_target_pairs={{0,8},{8,0},{1,9},{9,1},{2,10},{10,2},{3,11},{11,3},{4,12},{12,4},... | collective-permute-start | bytes 3981320 | tf_op jit(solution)/shard_map/cond/branch_1_fun/ppermute | solution.py:34
  307.5 12.6 %collective-permute-start.15 = (bf16[96,1152]{1,0:T(8,128)(2,1)S(1)}, bf16[96,1152]{1,0:T(8,128)(2,1)S(1)}, u32[]{:S(2)}, u32[]{:S(2)}) collective-permute-start(bf16[96,1152]{1,0:T(8,128)(2,1)S(1)} %get-tuple-element.194), channel_id=1, source_target_pairs={{0,1},{1,2},{2,3},{3,0},{4,5},{5,6},{6,7},{7,4},{8,9},{9,10},{10,1... | collective-permute-start | bytes 663560 | tf_op jit(solution)/shard_map/cond/branch_1_fun/ppermute | solution.py:34
  307.5 26.9 %collective-permute-start.19 = (bf16[96,1152]{1,0:T(8,128)(2,1)}, bf16[96,1152]{1,0:T(8,128)(2,1)}, u32[]{:S(2)}, u32[]{:S(2)}) collective-permute-start(bf16[96,1152]{1,0:T(8,128)(2,1)} %branch_1_fun.16), channel_id=1, source_target_pairs={{0,4},{4,0},{1,5},{5,1},{2,6},{6,2},{3,7},{7,3},{8,12},{12,8},{9,1... | collective-permute-start | bytes 663560 | tf_op jit(solution)/shard_map/cond/branch_1_fun/ppermute | solution.py:34
  307.5 13.2 %collective-permute-start.16 = (bf16[96,1152]{1,0:T(8,128)(2,1)S(1)}, bf16[96,1152]{1,0:T(8,128)(2,1)S(1)}, u32[]{:S(2)}, u32[]{:S(2)}) collective-permute-start(bf16[96,1152]{1,0:T(8,128)(2,1)S(1)} %get-tuple-element.195), channel_id=1, source_target_pairs={{0,2},{1,3},{2,0},{3,1},{4,6},{5,7},{6,4},{7,5},{8,10},{9,11},{10,... | collective-permute-start | bytes 663560 | tf_op jit(solution)/shard_map/cond/branch_1_fun/ppermute | solution.py:34
  338.0 13.0 %collective-permute-start.22 = (bf16[96,1152]{1,0:T(8,128)(2,1)S(1)}, bf16[96,1152]{1,0:T(8,128)(2,1)S(1)}, u32[]{:S(2)}, u32[]{:S(2)}) collective-permute-start(bf16[96,1152]{1,0:T(8,128)(2,1)S(1)} %get-tuple-element.214.c0), channel_id=1, source_target_pairs={{0,1},{1,2},{2,3},{3,0},{4,5},{5,6},{6,7},{7,4},{8,9},{9,10},{10,1... | collective-permute-start | bytes 663560 | tf_op jit(solution)/shard_map/cond/branch_1_fun/ppermute | solution.py:34
  379.7 15.9 %collective-permute-start.28 = (bf16[4,152,1152]{2,1,0:T(8,128)(2,1)}, bf16[4,152,1152]{2,1,0:T(8,128)(2,1)S(1)}, u32[]{:S(2)}, u32[]{:S(2)}) collective-permute-start(bf16[4,152,1152]{2,1,0:T(8,128)(2,1)} %get-tuple-element.253), channel_id=1, source_target_pairs={{0,8},{8,0},{1,9},{9,1},{2,10},{10,2},{3,11},{11,3},{4,12},{12,4},... | collective-permute-start | bytes 4202504 | tf_op jit(solution)/shard_map/cond/branch_1_fun/ppermute | solution.py:34
  380.8 13.0 %collective-permute-start.25 = (bf16[96,1152]{1,0:T(8,128)(2,1)S(1)}, bf16[96,1152]{1,0:T(8,128)(2,1)S(1)}, u32[]{:S(2)}, u32[]{:S(2)}) collective-permute-start(bf16[96,1152]{1,0:T(8,128)(2,1)S(1)} %copy-done.25), channel_id=1, source_target_pairs={{0,1},{1,2},{2,3},{3,0},{4,5},{5,6},{6,7},{7,4},{8,9},{9,10},{10,1... | collective-permute-start | bytes 663560 | tf_op jit(solution)/shard_map/cond/branch_1_fun/ppermute | solution.py:34
  380.8 13.0 %collective-permute-start.26 = (bf16[96,1152]{1,0:T(8,128)(2,1)S(1)}, bf16[96,1152]{1,0:T(8,128)(2,1)S(1)}, u32[]{:S(2)}, u32[]{:S(2)}) collective-permute-start(bf16[96,1152]{1,0:T(8,128)(2,1)S(1)} %copy-done.23), channel_id=1, source_target_pairs={{0,2},{1,3},{2,0},{3,1},{4,6},{5,7},{6,4},{7,5},{8,10},{9,11},{10,... | collective-permute-start | bytes 663560 | tf_op jit(solution)/shard_map/cond/branch_1_fun/ppermute | solution.py:34
  382.6 11.7 %collective-permute-start.27 = (bf16[96,1152]{1,0:T(8,128)(2,1)S(1)}, bf16[96,1152]{1,0:T(8,128)(2,1)S(1)}, u32[]{:S(2)}, u32[]{:S(2)}) collective-permute-start(bf16[96,1152]{1,0:T(8,128)(2,1)S(1)} %copy-done.21), channel_id=1, source_target_pairs={{0,3},{1,0},{2,1},{3,2},{4,7},{5,4},{6,5},{7,6},{8,11},{9,8},{10,9... | collective-permute-start | bytes 663560 | tf_op jit(solution)/shard_map/cond/branch_1_fun/ppermute | solution.py:34
  397.5 12.7 %collective-permute-start.30 = (bf16[152,1152]{1,0:T(8,128)(2,1)S(1)}, bf16[152,1152]{1,0:T(8,128)(2,1)}, u32[]{:S(2)}, u32[]{:S(2)}) collective-permute-start(bf16[152,1152]{1,0:T(8,128)(2,1)S(1)} %get-tuple-element.256), channel_id=1, source_target_pairs={{0,64},{32,96},{64,0},{96,32},{1,65},{33,97},{65,1},{97,33},{2,66}... | collective-permute-start | bytes 1050632 | tf_op jit(solution)/shard_map/cond/branch_1_fun/ppermute | solution.py:34
  398.5 18.9 %collective-permute-start.31 = (bf16[152,1152]{1,0:T(8,128)(2,1)S(1)}, bf16[152,1152]{1,0:T(8,128)(2,1)}, u32[]{:S(2)}, u32[]{:S(2)}) collective-permute-start(bf16[152,1152]{1,0:T(8,128)(2,1)S(1)} %get-tuple-element.257), channel_id=1, source_target_pairs={{0,96},{32,0},{64,32},{96,64},{1,97},{33,1},{65,33},{97,65},{2,98}... | collective-permute-start | bytes 1050632 | tf_op jit(solution)/shard_map/cond/branch_1_fun/ppermute | solution.py:34
  435.8 15.9 %collective-permute-start.77 = (bf16[2,96,1152]{2,1,0:T(8,128)(2,1)S(1)}, bf16[2,96,1152]{2,1,0:T(8,128)(2,1)}, u32[]{:S(2)}, u32[]{:S(2)}) collective-permute-start(bf16[2,96,1152]{2,1,0:T(8,128)(2,1)S(1)} %pad_maximum_fusion), channel_id=1, source_target_pairs={{0,3},{1,0},{2,1},{3,2},{4,7},{5,4},{6,5},{7,6},{8,11},{9,8},{10,9... | collective-permute-start | bytes 1327112 | tf_op jit(solution)/shard_map/ppermute | solution.py:34
  436.5 16.4 %collective-permute-start.78 = (bf16[2,96,1152]{2,1,0:T(8,128)(2,1)S(1)}, bf16[2,96,1152]{2,1,0:T(8,128)(2,1)S(1)}, u32[]{:S(2)}, u32[]{:S(2)}) collective-permute-start(bf16[2,96,1152]{2,1,0:T(8,128)(2,1)S(1)} %pad_maximum_fusion), channel_id=1, source_target_pairs={{0,2},{1,3},{2,0},{3,1},{4,6},{5,7},{6,4},{7,5},{8,10},{9,11},{10,... | collective-permute-start | bytes 1327112 | tf_op jit(solution)/shard_map/ppermute | solution.py:34
  436.8 22.8 %collective-permute-start.79 = (bf16[2,96,1152]{2,1,0:T(8,128)(2,1)S(1)}, bf16[2,96,1152]{2,1,0:T(8,128)(2,1)S(1)}, u32[]{:S(2)}, u32[]{:S(2)}) collective-permute-start(bf16[2,96,1152]{2,1,0:T(8,128)(2,1)S(1)} %pad_maximum_fusion), channel_id=1, source_target_pairs={{0,1},{1,2},{2,3},{3,0},{4,5},{5,6},{6,7},{7,4},{8,9},{9,10},{10,1... | collective-permute-start | bytes 1327112 | tf_op jit(solution)/shard_map/ppermute | solution.py:34
  448.7 11.5 %collective-permute-start.91 = (bf16[152,1152]{1,0:T(8,128)(2,1)S(1)}, bf16[152,1152]{1,0:T(8,128)(2,1)S(1)}, u32[]{:S(2)}, u32[]{:S(2)}) collective-permute-start(bf16[152,1152]{1,0:T(8,128)(2,1)S(1)} %shard_map.255.refs_0_), channel_id=1, source_target_pairs={{0,4},{4,16},{16,20},{20,0},{1,5},{5,17},{17,21},{21,1},{2,6},{6,1... | collective-permute-start | bytes 1050632 | tf_op jit(solution)/shard_map/ppermute | solution.py:34
  449.8 44.9 %collective-permute-start.99 = (bf16[4,288,1152]{2,1,0:T(8,128)(2,1)}, bf16[4,288,1152]{2,1,0:T(8,128)(2,1)}, u32[]{:S(2)}, u32[]{:S(2)}) collective-permute-start(bf16[4,288,1152]{2,1,0:T(8,128)(2,1)} %all-reduce.11.cloned.1.call-done.full1), channel_id=1, source_target_pairs={{0,8},{8,0},{1,9},{9,1},{2,10},{10,2},{3,11},{11,3},{4,12},{12,4},... | collective-permute-start | bytes 7962632 | tf_op jit(solution)/shard_map/ppermute | solution.py:34
  451.7 43.0 %collective-permute-start.98 = (bf16[4,288,1152]{2,1,0:T(8,128)(2,1)}, bf16[4,288,1152]{2,1,0:T(8,128)(2,1)S(1)}, u32[]{:S(2)}, u32[]{:S(2)}) collective-permute-start(bf16[4,288,1152]{2,1,0:T(8,128)(2,1)} %get-tuple-element.604.full0), channel_id=1, source_target_pairs={{0,8},{8,0},{1,9},{9,1},{2,10},{10,2},{3,11},{11,3},{4,12},{12,4},... | collective-permute-start | bytes 7962632 | tf_op jit(solution)/shard_map/ppermute | solution.py:34
  452.9 12.1 %collective-permute-start.92 = (bf16[152,1152]{1,0:T(8,128)(2,1)S(1)}, bf16[152,1152]{1,0:T(8,128)(2,1)S(1)}, u32[]{:S(2)}, u32[]{:S(2)}) collective-permute-start(bf16[152,1152]{1,0:T(8,128)(2,1)S(1)} %shard_map.255.refs_0_), channel_id=1, source_target_pairs={{0,16},{4,20},{16,0},{20,4},{1,17},{5,21},{17,1},{21,5},{2,18},{6,... | collective-permute-start | bytes 1050632 | tf_op jit(solution)/shard_map/ppermute | solution.py:34
  459.6 12.3 %collective-permute-start.93 = (bf16[152,1152]{1,0:T(8,128)(2,1)S(1)}, bf16[152,1152]{1,0:T(8,128)(2,1)S(1)}, u32[]{:S(2)}, u32[]{:S(2)}) collective-permute-start(bf16[152,1152]{1,0:T(8,128)(2,1)S(1)} %shard_map.255.refs_0_), channel_id=1, source_target_pairs={{0,20},{4,0},{16,4},{20,16},{1,21},{5,1},{17,5},{21,17},{2,22},{6,... | collective-permute-start | bytes 1050632 | tf_op jit(solution)/shard_map/ppermute | solution.py:34
  460.2 15.7 %collective-permute-start.88 = (bf16[2,96,1152]{2,1,0:T(8,128)(2,1)S(1)}, bf16[2,96,1152]{2,1,0:T(8,128)(2,1)S(1)}, u32[]{:S(2)}, u32[]{:S(2)}) collective-permute-start(bf16[2,96,1152]{2,1,0:T(8,128)(2,1)S(1)} %pad_maximum_fusion.1), channel_id=1, source_target_pairs={{0,3},{1,0},{2,1},{3,2},{4,7},{5,4},{6,5},{7,6},{8,11},{9,8},{10,9... | collective-permute-start | bytes 1327112 | tf_op jit(solution)/shard_map/ppermute | solution.py:34
  471.8 17.9 %collective-permute-start.90 = (bf16[2,96,1152]{2,1,0:T(8,128)(2,1)S(1)}, bf16[2,96,1152]{2,1,0:T(8,128)(2,1)S(1)}, u32[]{:S(2)}, u32[]{:S(2)}) collective-permute-start(bf16[2,96,1152]{2,1,0:T(8,128)(2,1)S(1)} %pad_maximum_fusion.1), channel_id=1, source_target_pairs={{0,1},{1,2},{2,3},{3,0},{4,5},{5,6},{6,7},{7,4},{8,9},{9,10},{10,1... | collective-permute-start | bytes 1327112 | tf_op jit(solution)/shard_map/ppermute | solution.py:34
  489.9 15.6 %collective-permute-start.94 = (bf16[152,1152]{1,0:T(8,128)(2,1)S(1)}, bf16[152,1152]{1,0:T(8,128)(2,1)S(1)}, u32[]{:S(2)}, u32[]{:S(2)}) collective-permute-start(bf16[152,1152]{1,0:T(8,128)(2,1)S(1)} %shard_map.257.refs_0_), channel_id=1, source_target_pairs={{32,0},{44,12},{64,32},{76,44},{96,64},{108,76},{0,96},{12,108},{3... | collective-permute-start | bytes 1050632 | tf_op jit(solution)/shard_map/ppermute | solution.py:565
  490.6 14.9 %collective-permute-start.95 = (bf16[152,1152]{1,0:T(8,128)(2,1)S(1)}, bf16[152,1152]{1,0:T(8,128)(2,1)S(1)}, u32[]{:S(2)}, u32[]{:S(2)}) collective-permute-start(bf16[152,1152]{1,0:T(8,128)(2,1)S(1)} %shard_map.257.refs_0_), channel_id=1, source_target_pairs={{64,0},{76,12},{96,32},{108,44},{0,64},{12,76},{32,96},{44,108},{6... | collective-permute-start | bytes 1050632 | tf_op jit(solution)/shard_map/ppermute | solution.py:565
  491.3 14.2 %collective-permute-start.96 = (bf16[152,1152]{1,0:T(8,128)(2,1)S(1)}, bf16[152,1152]{1,0:T(8,128)(2,1)S(1)}, u32[]{:S(2)}, u32[]{:S(2)}) collective-permute-start(bf16[152,1152]{1,0:T(8,128)(2,1)S(1)} %shard_map.257.refs_0_), channel_id=1, source_target_pairs={{96,0},{108,12},{0,32},{12,44},{32,64},{44,76},{64,96},{76,108},{9... | collective-permute-start | bytes 1050632 | tf_op jit(solution)/shard_map/ppermute | solution.py:565
  505.6 13.5 %collective-permute-start.100 = (bf16[4,152,1152]{2,1,0:T(8,128)(2,1)S(1)}, bf16[4,152,1152]{2,1,0:T(8,128)(2,1)S(1)}, u32[]{:S(2)}, u32[]{:S(2)}) collective-permute-start(bf16[4,152,1152]{2,1,0:T(8,128)(2,1)S(1)} %shard_map.260.full0), channel_id=1, source_target_pairs={{0,8},{8,0},{1,9},{9,1},{2,10},{10,2},{3,11},{11,3},{4,12},{12,4},... | collective-permute-start | bytes 4202504 | tf_op jit(solution)/shard_map/ppermute | solution.py:34
  (142 other events, 1803.3 us)
Sparse Core Ops, SparseCore 0:
  204.4 87.6 all-reduce.10
  334.7 111.6 all-reduce.12
